TPU v7x, 32 devices: a whole 2x2x4 slice. The times are simulated.
32 devices in a mesh: seq: 8 (over y, x, core), head: 4 (over z).
Axes of the slice: x: 2, y: 2, z: 4, core: 2. Of those that a mesh axis runs over, the one named last changes fastest.
Arguments:
- tokens: bfloat16 [2, 8192, 1024], P(None, 'seq', 'head'), may hold values from -6 to 6
- decay_codes: int32 [2, 8192, 512], P(None, 'seq', 'head'), may hold values from 1 to 32704
- cotangent: bfloat16 [2, 8192, 1024], P(None, 'seq', 'head'), may hold values from -6 to 6
- attn_gain: float32 [1024], replicated, may hold values from 0.5 to 1.5
- w_query: bfloat16 [1024, 512], P(None, 'head'), may hold values from -0.1875 to 0.1875
- w_key: bfloat16 [1024, 512], P(None, 'head'), may hold values from -0.1875 to 0.1875
- w_value: bfloat16 [1024, 1024], P(None, 'head'), may hold values from -0.1875 to 0.1875
- w_out_gate: bfloat16 [1024, 1024], P(None, 'head'), may hold values from -0.1875 to 0.1875
- conv_query: float32 [4, 512], P(None, 'head'), may hold values from -3 to 3
- conv_key: float32 [4, 512], P(None, 'head'), may hold values from -3 to 3
- conv_value: float32 [4, 1024], P(None, 'head'), may hold values from -3 to 3
- out_gain: float32 [256], replicated, may hold values from 0.5 to 1.5
- w_out: bfloat16 [1024, 1024], P('head'), may hold values from -0.375 to 0.375
- mlp_gain: float32 [1024], replicated, may hold values from 0.5 to 1.5
- w_gate: bfloat16 [1024, 2816], P(None, 'head'), may hold values from -0.1875 to 0.1875
- w_up: bfloat16 [1024, 2816], P(None, 'head'), may hold values from -0.1875 to 0.1875
- w_down: bfloat16 [2816, 1024], P('head'), may hold values from -0.21875 to 0.21875
Outputs:
- layer_out: float32 [2, 8192, 1024], P(None, 'seq', 'head')
- tokens_grad: float32 [2, 8192, 1024], P(None, 'seq', 'head')
- attn_gain_grad: float32 [1024], P('head')
- w_query_grad: float32 [1024, 512], P(None, 'head')
- w_key_grad: float32 [1024, 512], P(None, 'head')
- w_value_grad: float32 [1024, 1024], P(None, 'head')
- w_out_gate_grad: float32 [1024, 1024], P(None, 'head')
- conv_query_grad: float32 [4, 512], P(None, 'head')
- conv_key_grad: float32 [4, 512], P(None, 'head')
- conv_value_grad: float32 [4, 1024], P(None, 'head')
- out_gain_grad: float32 [256], replicated
- w_out_grad: float32 [1024, 1024], P('head')
- mlp_gain_grad: float32 [1024], P('head')
- w_gate_grad: float32 [1024, 2816], P(None, 'head')
- w_up_grad: float32 [1024, 2816], P(None, 'head')
- w_down_grad: float32 [2816, 1024], P('head')
All inputs are finite; a program needn't handle non-finite values.
Results may differ from a plain program's by a relative error of at most 0.035.
The roundings to bfloat16 on the way count: a program that leaves them out, or rounds other values in their place, can miss the bound.
Values may be sent and summed in bfloat16 or wider, within the bound.
A program may use at most 192 MiB of HBM per device.

v0:
```python
from functools import partial

import jax
import jax.numpy as jnp
from jax import lax
from jax.sharding import PartitionSpec as P

SPAN = 64
KEY_HEAD = 128


epsilon = 1e-06
decay_unit = 2.0 ** (-17)
highest = lax.Precision.HIGHEST


def shifted(block, axis, distance):
    devices = range(lax.axis_size(axis))
    route = [(i - distance, i) for i in devices if i - distance in devices]
    return lax.ppermute(block, axis, route)


def entering(shard, axis, join, neutral):
    place = lax.axis_index(axis)
    gathered = jax.tree.map(
        lambda a, kind: lax.all_gather(a.astype(kind), axis), shard, (jnp.bfloat16, jnp.bfloat16)
    )
    state = jax.tree.map(lambda a, e: jnp.zeros_like(a) + jnp.asarray(e, a.dtype), shard, neutral)

    def one(turn, state):
        return join(
            state,
            jax.tree.map(
                lambda a, own: lax.dynamic_index_in_dim(a, turn, 0, False).astype(own.dtype),
                gathered,
                shard,
            ),
        )

    return lax.fori_loop(0, place, one, state)


def prefix(shard, axis, combine, identity):
    count, here = (lax.axis_size(axis), lax.axis_index(axis))
    everything = jax.tree.map(
        lambda part, kind: lax.all_gather(part.astype(kind), axis),
        shard,
        jax.tree.map(lambda a: jnp.bfloat16 if a.dtype == jnp.float32 else a.dtype, shard),
    )
    start = jax.tree.map(
        lambda part, zero: jnp.broadcast_to(jnp.asarray(zero, part.dtype), part.shape),
        shard,
        identity,
    )

    def turn(k, before):
        at = count - 1 - k
        reached = at > here
        new = combine(
            before, jax.tree.map(lambda part, own: part[at].astype(own.dtype), everything, shard)
        )
        return jax.tree.map(lambda a, b: jnp.where(reached, a, b), new, before)

    return lax.fori_loop(0, count, turn, start)


def row_scale(values):
    return lax.rsqrt(jnp.mean(values * values, axis=-1, keepdims=True) + epsilon)


def silu_slope(values):
    logistic = jax.nn.sigmoid(values)
    return logistic * (1.0 + values * (1.0 - logistic))


def norm_back(values, inverse, weights, upstream):
    weighted = weights * upstream
    return inverse * weighted - values * inverse**3 * jnp.mean(
        weighted * values, axis=-1, keepdims=True
    )


def rounded(values):
    return lax.optimization_barrier(values.astype(jnp.bfloat16)).astype(jnp.float32)


def chain_step(earlier, later):
    return (earlier[0] * later[0], later[0][..., None] * earlier[1] + later[1])


def span_parts(cumul, span_log, causal, query, keyed, valued):
    query_exp = query * query.shape[-1] ** (-0.5) * jnp.exp(cumul)
    keyed_exp = keyed * jnp.exp(-cumul)
    keyed_end = keyed * jnp.exp(span_log[:, :, None] - cumul)
    scores = jnp.einsum("anthk,anuhk->anhtu", query_exp, keyed_exp, precision=highest)
    scores = jnp.where(causal, scores, 0.0)
    inner = jnp.einsum("anhtu,anuhv->anthv", scores, valued, precision=highest)
    update = jnp.einsum("anthk,anthv->anhkv", keyed_end, valued, precision=highest)
    span_decay = jnp.exp(span_log)

    def advance(state, pieces):
        return (pieces[0][..., None] * state + pieces[1], state)

    local_end, starts = lax.scan(
        advance,
        jnp.zeros_like(update[:, 0]),
        (jnp.moveaxis(span_decay, 1, 0), jnp.moveaxis(update, 1, 0)),
    )
    return (query_exp, inner, jnp.moveaxis(starts, 0, 1), local_end)


def finish(carry_decay, total_decay, incoming, query_exp, inner, starts, local_end):
    begin_offset = starts + carry_decay[..., None] * incoming[:, None]
    output = inner + jnp.einsum("anthk,anhkv->anthv", query_exp, begin_offset, precision=highest)
    return (output, total_decay[..., None] * incoming + local_end)


def local(
    tokens,
    decay_codes,
    cotangent,
    attn_gain,
    w_query,
    w_key,
    w_value,
    w_out_gate,
    conv_query,
    conv_key,
    conv_value,
    out_gain,
    w_out,
    mlp_gain,
    w_gate,
    w_up,
    w_down,
):
    seqs, rows, own_width = tokens.shape
    own_start = lax.axis_index("head") * own_width
    full_tokens = lax.all_gather(tokens, "head", axis=2, tiled=True)
    resid = full_tokens.astype(jnp.float32)
    first_scale = row_scale(resid)
    normed = (resid * first_scale * attn_gain).astype(jnp.bfloat16)
    w_mixer = jnp.concatenate([w_query, w_key, w_value, w_out_gate], axis=1)
    projected = jnp.einsum(
        "std,de->ste", normed, w_mixer, preferred_element_type=jnp.float32
    ).astype(jnp.bfloat16)
    key_width = w_query.shape[1]
    value_width = w_value.shape[1]
    conv_width = 2 * key_width + value_width
    mixed_in = projected[:, :, :conv_width]
    gate_pre = projected[:, :, conv_width:].astype(jnp.float32)
    taps = jnp.concatenate([conv_query, conv_key, conv_value], axis=1)
    tap_count = taps.shape[0]
    edge_rows = shifted(mixed_in[:, rows - tap_count + 1 :], "seq", 1)
    extended = jnp.concatenate([edge_rows, mixed_in], axis=1).astype(jnp.float32)
    conv_sum = taps[0] * extended[:, 0:rows]
    for offset in range(1, tap_count):
        conv_sum = conv_sum + taps[offset] * extended[:, offset : offset + rows]
    activated = jax.nn.silu(conv_sum)
    heads_here = key_width // KEY_HEAD
    blocks = rows // SPAN

    def spanned(values):
        return values.reshape(seqs, blocks, SPAN, heads_here, values.shape[-1] // heads_here)

    query = spanned(activated[:, :, :key_width])
    keyed = spanned(activated[:, :, key_width : 2 * key_width])
    valued = spanned(activated[:, :, 2 * key_width :])
    log_decay = spanned(-decay_codes.astype(jnp.float32) * decay_unit)
    cumul = jnp.cumsum(log_decay, axis=2)
    span_log = cumul[:, :, -1]
    running = jnp.cumsum(span_log, axis=1)
    carry_decay = jnp.exp(running - span_log)
    total_decay = jnp.exp(running[:, -1])
    positions = jnp.arange(SPAN)
    causal = positions[:, None] >= positions[None, :]
    parts, parts_pull = jax.vjp(partial(span_parts, cumul, span_log, causal), query, keyed, valued)
    incoming = entering(
        (total_decay, parts[3]),
        "seq",
        chain_step,
        (jnp.ones_like(total_decay), jnp.zeros_like(parts[3])),
    )[1]
    finished, finish_pull = jax.vjp(
        partial(finish, carry_decay, total_decay, incoming), parts[0], parts[1], parts[2], parts[3]
    )
    core_out = finished[0]
    value_head = core_out.shape[-1]
    core_rows = core_out.reshape(seqs, rows, heads_here, value_head)
    out_scale = row_scale(core_rows)
    normed_out = core_rows * out_scale * out_gain
    gate_rows = gate_pre.reshape(seqs, rows, heads_here, value_head)
    gate_silu = jax.nn.silu(gate_rows)
    gated = (
        (normed_out * gate_silu).astype(jnp.bfloat16).reshape(seqs, rows, heads_here * value_head)
    )
    mixer_term = rounded(
        jnp.einsum("ste,ed->std", gated, w_out, preferred_element_type=jnp.float32)
    )
    hidden_in = resid + lax.psum(mixer_term.astype(jnp.bfloat16), "head").astype(jnp.float32)
    second_scale = row_scale(hidden_in)
    normed_two = (hidden_in * second_scale * mlp_gain).astype(jnp.bfloat16)
    w_pair = jnp.concatenate([w_gate, w_up], axis=1)
    gate_up = jnp.einsum("std,df->stf", normed_two, w_pair, preferred_element_type=jnp.float32)
    ff_here = w_gate.shape[1]
    gate_val = gate_up[:, :, :ff_here]
    up_val = gate_up[:, :, ff_here:]
    gate_act = jax.nn.silu(gate_val)
    hidden = (gate_act * up_val).astype(jnp.bfloat16)
    mlp_term = rounded(
        jnp.einsum("stf,fd->std", hidden, w_down, preferred_element_type=jnp.float32)
    )
    layer_out = lax.dynamic_slice_in_dim(hidden_in, own_start, own_width, 2) + lax.psum_scatter(
        mlp_term.astype(jnp.bfloat16), "head", scatter_dimension=2, tiled=True
    ).astype(jnp.float32)
    upstream = lax.all_gather(cotangent, "head", axis=2, tiled=True)
    d_hidden = rounded(
        jnp.einsum("std,fd->stf", upstream, w_down, preferred_element_type=jnp.float32)
    )
    grad_down = jnp.einsum("stf,std->fd", hidden, upstream, preferred_element_type=jnp.float32)
    d_gate_up = jnp.concatenate(
        [d_hidden * up_val * silu_slope(gate_val), d_hidden * gate_act], axis=2
    ).astype(jnp.bfloat16)
    grad_pair = jnp.einsum("std,stf->df", normed_two, d_gate_up, preferred_element_type=jnp.float32)
    grad_gate = grad_pair[:, :ff_here]
    grad_up = grad_pair[:, ff_here:]
    d_normed_two = lax.psum(
        jnp.einsum("stf,df->std", d_gate_up, w_pair, preferred_element_type=jnp.float32).astype(
            jnp.bfloat16
        ),
        "head",
    ).astype(jnp.float32)
    d_hidden_in = upstream.astype(jnp.float32) + norm_back(
        hidden_in, second_scale, mlp_gain, d_normed_two
    )
    grad_mlp_gain = jnp.sum(
        lax.dynamic_slice_in_dim(d_normed_two * hidden_in * second_scale, own_start, own_width, 2),
        axis=(0, 1),
    )
    d_mixer = d_hidden_in.astype(jnp.bfloat16)
    grad_out = jnp.einsum("ste,std->ed", gated, d_mixer, preferred_element_type=jnp.float32)
    d_gated = rounded(jnp.einsum("std,ed->ste", d_mixer, w_out, preferred_element_type=jnp.float32))
    d_gated = d_gated.reshape(seqs, rows, heads_here, value_head)
    d_normed_out = d_gated * gate_silu
    d_gate_rows = d_gated * normed_out * silu_slope(gate_rows)
    grad_out_gain = jnp.sum(d_normed_out * core_rows * out_scale, axis=(0, 1, 2))
    d_core = norm_back(core_rows, out_scale, out_gain, d_normed_out).reshape(core_out.shape)
    own_grad = jnp.einsum(
        "anthk,anhk,anthv->ahkv", parts[0], carry_decay, d_core, precision=highest
    )
    d_leaving = prefix(
        (total_decay, own_grad),
        "seq",
        chain_step,
        (jnp.ones_like(total_decay), jnp.zeros_like(own_grad)),
    )[1]
    d_parts = finish_pull((d_core, d_leaving))
    d_query, d_keyed, d_valued = parts_pull(d_parts)
    d_activated = jnp.concatenate(
        [
            d_query.reshape(seqs, rows, key_width),
            d_keyed.reshape(seqs, rows, key_width),
            d_valued.reshape(seqs, rows, value_width),
        ],
        axis=2,
    )
    d_conv = d_activated * silu_slope(conv_sum)
    tap_grads = []
    d_extended = jnp.zeros(extended.shape, jnp.float32)
    for offset in range(tap_count):
        tap_grads.append(jnp.sum(d_conv * extended[:, offset : offset + rows], axis=(0, 1)))
        d_extended = d_extended + jnp.pad(
            taps[offset] * d_conv, ((0, 0), (offset, tap_count - 1 - offset), (0, 0))
        )
    grad_taps = jnp.stack(tap_grads)
    edge_back = shifted(d_extended[:, : tap_count - 1], "seq", -1)
    d_mixed = d_extended[:, tap_count - 1 :] + jnp.pad(
        edge_back, ((0, 0), (rows - tap_count + 1, 0), (0, 0))
    )
    d_projected = jnp.concatenate(
        [d_mixed, d_gate_rows.reshape(seqs, rows, value_width)], axis=2
    ).astype(jnp.bfloat16)
    grad_mixer = jnp.einsum("std,ste->de", normed, d_projected, preferred_element_type=jnp.float32)
    normed_term = jnp.einsum(
        "ste,de->std", d_projected, w_mixer, preferred_element_type=jnp.float32
    )
    d_normed, grad_out_gain = (
        lax.psum(normed_term.astype(jnp.bfloat16), "head").astype(jnp.float32),
        lax.psum(grad_out_gain.astype(jnp.bfloat16), "head").astype(jnp.float32),
    )
    tokens_full = d_hidden_in + norm_back(resid, first_scale, attn_gain, d_normed)
    tokens_grad = lax.dynamic_slice_in_dim(tokens_full, own_start, own_width, 2)
    grad_attn_gain = jnp.sum(
        lax.dynamic_slice_in_dim(d_normed * resid * first_scale, own_start, own_width, 2),
        axis=(0, 1),
    )
    grad_query = grad_mixer[:, :key_width]
    grad_key = grad_mixer[:, key_width : 2 * key_width]
    grad_value = grad_mixer[:, 2 * key_width : conv_width]
    grad_out_gate = grad_mixer[:, conv_width:]
    taps_query = grad_taps[:, :key_width]
    taps_key = grad_taps[:, key_width : 2 * key_width]
    taps_value = grad_taps[:, 2 * key_width :]
    (
        grad_attn_gain,
        grad_query,
        grad_key,
        grad_value,
        grad_out_gate,
        taps_query,
        taps_key,
        taps_value,
        grad_out_gain,
        grad_out,
        grad_mlp_gain,
        grad_gate,
        grad_up,
        grad_down,
    ) = (
        lax.psum(grad_attn_gain.astype(jnp.bfloat16), "seq").astype(jnp.float32),
        lax.psum(grad_query.astype(jnp.bfloat16), "seq").astype(jnp.float32),
        lax.psum(grad_key.astype(jnp.bfloat16), "seq").astype(jnp.float32),
        lax.psum(grad_value.astype(jnp.bfloat16), "seq").astype(jnp.float32),
        lax.psum(grad_out_gate.astype(jnp.bfloat16), "seq").astype(jnp.float32),
        lax.psum(taps_query.astype(jnp.bfloat16), "seq").astype(jnp.float32),
        lax.psum(taps_key.astype(jnp.bfloat16), "seq").astype(jnp.float32),
        lax.psum(taps_value.astype(jnp.bfloat16), "seq").astype(jnp.float32),
        lax.psum(grad_out_gain.astype(jnp.bfloat16), "seq").astype(jnp.float32),
        lax.psum(grad_out.astype(jnp.bfloat16), "seq").astype(jnp.float32),
        lax.psum(grad_mlp_gain.astype(jnp.bfloat16), "seq").astype(jnp.float32),
        lax.psum(grad_gate.astype(jnp.bfloat16), "seq").astype(jnp.float32),
        lax.psum(grad_up.astype(jnp.bfloat16), "seq").astype(jnp.float32),
        lax.psum(grad_down.astype(jnp.bfloat16), "seq").astype(jnp.float32),
    )
    return (
        layer_out,
        tokens_grad,
        grad_attn_gain,
        grad_query,
        grad_key,
        grad_value,
        grad_out_gate,
        taps_query,
        taps_key,
        taps_value,
        grad_out_gain,
        grad_out,
        grad_mlp_gain,
        grad_gate,
        grad_up,
        grad_down,
    )


def solution(mesh):
    in_specs = (
        P(None, "seq", "head"),
        P(None, "seq", "head"),
        P(None, "seq", "head"),
        P(),
        P(None, "head"),
        P(None, "head"),
        P(None, "head"),
        P(None, "head"),
        P(None, "head"),
        P(None, "head"),
        P(None, "head"),
        P(),
        P("head", None),
        P(),
        P(None, "head"),
        P(None, "head"),
        P("head", None),
    )
    out_specs = (
        P(None, "seq", "head"),
        P(None, "seq", "head"),
        P("head"),
        P(None, "head"),
        P(None, "head"),
        P(None, "head"),
        P(None, "head"),
        P(None, "head"),
        P(None, "head"),
        P(None, "head"),
        P(),
        P("head", None),
        P("head"),
        P(None, "head"),
        P(None, "head"),
        P("head", None),
    )
    return jax.shard_map(local, mesh=mesh, in_specs=in_specs, out_specs=out_specs, check_vma=False)
```

profile of v0, /device:TPU:1, one launch (start us, length us, event | category | flops | bytes accessed | tf_op | source)
XLA Modules:
  0.0 1091.1 jit_solution(12774620326177973625)
XLA Ops:
  12.1 80.3 %all-gather.8.cloned.1.call-done = bf16[2,1024,1024]{2,1,0:T(8,128)(2,1)} async-done(((bf16[2,1024,256]{2,1,0:T(8,128)(2,1)}), bf16[2,1024,1024]{2,1,0:T(8,128)(2,1)}) %all-gather.8.cloned.1.call-update) | async-done | bytes 4194320 | tf_op jit(solution)/shard_map/all_gather | solution.py:139
  112.2 5.5 convolution_bitcast_fusion.1
  120.3 38.0 %while.61 = (s32[]{:T(128)}, f32[2,1,128,256]{3,2,1,0:T(8,128)S(1)}, f32[16,2,1,128,256]{4,3,1,2,0:T(8,128)}, f32[16,2,1,128,1]{3,1,4,2,0:T(2,128)}, f32[16,2,1,...) while((s32[]{:T(128)}, f32[2,1,128,256]{3,2,1,0:T(8,128)S(1)}, ...), condition=%wide.region_3.4_spmd.clone, body=%wide.region_2.3_spmd.clone.sunk | while | flops 262147 | bytes 1316968 | solution.py:104
  159.8 10.1 all-gather
  184.0 7.3 fusion.40
  203.9 58.8 %all-gather.10.cloned.1.call-done = bf16[2,1024,1024]{2,1,0:T(8,128)(2,1)} async-done(((bf16[2,1024,256]{2,1,0:T(8,128)(2,1)}), bf16[2,1024,1024]{2,1,0:T(8,128)(2,1)}) %all-gather.10.cloned.1.call-update) | async-done | bytes 4194320 | tf_op jit(solution)/shard_map/all_gather | solution.py:216
  262.7 6.7 convolution_convert_fusion.3
  269.4 148.6 %all-reduce.12.cloned.1.call-done = bf16[2,1024,1024]{2,1,0:T(8,128)(2,1)} async-done(((bf16[2,1024,1024]{2,1,0:T(8,128)(2,1)}), bf16[2,1024,1024]{2,1,0:T(8,128)(2,1)}) %all-reduce.12.cloned.1.call-update) | async-done | bytes 4194320 | tf_op jit(solution)/shard_map/psum | solution.py:200
  418.0 5.0 multiply_reduce_fusion.2
  423.9 12.9 %fusion.45 = f32[2,1024,1408]{1,2,0:T(8,128)} fusion(bf16[1024,704]{1,0:T(8,128)(2,1)} %copy.135, bf16[1024,704]{1,0:T(8,128)(2,1)} %copy.134, f32[1024]{0:T(1024)S(1)} %copy-done.65, f32[2,1024]{1,0:T(2,128)S(1)} %get-tuple-element.643, bf16[2,1024,1024]{2,1,0:T(8,128)(2,1)S(1)} %copy-done.15, bf16[2,1024,1024]{2,1,0:T(8,128)(2,1)S(1)} %copy-done.4), kind=kOutput, calls=%fused_computation.114 | convolution fusion | flops 5923930112 | bytes 22818816 | tf_op jit(solution)/shard_map/std,df->stf/dot_general | solution.py:204
  436.8 8.1 fusion.3
  447.5 9.5 fusion.20
  457.1 7.1 convolution_convert_fusion
  464.2 146.9 %all-reduce.14.cloned.1.call-done = bf16[2,1024,1024]{2,1,0:T(8,128)(2,1)} async-done(((bf16[2,1024,1024]{2,1,0:T(8,128)(2,1)}), bf16[2,1024,1024]{2,1,0:T(8,128)(2,1)}) %all-reduce.14.cloned.1.call-update) | async-done | bytes 4194320 | tf_op jit(solution)/shard_map/psum | solution.py:227
  611.2 6.8 multiply_reduce_fusion.1
  618.3 7.4 subtract_add_fusion
  639.9 12.4 %bitcast_convert_fusion.2 = bf16[1024,1408]{1,0:T(8,128)(2,1)S(1)} fusion(bf16[2,1024,704]{1,2,0:T(8,128)(2,1)} %copy-done.35, bf16[2,1024,704]{1,2,0:T(8,128)(2,1)} %copy-done.34, f32[1024]{0:T(1024)S(1)} %copy-done.65, f32[2,1024]{1,0:T(2,128)S(1)} %get-tuple-element.643, bf16[2,1024,1024]{2,1,0:T(8,128)(2,1)} %all-reduce.12.cloned.1.call-done, ...), kind=kOutput, calls=%fused_computation.29 | convolution fusion | flops 5931139072 | bytes 17051648 | tf_op jit(solution)/shard_map/std,stf->df/dot_general | solution.py:224
  655.1 7.6 bitcast_convert_fusion.4
  669.6 9.0 convolution_bitcast_fusion
  684.4 5.9 fusion.70
  690.3 13.7 %while.62 = (s32[]{:T(128)}, f32[2,1,128,256]{3,2,1,0:T(8,128)S(1)}, s32[]{:T(128)}, bf16[8,2,1,128]{3,1,2,0:T(2,128)(2,1)}, bf16[8,2,1,128,256]{4,3,1,2,0:T(8,1...) while((s32[]{:T(128)}, f32[2,1,128,256]{3,2,1,0:T(8,128)S(1)}, s32[]{:T(128)}, ...), condition=%wide.region_15.16_spmd.clone, body=%wide.region_14.15_spmd.clone.sunk | while | flops 327944 | bytes 658087 | solution.py:64
  706.5 42.4 %while.60 = (s32[]{:T(128)}, f32[2,1,128,256]{3,2,1,0:T(8,128)S(1)}, f32[16,2,1,128,256]{4,3,1,2,0:T(8,128)}, f32[16,2,1,128,256]{3,4,0,1,2:T(8,128)}, f32[16,2,1,128,1]{3,1,4,2,0:T(2,128)}, /*index=5*/s32[]{:T(128)}, s32[]{:T(128)}) while((s32[]{:T(128)}, f32[2,1,128,256]{3,2,1,0:T(8,128)S(1)}, f32[16,2,1,128,256]{4,3,1,2,0:T(8,128)}, ...), condition=%wide.region_17.18_spmd, body=%wide.region_16.17_spmd.sunk | while | flops 131075 | bytes 2362469 | solution.py:104
  748.9 7.9 fusion.76
  766.0 6.8 broadcast_multiply_fusion.4
  776.4 6.3 pad_add_fusion
  792.3 6.4 convolution_convert_fusion.2
  798.7 6.7 convert_element_type.245
  809.8 9.2 psum.137
  824.4 76.3 %all-reduce.18.cloned.1.call-done = (bf16[1024,704]{1,0:T(8,128)(2,1)}, bf16[1024,704]{1,0:T(8,128)(2,1)}, bf16[1024,128]{1,0:T(8,128)(2,1)}, bf16[1024,128]{1,0...) async-done(((bf16[1024,704]{1,0:T(8,128)(2,1)}, bf16[1024,704]{1,0:T(8,128)(2,1)}, ...) | async-done | bytes 6422544 | tf_op jit(solution)/shard_map/psum | solution.py:331
  914.1 144.5 %all-reduce.16.cloned.1.call-done = bf16[2,1024,1024]{2,1,0:T(8,128)(2,1)} async-done(((bf16[2,1024,1024]{2,1,0:T(8,128)(2,1)}), bf16[2,1024,1024]{2,1,0:T(8,128)(2,1)}) %all-reduce.16.cloned.1.call-update) | async-done | bytes 4194320 | tf_op jit(solution)/shard_map/psum | solution.py:288
  1058.6 5.0 multiply_reduce_fusion
  1068.6 12.0 %all-reduce.5 = (bf16[256]{0:T(256)(128)(2,1)S(1)}, bf16[4,128]{1,0:T(4,128)(2,1)S(1)}, bf16[4,128]{1,0:T(4,128)(2,1)S(1)}, bf16[4,256]{1,0:T(4,128)(2,1)S(1)}, ...) all-reduce(bf16[256]{0:T(256)(128)(2,1)S(1)} %get-tuple-element.614, ...), channel_id=1, replica_groups=mesh['seq'=8,'head'=4] {'seq'}, use_global_device_ids=true, to_apply=%region_21.22 | all-reduce | flops 2816 | bytes 11264 | tf_op jit(solution)/shard_map/psum | solution.py:320
  (425 shorter events, 239.8 us)
Async XLA Ops:
  7.2 255.5 %copy-start = (bf16[704,1024]{1,0:T(8,128)(2,1)S(1)}, bf16[704,1024]{1,0:T(8,128)(2,1)}, u32[]{:S(2)}) copy-start(bf16[704,1024]{1,0:T(8,128)(2,1)} %param.41) | copy-start | bytes 4325380
  7.2 85.2 %all-gather.8.cloned.1.call-start = ((), (), s32[]{:S(2)}) async-start(), calls=%async_computation.1 | async-start | bytes 5242880 | tf_op jit(solution)/shard_map/all_gather | solution.py:139
  7.9 172.9 %all-gather.12.cloned.1.call-start = ((), (), s32[]{:S(2)}) async-start(), calls=%async_computation.7 | async-start | bytes 1179648 | tf_op jit(solution)/shard_map/all_gather | solution.py:26
  10.0 86.2 %copy-start.67 = (f32[1024]{0:T(1024)S(1)}, f32[1024]{0:T(1024)}, u32[]{:S(2)}) copy-start(f32[1024]{0:T(1024)} %param.28) | copy-start | bytes 12292
  10.0 86.2 %copy-start.72 = (bf16[1024,256]{1,0:T(8,128)(2,1)S(1)}, bf16[1024,256]{1,0:T(8,128)(2,1)}, u32[]{:S(2)}) copy-start(bf16[1024,256]{1,0:T(8,128)(2,1)} %param.32) | copy-start | bytes 1572868
  101.1 4.3 collective-permute-start
  159.0 103.8 %all-gather.10.cloned.1.call-start = ((), (), s32[]{:S(2)}) async-start(), calls=%async_computation.4 | async-start | bytes 5242880 | tf_op jit(solution)/shard_map/all_gather | solution.py:216
  159.7 258.3 %all-reduce.12.cloned.1.call-start = ((), (), s32[]{:S(2)}) async-start(), calls=%async_computation.2 | async-start | bytes 8388608 | tf_op jit(solution)/shard_map/psum | solution.py:200
  172.8 11.2 %copy-start.18 = (f32[2,16,64,128]{3,2,1,0:T(8,128)}, f32[2,16,64,128]{3,2,1,0:T(8,128)S(1)}, u32[]{:S(2)}) copy-start(f32[2,16,64,128]{3,2,1,0:T(8,128)S(1)} %fusion.90) | copy-start | bytes 3145732
  198.3 412.9 %all-reduce.14.cloned.1.call-start = ((), (), s32[]{:S(2)}) async-start(), calls=%async_computation.5 | async-start | bytes 8388608 | tf_op jit(solution)/shard_map/psum | solution.py:227
  269.4 153.7 %copy-start.65 = (f32[1024]{0:T(1024)S(1)}, f32[1024]{0:T(1024)}, u32[]{:S(2)}) copy-start(f32[1024]{0:T(1024)} %param.38) | copy-start | bytes 12292
  423.0 216.8 %copy-start.50 = (f32[2,1024]{1,0:T(2,128)}, f32[2,1024]{1,0:T(2,128)S(1)}, u32[]{:S(2)}) copy-start(f32[2,1024]{1,0:T(2,128)S(1)} %get-tuple-element.643) | copy-start | bytes 24580
  423.9 12.9 %copy-start.36 = (bf16[2,1024,704]{1,2,0:T(8,128)(2,1)S(1)}, bf16[2,1024,704]{1,2,0:T(8,128)(2,1)}, u32[]{:S(2)}) copy-start(bf16[2,1024,704]{1,2,0:T(8,128)(2,1)} %convolution_convert_fusion.3) | copy-start | bytes 8650756
  436.8 10.7 copy-start.39
  436.8 10.7 copy-start.40
  457.0 233.3 %all-gather.14.cloned.1.call-start = ((), (), s32[]{:S(2)}) async-start(), calls=%async_computation.8 | async-start | bytes 1179648 | tf_op jit(solution)/shard_map/all_gather | solution.py:46
  611.2 7.1 copy-start.13
  639.6 180.0 %reduce-scatter.2.cloned.1.call-start = ((), (), s32[]{:S(2)}) async-start(), calls=%async_computation.3 | async-start | bytes 5242880 | tf_op jit(solution)/shard_map/reduce_scatter | solution.py:213
  654.6 8.1 copy-start.53
  654.6 246.1 %all-reduce.18.cloned.1.call-start = ((), (), s32[]{:S(2)}) async-start(), calls=%async_computation.9 | async-start | bytes 13369344 | tf_op jit(solution)/shard_map/psum | solution.py:331
  655.1 7.7 copy-start.9
  655.1 7.7 copy-start.12
  666.5 15.7 %slice-start.2 = ((s8[8388608]{0:T(1024)(128)(4,1)}), s8[4194304]{0:T(1024)(128)(4,1)S(1)}, s32[]{:S(2)}) async-start(s8[8388608]{0:T(1024)(128)(4,1)} %bitcast.268), calls=%async_computation.12 | async-start | bytes 8388608
  669.6 9.1 copy-start.30
  669.6 12.6 %slice-start.3 = ((s8[8388608]{0:T(1024)(128)(4,1)}), s8[4194304]{0:T(1024)(128)(4,1)S(1)}, s32[]{:S(2)}) async-start(s8[8388608]{0:T(1024)(128)(4,1)} %bitcast.268), calls=%async_computation.13 | async-start | bytes 8388608
  748.9 8.0 copy-start.17
  748.9 8.0 copy-start.23
  748.9 12.6 %slice-start = ((s8[4227072]{0:T(1024)(128)(4,1)}), s8[4194304]{0:T(1024)(128)(4,1)S(1)}, s32[]{:S(2)}) async-start(s8[4227072]{0:T(1024)(128)(4,1)} %bitcast.266), calls=%async_computation.10 | async-start | bytes 8388608
  773.7 9.1 collective-permute-start.1
  792.3 266.3 %all-reduce.16.cloned.1.call-start = ((), (), s32[]{:S(2)}) async-start(), calls=%async_computation.6 | async-start | bytes 8388608 | tf_op jit(solution)/shard_map/psum | solution.py:288
  805.5 14.1 %copy-start.51 = (f32[2,1024]{1,0:T(2,128)S(1)}, f32[2,1024]{1,0:T(2,128)}, u32[]{:S(2)}) copy-start(f32[2,1024]{1,0:T(2,128)} %copy-done.50) | copy-start | bytes 24580
  1064.7 19.4 %copy-start.1 = (bf16[704,1024]{1,0:T(8,128)(2,1)S(1)}, bf16[704,1024]{1,0:T(8,128)(2,1)}, u32[]{:S(2)}) copy-start(bf16[704,1024]{1,0:T(8,128)(2,1)} %param.41) | copy-start | bytes 4325380
  (57 other events, 218.4 us)
Sparse Core Ops, SparseCore 0:
  9.6 82.7 all-gather.7
  159.1 21.7 all-gather.11
  182.4 80.2 all-gather.9
  264.9 153.0 all-reduce.11
  457.2 153.9 all-reduce.13
  639.7 22.9 all-gather.13
  665.0 76.3 reduce-scatter.1
  792.4 108.2 all-reduce.17
  903.2 155.2 all-reduce.15
where the time goes:
time: 1100 us; the launch traced here: 1090 us
  waiting for transfers between devices  658 us (60%)
  other arithmetic  154 us (14%)
  matrix products  138 us (13%)
  local copies, waits for them, and re-layouts  85.9 us (8%)
  blocking collectives  31.3 us (3%)
  between operations  15.3 us (1%)
    psum x1, waiting for transfers between devices, local(): lax.psum(mixer_term.astype(jnp.bfloat16), 'head').astype(jnp.float32)  149 us
    psum x1, waiting for transfers between devices, local(): lax.psum(jnp.einsum('stf,df->std', d_gate_up, w_pair, preferred_element_t...  147 us
    psum x1, waiting for transfers between devices, local(): lax.psum(normed_term.astype(jnp.bfloat16), 'head').astype(jnp.float32)  144 us
    all_gather x1, waiting for transfers between devices, local(): full_tokens = lax.all_gather(tokens, 'head', axis=2, tiled=True)  80.3 us
    psum x1, waiting for transfers between devices, local(): lax.psum(grad_gate.astype(jnp.bfloat16), 'seq').astype(jnp.float32)  76.3 us
    all_gather x1, waiting for transfers between devices, local(): upstream = lax.all_gather(cotangent, 'head', axis=2, tiled=True)  58.8 us
    unnamed x161, local copies, waits for them, and re-layouts  24.4 us
    dot_general x3, matrix products, finish(): jnp.einsum('anthk,anhkv->anthv', query_exp, begin_offset, precision=highest)  22.2 us
  transfers between devices with their start and end apart: 11, of which 8 were waited for; matrix products, arithmetic and copies ran while one was open for 21% of the time, Pallas kernels for 0%

commit v1 on v0

v1 whole, which is shorter than its diff:
```python
from functools import partial

import jax
import jax.numpy as jnp
from jax import lax
from jax.sharding import PartitionSpec as P

SPAN = 64
KEY_HEAD = 128

epsilon = 1e-06
decay_unit = 2.0 ** (-17)
BOTH = ("seq", "head")
f32 = jnp.float32
bf16 = jnp.bfloat16


def shifted(block, distance):
    count = lax.axis_size("seq") * lax.axis_size("head")
    route = [(i - distance, i) for i in range(count) if 0 <= i - distance < count]
    return lax.ppermute(block, BOTH, route)


def row_scale(values):
    return lax.rsqrt(jnp.mean(values * values, axis=-1, keepdims=True) + epsilon)


def silu_slope(values):
    logistic = jax.nn.sigmoid(values)
    return logistic * (1.0 + values * (1.0 - logistic))


def norm_back(values, inverse, weights, upstream):
    weighted = weights * upstream
    return inverse * weighted - values * inverse**3 * jnp.mean(
        weighted * values, axis=-1, keepdims=True
    )


def rounded(values):
    return values.astype(bf16).astype(f32)


def dot(spec, left, right):
    return jnp.einsum(spec, left.astype(bf16), right.astype(bf16), preferred_element_type=f32)


def cumulated(spec, values, count):
    at = jnp.arange(count)
    lower = (at[:, None] >= at[None, :]).astype(f32)
    return jnp.einsum(spec, lower, values, precision=lax.Precision.HIGHEST, preferred_element_type=f32)


def whole(weight):
    seq = lax.axis_size("seq")
    part = weight.shape[0] // seq
    mine = lax.dynamic_slice_in_dim(weight, lax.axis_index("seq") * part, part, 0)
    every = lax.all_gather(mine, ("head", "seq"), axis=0, tiled=True)
    return every.reshape(lax.axis_size("head"), *weight.shape)


def reduced(grad):
    flat = grad.astype(bf16).reshape(-1, grad.shape[-1])
    mine = lax.psum_scatter(flat, ("head", "seq"), scatter_dimension=0, tiled=True)
    return lax.all_gather(mine, "seq", axis=0, tiled=True).astype(f32)


def exchange(log_total, value, back):
    count = lax.axis_size("seq") * lax.axis_size("head")
    rows, width = value.shape
    part = rows // count
    pieces = lax.all_to_all(value.astype(bf16).reshape(count, part, width), BOTH, 0, 0, tiled=True)
    logs = lax.all_to_all(log_total.reshape(count, part), BOTH, 0, 0, tiled=True)
    upto = cumulated("pq,qr->pr", logs, count)
    before = upto - logs
    at = jnp.arange(count)
    if back:
        mask = at[:, None] < at[None, :]
        gap = before[None, :] - upto[:, None]
    else:
        mask = at[:, None] > at[None, :]
        gap = before[:, None] - upto[None, :]
    weight = jnp.where(mask[:, :, None], jnp.exp(jnp.minimum(gap, 0.0)), 0.0)
    total = jnp.einsum(
        "pqr,qrv->prv", weight, pieces.astype(f32), preferred_element_type=f32, precision=lax.Precision.HIGHEST
    )
    ours = lax.all_to_all(total.astype(bf16), BOTH, 0, 0, tiled=True)
    return ours.reshape(rows, width).astype(f32)


def local(
    tokens,
    decay_codes,
    cotangent,
    attn_gain,
    w_query,
    w_key,
    w_value,
    w_out_gate,
    conv_query,
    conv_key,
    conv_value,
    out_gain,
    w_out,
    mlp_gain,
    w_gate,
    w_up,
    w_down,
):
    seqs, rows, own_width = tokens.shape
    heads = lax.axis_size("head")
    own_head = lax.axis_index("head")
    mine = rows // heads

    def to_tokens(array):
        return lax.all_to_all(array, "head", 1, 2, tiled=True)

    def to_features(array):
        return lax.all_to_all(array, "head", 2, 1, tiled=True)

    resid = to_tokens(tokens).astype(f32)
    codes = to_tokens(decay_codes.astype(jnp.int16))
    upstream = to_tokens(cotangent)
    key_width = w_query.shape[1]
    value_width = w_value.shape[1]
    conv_width = 2 * key_width + value_width
    w_mixer = whole(jnp.concatenate([w_query, w_key, w_value, w_out_gate], axis=1))
    w_proj = whole(w_out)
    w_pair = whole(jnp.concatenate([w_gate, w_up], axis=1))
    w_low = whole(w_down)
    taps = lax.all_gather(jnp.concatenate([conv_query, conv_key, conv_value], axis=1), "head")

    first_scale = row_scale(resid)
    normed = (resid * first_scale * attn_gain).astype(bf16)
    projected = dot("std,hde->hste", normed, w_mixer).astype(bf16)
    mixed_in = projected[..., :conv_width]
    gate_rows = projected[..., conv_width:].astype(f32)
    tap_count = taps.shape[1]
    edge_rows = shifted(mixed_in[:, :, mine - tap_count + 1 :], 1)
    extended = jnp.concatenate([edge_rows, mixed_in], axis=2).astype(f32)
    conv_sum = sum(
        taps[:, j, None, None, :] * extended[:, :, j : j + mine] for j in range(tap_count)
    )
    activated = jax.nn.silu(conv_sum)
    blocks = mine // SPAN

    def spanned(values):
        return values.reshape(heads, seqs, blocks, SPAN, values.shape[-1])

    query = spanned(activated[..., :key_width])
    keyed = spanned(activated[..., key_width : 2 * key_width])
    valued = spanned(activated[..., 2 * key_width :])
    log_decay = -codes.astype(f32) * decay_unit
    log_decay = jnp.moveaxis(log_decay.reshape(seqs, blocks, SPAN, heads, key_width), 3, 0)
    cumul = cumulated("tu,hanuk->hantk", log_decay, SPAN)
    span_log = cumul[:, :, :, -1]
    running = cumulated("mn,hank->hamk", span_log, blocks)
    carry_decay = jnp.exp(running - span_log)
    log_total = running[:, :, -1]
    positions = jnp.arange(SPAN)
    causal = positions[:, None] >= positions[None, :]
    grow = jnp.exp(cumul)
    shrink = jnp.exp(-cumul)
    to_end = jnp.exp(span_log[:, :, :, None] - cumul)
    scale = key_width ** (-0.5)
    query_exp = query * scale * grow
    keyed_exp = keyed * shrink
    keyed_end = keyed * to_end
    scores = jnp.where(causal, dot("hantk,hanuk->hantu", query_exp, keyed_exp), 0.0)
    inner = dot("hantu,hanuv->hantv", scores, valued)
    update = dot("hantk,hantv->hankv", keyed_end, valued)
    span_decay = jnp.exp(span_log)
    starts = [jnp.zeros_like(update[:, :, 0])]
    for n in range(blocks):
        starts.append(span_decay[:, :, n, :, None] * starts[n] + update[:, :, n])
    local_end = starts.pop()
    flat = (-1, value_width)
    incoming = exchange(log_total.reshape(-1), local_end.reshape(flat), False).reshape(local_end.shape)
    states = jnp.stack(starts, 2) + carry_decay[..., None] * incoming[:, :, None]
    core_rows = (inner + dot("hantk,hankv->hantv", query_exp, states)).reshape(heads, seqs, mine, value_width)
    out_scale = row_scale(core_rows)
    normed_out = core_rows * out_scale * out_gain
    gate_silu = jax.nn.silu(gate_rows)
    gated = (normed_out * gate_silu).astype(bf16)
    mixer = jnp.sum(rounded(dot("hste,hed->hstd", gated, w_proj)), axis=0)
    hidden_in = resid + mixer
    second_scale = row_scale(hidden_in)
    normed_two = (hidden_in * second_scale * mlp_gain).astype(bf16)
    gate_up = dot("std,hdf->hstf", normed_two, w_pair)
    ff_here = w_gate.shape[1]
    gate_val = gate_up[..., :ff_here]
    up_val = gate_up[..., ff_here:]
    gate_act = jax.nn.silu(gate_val)
    hidden = (gate_act * up_val).astype(bf16)
    layer_out = hidden_in + jnp.sum(rounded(dot("hstf,hfd->hstd", hidden, w_low)), axis=0)
    layer_out = to_features(layer_out.astype(bf16)).astype(f32)

    d_hidden = rounded(dot("std,hfd->hstf", upstream, w_low))
    grad_down = reduced(dot("hstf,std->hfd", hidden, upstream))
    d_gate_up = jnp.concatenate(
        [d_hidden * up_val * silu_slope(gate_val), d_hidden * gate_act], axis=-1
    ).astype(bf16)
    grad_pair = reduced(dot("std,hstf->hdf", normed_two, d_gate_up))
    d_normed_two = dot("hstf,hdf->std", d_gate_up, w_pair)
    d_hidden_in = upstream.astype(f32) + norm_back(hidden_in, second_scale, mlp_gain, d_normed_two)
    grad_mlp_gain = jnp.sum(d_normed_two * hidden_in * second_scale, axis=(0, 1))
    d_mixer = d_hidden_in.astype(bf16)
    grad_out = reduced(dot("hste,std->hed", gated, d_mixer))
    d_gated = rounded(dot("std,hed->hste", d_mixer, w_proj))
    d_normed_out = d_gated * gate_silu
    d_gate_rows = d_gated * normed_out * silu_slope(gate_rows)
    grad_out_gain = jnp.sum(d_normed_out * core_rows * out_scale, axis=(0, 1, 2))
    d_core = norm_back(core_rows, out_scale, out_gain, d_normed_out)
    d_core = spanned(d_core)

    d_states = dot("hantk,hantv->hankv", query_exp, d_core)
    own_grad = jnp.sum(carry_decay[..., None] * d_states, axis=2)
    leaving = exchange(log_total.reshape(-1), own_grad.reshape(flat), True).reshape(own_grad.shape)
    d_ends = [leaving]
    for n in range(blocks - 1, 0, -1):
        d_ends.append(span_decay[:, :, n, :, None] * d_ends[-1] + d_states[:, :, n])
    d_ends = jnp.stack(d_ends[::-1], 2)
    d_scores = jnp.where(causal, dot("hantv,hanuv->hantu", d_core, valued), 0.0)
    d_query = dot("hantu,hanuk->hantk", d_scores, keyed_exp) + dot("hantv,hankv->hantk", d_core, states)
    d_query = d_query * scale * grow
    d_keyed = dot("hantu,hantk->hanuk", d_scores, query_exp) * shrink + dot("hanuv,hankv->hanuk", valued, d_ends) * to_end
    d_valued = dot("hantu,hantv->hanuv", scores, d_core) + dot("hanuk,hankv->hanuv", keyed_end, d_ends)
    d_activated = jnp.concatenate(
        [a.reshape(heads, seqs, mine, -1) for a in (d_query, d_keyed, d_valued)], axis=-1
    )
    d_conv = d_activated * silu_slope(conv_sum)
    tap_grads = []
    d_extended = jnp.zeros(extended.shape, f32)
    for j in range(tap_count):
        tap_grads.append(jnp.sum(d_conv * extended[:, :, j : j + mine], axis=(1, 2)))
        d_extended = d_extended + jnp.pad(
            taps[:, j, None, None, :] * d_conv, ((0, 0), (0, 0), (j, tap_count - 1 - j), (0, 0))
        )
    grad_taps = jnp.stack(tap_grads)
    edge_back = shifted(d_extended[:, :, : tap_count - 1], -1)
    d_mixed = d_extended[:, :, tap_count - 1 :] + jnp.pad(
        edge_back, ((0, 0), (0, 0), (mine - tap_count + 1, 0), (0, 0))
    )
    d_projected = jnp.concatenate([d_mixed, d_gate_rows], axis=-1).astype(bf16)
    grad_mixer = reduced(dot("std,hste->hde", normed, d_projected))
    d_normed = dot("hste,hde->std", d_projected, w_mixer)
    tokens_grad = d_hidden_in + norm_back(resid, first_scale, attn_gain, d_normed)
    tokens_grad = to_features(tokens_grad.astype(bf16)).astype(f32)
    grad_attn_gain = jnp.sum(d_normed * resid * first_scale, axis=(0, 1))

    small = jnp.concatenate([grad_attn_gain, grad_mlp_gain, grad_out_gain, grad_taps.reshape(-1)])
    small = lax.psum(small.astype(bf16), BOTH).astype(f32)
    width = grad_attn_gain.shape[0]
    own = own_head * own_width
    grad_attn_gain = lax.dynamic_slice_in_dim(small[:width], own, own_width, 0)
    grad_mlp_gain = lax.dynamic_slice_in_dim(small[width : 2 * width], own, own_width, 0)
    grad_out_gain = small[2 * width : 2 * width + value_width]
    grad_taps = small[2 * width + value_width :].reshape(grad_taps.shape)
    grad_taps = lax.dynamic_index_in_dim(grad_taps, own_head, 1, False)
    return (
        layer_out,
        tokens_grad,
        grad_attn_gain,
        grad_mixer[:, :key_width],
        grad_mixer[:, key_width : 2 * key_width],
        grad_mixer[:, 2 * key_width : conv_width],
        grad_mixer[:, conv_width:],
        grad_taps[:, :key_width],
        grad_taps[:, key_width : 2 * key_width],
        grad_taps[:, 2 * key_width :],
        grad_out_gain,
        grad_out,
        grad_mlp_gain,
        grad_pair[:, :ff_here],
        grad_pair[:, ff_here:],
        grad_down,
    )

def solution(mesh):
    in_specs = (
        P(None, "seq", "head"),
        P(None, "seq", "head"),
        P(None, "seq", "head"),
        P(),
        P(None, "head"),
        P(None, "head"),
        P(None, "head"),
        P(None, "head"),
        P(None, "head"),
        P(None, "head"),
        P(None, "head"),
        P(),
        P("head", None),
        P(),
        P(None, "head"),
        P(None, "head"),
        P("head", None),
    )
    out_specs = (
        P(None, "seq", "head"),
        P(None, "seq", "head"),
        P("head"),
        P(None, "head"),
        P(None, "head"),
        P(None, "head"),
        P(None, "head"),
        P(None, "head"),
        P(None, "head"),
        P(None, "head"),
        P(),
        P("head", None),
        P("head"),
        P(None, "head"),
        P(None, "head"),
        P("head", None),
    )
    return jax.shard_map(local, mesh=mesh, in_specs=in_specs, out_specs=out_specs, check_vma=False)
```

time: 1100 us -> 1120 us (1.018)
  other arithmetic: 154 us -> 72.1 us
  blocking collectives: 31.3 us -> 106 us
  starting transfers between devices: 7.61 us -> 50.4 us
  matrix products: 138 us -> 121 us
    psum x4 -> x0, waiting for transfers between devices: 516 us -> none  [the longest x1 149 us: local(): lax.psum(mixer_term.astype(jnp.bfloat16), 'head').astype(jnp.float32)]
    reduce_scatter x1 -> x3, waiting for transfers between devices: 0.01 us -> 253 us  [reduced(): lax.psum_scatter(flat, ('head', 'seq'), scatter_dimension=0, tiled=True)]
    unnamed x9 -> x12, waiting for transfers between devices: 1.48 us -> 144 us
    all_to_all x0 -> x10, waiting for transfers between devices: none -> 121 us  [the longest x3 44.7 us: to_tokens(): return lax.all_to_all(array, 'head', 1, 2, tiled=True)]
    all_to_all x0 -> x10, starting transfers between devices: none -> 42.7 us  [the longest x3 13.2 us: to_tokens(): return lax.all_to_all(array, 'head', 1, 2, tiled=True)]
    all_gather x1 -> x2, blocking collectives: 10.1 us -> 52.2 us  [the longest x1 37.5 us: local(): lax.all_gather(jnp.concatenate([conv_query, conv_key, conv_value], axis=1...]
    psum x2 -> x1, blocking collectives: 21.2 us -> 53.7 us  [local(): small = lax.psum(small.astype(bf16), BOTH).astype(f32)]
    convert_element_type x0 -> x11, local copies, waits for them, and re-layouts: none -> 27.8 us  [the longest x1 8.68 us: reduced(): flat = grad.astype(bf16).reshape(-1, grad.shape[-1])]
  transfers between devices with their start and end apart: 11 -> 23, of which waited for: 8 -> 17; matrix products, arithmetic and copies ran while one was open for 21% -> 15% of each run, Pallas kernels for 0% -> 0%
where the time goes in v1:
time: 1120 us
  waiting for transfers between devices  669 us (60%)
  matrix products  121 us (11%)
  blocking collectives  106 us (9%)
  local copies, waits for them, and re-layouts  82.8 us (7%)
  other arithmetic  72.1 us (6%)
  starting transfers between devices  50.4 us (4%)
  between operations  15.4 us (1%)
    reduce_scatter x3, waiting for transfers between devices, reduced(): lax.psum_scatter(flat, ('head', 'seq'), scatter_dimension=0, tiled=True)  253 us
    unnamed x12, waiting for transfers between devices  144 us
    dot_general x24, matrix products, dot(): jnp.einsum(spec, left.astype(bf16), right.astype(bf16), preferred_element...  117 us
    all_gather x4, waiting for transfers between devices, whole(): every = lax.all_gather(mine, ('head', 'seq'), axis=0, tiled=True)  83.4 us
    all_gather x3, waiting for transfers between devices, reduced(): return lax.all_gather(mine, 'seq', axis=0, tiled=True).astype(f32)  67.7 us
    psum x1, blocking collectives, local(): small = lax.psum(small.astype(bf16), BOTH).astype(f32)  53.7 us
    all_to_all x3, waiting for transfers between devices, to_tokens(): return lax.all_to_all(array, 'head', 1, 2, tiled=True)  44.7 us
    all_gather x1, blocking collectives, local(): lax.all_gather(jnp.concatenate([conv_query, conv_key, conv_value], axis=1...  37.5 us
  transfers between devices with their start and end apart: 23, of which 17 were waited for; matrix products, arithmetic and copies ran while one was open for 15% of the time, Pallas kernels for 0%

profile of v1, /device:TPU:1, one launch (start us, length us, event | category | flops | bytes accessed | tf_op | source)
XLA Modules:
  0.0 1116.6 jit_solution(12553423857370796407)
XLA Ops:
  27.0 14.9 %all-to-all-done.1 = s16[2,1024,128]{2,0,1:T(2,128)(2,1)S(1)} async-done(((s16[2,1024,128]{2,0,1:T(2,128)(2,1)}), s16[2,1024,128]{2,0,1:T(2,128)(2,1)S(1)}, u32[]{:S(2)}, u32[]{:S(2)}) %all-to-all-start.1) | async-done | bytes 524320 | tf_op jit(solution)/shard_map/all_to_all | solution.py:116
  46.3 37.5 %all-gather.1 = f32[4,4,512]{2,1,0:T(4,128)S(1)} all-gather(f32[1,4,512]{2,1,0:T(4,128)S(1)} %maximum_bitcast_fusion.1), channel_id=2, replica_groups=mesh['seq'=8,'head'=4] {'head'}, dimensions={0}, use_global_device_ids=true | all-gather | bytes 40960 | tf_op jit(solution)/shard_map/all_gather | solution.py:131
  92.5 7.6 all-gather.10.cloned.1.call-done
  100.1 6.5 convert_bitcast_fusion
  131.0 5.9 all-to-all-start.2
  140.1 17.7 %all-to-all-done.2 = bf16[32,32,256]{2,1,0:T(8,128)(2,1)} async-done(((bf16[32,32,256]{2,1,0:T(8,128)(2,1)}), bf16[32,32,256]{2,1,0:T(8,128)(2,1)}, u32[]{:S(2)}, u32[]{:S(2)}) %all-to-all-start.2) | async-done | bytes 524320 | tf_op jit(solution)/shard_map/all_to_all | solution.py:72
  165.4 29.8 %all-to-all-done.6 = bf16[2,1024,256]{2,0,1:T(2,128)(2,1)} async-done(((bf16[2,1024,256]{2,0,1:T(2,128)(2,1)}), bf16[2,1024,256]{2,0,1:T(2,128)(2,1)}, u32[]{:S(2)}, u32[]{:S(2)}) %all-to-all-start.6) | async-done | bytes 1048608 | tf_op jit(solution)/shard_map/all_to_all | solution.py:116
  216.2 11.0 all-to-all-done.4
  250.5 20.9 %all-gather.14.cloned.1.call-done = bf16[4096,1408]{1,0:T(8,128)(2,1)} async-done(((bf16[128,1408]{1,0:T(8,128)(2,1)}), bf16[4096,1408]{1,0:T(8,128)(2,1)}) %all-gather.14.cloned.1.call-update) | async-done | bytes 11534352 | tf_op jit(solution)/shard_map/all_gather | solution.py:58
  271.5 13.6 %convolution_bitcast_fusion = f32[4,2,256,1408]{2,3,1,0:T(8,128)} fusion(bf16[4,1024,1408,1]{2,1,3,0:T(8,128)(2,1)} %bitcast.332, bf16[2,256,1024,1]{2,1,0,3:T(8,128)(2,1)S(1)} %reshape.336), kind=kOutput, calls=%fused_computation.5 | convolution fusion | flops 5905580032 | bytes 24117248 | tf_op jit(solution)/shard_map/std,hdf->hstf/dot_general | solution.py:45
  285.1 54.8 %all-gather.16.cloned.1.call-done = bf16[2816,1024]{1,0:T(8,128)(2,1)} async-done(((bf16[88,1024]{1,0:T(8,128)(2,1)}), bf16[2816,1024]{1,0:T(8,128)(2,1)}) %all-gather.16.cloned.1.call-update) | async-done | bytes 5767184 | tf_op jit(solution)/shard_map/all_gather | solution.py:58
  339.8 11.7 %fusion.2 = (bf16[4,2,256,704]{2,3,1,0:T(8,128)(2,1)}, bf16[4,2,256,704]{2,3,1,0:T(8,128)(2,1)}, bf16[4,2,256,704]{2,3,1,0:T(8,128)(2,1)}) fusion(f32[4,2,256,1408]{2,3,1,0:T(8,128)} %convolution_bitcast_fusion, bf16[4,704,1024,1]{2,1,3,0:T(8,128)(2,1)} %bitcast.336, bf16[2,256,1024,1]{2,1,0,3:T(8,128)(2,1)S(1)} %copy-done.41), kind=kOutput, calls=%fused_computation.11 | convolution fusion | flops 2977300480 | bytes 27000832 | tf_op jit(solution)/shard_map/std,hfd->hstf/dot_general | solution.py:45
  351.6 13.6 %fusion.19 = (bf16[1024]{0:T(1024)(128)(2,1)S(1)}, f32[2,256]{1,0:T(2,128)S(1)}, f32[2,256,1024]{2,1,0:T(8,128)S(1)}, f32[2,256,1024,1]{2,1,0,3:T(8,128)}) fusion(f32[2,256]{1,0:T(2,128)S(1)} %get-tuple-element.83, f32[1024]{0:T(1024)S(1)} %copy-done.46, f32[2,256,1024]{2,1,0:T(8,128)} %reshape.316, f32[2,256,1024]{2,1,0:T(8,128)} %convert_reduce_fusion.1, ...), kind=kOutput, calls=%fused_computation.61 | convolution fusion | flops 5920782848 | bytes 25700352 | tf_op jit(solution)/shard_map/hstf,hdf->std/dot_general | solution.py:45
  383.2 15.3 %all-to-all-done.7 = bf16[32,32,256]{2,1,0:T(8,128)(2,1)S(1)} async-done(((bf16[32,32,256]{2,1,0:T(8,128)(2,1)}), bf16[32,32,256]{2,1,0:T(8,128)(2,1)S(1)}, u32[]{:S(2)}, u32[]{:S(2)}) %all-to-all-start.7) | async-done | bytes 524320 | tf_op jit(solution)/shard_map/all_to_all | solution.py:72
  409.6 9.4 all-to-all-done.8
  433.8 6.8 broadcast_multiply_fusion.3
  445.4 6.4 pad_add_fusion
  461.8 8.7 copy.120
  471.7 6.8 bitcast_convert_fusion.2
  480.2 11.9 %bitcast_convert_fusion = bf16[4,1408,1024]{1,2,0:T(8,128)(2,1)} fusion(bf16[4,2,256,704]{2,3,1,0:T(8,128)(2,1)} %get-tuple-element.38, bf16[4,2,256,704]{2,3,1,0:T(8,128)(2,1)} %get-tuple-element.37, f32[2,256,1024]{2,1,0:T(8,128)S(1)} %copy-done.20, f32[1024]{0:T(1024)S(1)} %copy-done.46, f32[2,256]{1,0:T(2,128)S(1)} %get-tuple-element.83), kind=kOutput, calls=%fused_computation | convolution fusion | flops 5924454400 | bytes 19404800 | tf_op jit(solution)/shard_map/std,hstf->hdf/dot_general | solution.py:45
  497.3 83.2 %reduce-scatter.7.cloned.1.call-done = bf16[128,768]{1,0:T(8,128)(2,1)} async-done(((bf16[4096,768]{1,0:T(8,128)(2,1)}), bf16[128,768]{1,0:T(8,128)(2,1)}) %reduce-scatter.7.cloned.1.call-update) | async-done | bytes 196624 | tf_op jit(solution)/shard_map/reduce_scatter | solution.py:64
  580.7 141.6 %reduce-scatter.11.cloned.1.call-done = bf16[88,1024]{1,0:T(8,128)(2,1)} async-done(((bf16[2816,1024]{1,0:T(8,128)(2,1)}), bf16[88,1024]{1,0:T(8,128)(2,1)}) %reduce-scatter.11.cloned.1.call-update) | async-done | bytes 180240 | tf_op jit(solution)/shard_map/reduce_scatter | solution.py:64
  722.6 8.4 convert_reduce_fusion
  731.0 144.2 %reduce-scatter.13.cloned.1.call-done = bf16[128,1408]{1,0:T(8,128)(2,1)} async-done(((bf16[4096,1408]{1,0:T(8,128)(2,1)}), bf16[128,1408]{1,0:T(8,128)(2,1)}) %reduce-scatter.13.cloned.1.call-update) | async-done | bytes 360464
  877.2 7.8 fusion.17
  894.8 22.5 %all-to-all-done.5 = bf16[2,256,1024]{1,0,2:T(2,128)(2,1)S(1)} async-done(((bf16[2,256,1024]{1,0,2:T(2,128)(2,1)}), bf16[2,256,1024]{1,0,2:T(2,128)(2,1)S(1)}, u32[]{:S(2)}, u32[]{:S(2)}) %all-to-all-start.5) | async-done | bytes 1048608 | tf_op jit(solution)/shard_map/all_to_all | solution.py:119
  921.7 53.7 %psum.7 = bf16[10496]{0:T(1024)(128)(2,1)S(1)} all-reduce(bf16[10496]{0:T(1024)(128)(2,1)S(1)} %pad_maximum_fusion.9), channel_id=1, replica_groups=mesh['seq'=8,'head'=4] {'seq','head'}, use_global_device_ids=true, to_apply=%region_16.17 | all-reduce | flops 10496 | bytes 41984 | tf_op jit(solution)/shard_map/psum | solution.py:252
  985.8 28.3 %reduce-scatter.9.cloned.1.call-done = bf16[32,1024]{1,0:T(8,128)(2,1)} async-done(((bf16[1024,1024]{1,0:T(8,128)(2,1)}), bf16[32,1024]{1,0:T(8,128)(2,1)}) %reduce-scatter.9.cloned.1.call-update) | async-done | bytes 65552 | tf_op jit(solution)/shard_map/reduce_scatter | solution.py:64
  1014.1 14.7 %all_gather.37 = bf16[256,1024]{1,0:T(8,128)(2,1)S(1)} all-gather(bf16[32,1024]{1,0:T(8,128)(2,1)} %reduce-scatter.9.cloned.1.call-done), channel_id=1, replica_groups=mesh['seq'=8,'head'=4] {'seq'}, dimensions={0}, use_global_device_ids=true | all-gather | bytes 589824 | tf_op jit(solution)/shard_map/all_gather | solution.py:65
  1029.9 13.6 %all-gather.18.cloned.1.call-done = bf16[1024,768]{1,0:T(8,128)(2,1)} async-done(((bf16[128,768]{1,0:T(8,128)(2,1)}), bf16[1024,768]{1,0:T(8,128)(2,1)}) %all-gather.18.cloned.1.call-update) | async-done | bytes 1572880 | tf_op jit(solution)/shard_map/all_gather | solution.py:65
  1047.1 23.2 %all-gather.22.cloned.1.call-done = bf16[704,1024]{1,0:T(8,128)(2,1)} async-done(((bf16[88,1024]{1,0:T(8,128)(2,1)}), bf16[704,1024]{1,0:T(8,128)(2,1)}) %all-gather.22.cloned.1.call-update) | async-done | bytes 1441808 | tf_op jit(solution)/shard_map/all_gather | solution.py:65
  1073.7 30.8 %all-gather.20.cloned.1.call-done = bf16[1024,1408]{0,1:T(8,128)(2,1)} async-done(((bf16[128,1408]{0,1:T(8,128)(2,1)}), bf16[1024,1408]{0,1:T(8,128)(2,1)}) %all-gather.20.cloned.1.call-update) | async-done | bytes 2883600 | tf_op jit(solution)/shard_map/all_gather | solution.py:65
  (269 shorter events, 218.3 us)
Async XLA Ops:
  7.2 38.4 %copy-start = (bf16[704,1024]{1,0:T(8,128)(2,1)S(1)}, bf16[704,1024]{1,0:T(8,128)(2,1)}, u32[]{:S(2)}) copy-start(bf16[704,1024]{1,0:T(8,128)(2,1)} %param.33) | copy-start | bytes 4325380
  7.2 92.9 %all-gather.10.cloned.1.call-start = ((), (), s32[]{:S(2)}) async-start(), calls=%async_computation.14 | async-start | bytes 6488064 | tf_op jit(solution)/shard_map/all_gather | solution.py:58
  8.9 227.9 %all-gather.12.cloned.1.call-start = ((), (), s32[]{:S(2)}) async-start(), calls=%async_computation.15 | async-start | bytes 2162688 | tf_op jit(solution)/shard_map/all_gather | solution.py:58
  10.5 261.0 %all-gather.14.cloned.1.call-start = ((), (), s32[]{:S(2)}) async-start(), calls=%async_computation.16 | async-start | bytes 11894784 | tf_op jit(solution)/shard_map/all_gather | solution.py:58
  19.5 22.4 %all-to-all-start.1 = ((s16[2,1024,128]{2,0,1:T(2,128)(2,1)}), s16[2,1024,128]{2,0,1:T(2,128)(2,1)S(1)}, u32[]{:S(2)}, u32[]{:S(2)}) async-start(s16[2,1024,128]{2,0,1:T(2,128)(2,1)} %copy_convert_fusion), calls=%async_computation.1 | async-start | bytes 1048576 | tf_op jit(solution)/shard_map/all_to_all | solution.py:116
  25.0 21.3 %copy-start.47 = (f32[1024]{0:T(1024)S(1)}, f32[1024]{0:T(1024)}, u32[]{:S(2)}) copy-start(f32[1024]{0:T(1024)} %param.20) | copy-start | bytes 12292
  25.0 21.3 %copy-start.49 = (f32[4,256]{1,0:T(4,128)S(1)}, f32[4,256]{1,0:T(4,128)}, u32[]{:S(2)}) copy-start(f32[4,256]{1,0:T(4,128)} %param.27) | copy-start | bytes 12292
  25.0 21.3 %copy-start.51 = (f32[4,128]{1,0:T(4,128)S(1)}, f32[4,128]{1,0:T(4,128)}, u32[]{:S(2)}) copy-start(f32[4,128]{1,0:T(4,128)} %param.26) | copy-start | bytes 6148
  25.0 21.3 %copy-start.52 = (f32[4,128]{1,0:T(4,128)S(1)}, f32[4,128]{1,0:T(4,128)}, u32[]{:S(2)}) copy-start(f32[4,128]{1,0:T(4,128)} %param.25) | copy-start | bytes 6148
  42.0 44.5 %all-to-all-start = ((bf16[2,1024,256]{2,0,1:T(2,128)(2,1)}), bf16[2,1024,256]{2,0,1:T(2,128)(2,1)S(1)}, u32[]{:S(2)}, u32[]{:S(2)}) async-start(bf16[2,1024,256]{2,0,1:T(2,128)(2,1)} %copy.94), calls=%async_computation | async-start | bytes 2097152 | tf_op jit(solution)/shard_map/all_to_all | solution.py:116
  45.5 294.3 %all-gather.16.cloned.1.call-start = ((), (), s32[]{:S(2)}) async-start(), calls=%async_computation.17 | async-start | bytes 5947392 | tf_op jit(solution)/shard_map/all_gather | solution.py:58
  108.4 9.0 collective-permute-start
  112.6 18.4 %all-to-all-start.3 = ((f32[32,1,32]{2,1,0:T(1,128)}), f32[32,1,32]{2,1,0:T(1,128)S(1)}, u32[]{:S(2)}, u32[]{:S(2)}) async-start(f32[32,1,32]{2,1,0:T(1,128)} %bitcast.28), calls=%async_computation.3 | async-start | bytes 32768 | tf_op jit(solution)/shard_map/all_to_all | solution.py:73
  123.7 107.3 %copy-start.5 = (bf16[4,2,256,256]{3,2,1,0:T(8,128)(2,1)}, bf16[4,2,256,256]{3,2,1,0:T(8,128)(2,1)S(1)}, u32[]{:S(2)}) copy-start(bf16[4,2,256,256]{3,2,1,0:T(8,128)(2,1)S(1)} %slice.290) | copy-start | bytes 3145732
  131.0 26.9 %all-to-all-start.2 = ((bf16[32,32,256]{2,1,0:T(8,128)(2,1)}), bf16[32,32,256]{2,1,0:T(8,128)(2,1)}, u32[]{:S(2)}, u32[]{:S(2)}) async-start(bf16[32,32,256]{2,1,0:T(8,128)(2,1)} %add_convert_fusion.2), calls=%async_computation.2 | async-start | bytes 1048576 | tf_op jit(solution)/shard_map/all_to_all | solution.py:72
  157.9 37.3 %all-to-all-start.6 = ((bf16[2,1024,256]{2,0,1:T(2,128)(2,1)}), bf16[2,1024,256]{2,0,1:T(2,128)(2,1)}, u32[]{:S(2)}, u32[]{:S(2)}) async-start(bf16[2,1024,256]{2,0,1:T(2,128)(2,1)} %copy.108), calls=%async_computation.6 | async-start | bytes 2097152 | tf_op jit(solution)/shard_map/all_to_all | solution.py:116
  162.1 37.4 %copy-start.46 = (f32[1024]{0:T(1024)S(1)}, f32[1024]{0:T(1024)}, u32[]{:S(2)}) copy-start(f32[1024]{0:T(1024)} %param.30) | copy-start | bytes 12292
  195.2 31.9 %all-to-all-start.4 = ((bf16[32,32,256]{2,1,0:T(8,128)(2,1)}), bf16[32,32,256]{2,1,0:T(8,128)(2,1)}, u32[]{:S(2)}, u32[]{:S(2)}) async-start(bf16[32,32,256]{2,1,0:T(8,128)(2,1)} %copy.102), calls=%async_computation.4 | async-start | bytes 1048576 | tf_op jit(solution)/shard_map/all_to_all | solution.py:87
  271.4 68.4 %copy-start.41 = (bf16[2,256,1024,1]{2,1,0,3:T(8,128)(2,1)S(1)}, bf16[2,256,1024,1]{2,1,0,3:T(8,128)(2,1)}, u32[]{:S(2)}) copy-start(bf16[2,256,1024,1]{2,1,0,3:T(8,128)(2,1)} %reshape.338) | copy-start | bytes 3145732
  379.6 18.9 %all-to-all-start.7 = ((bf16[32,32,256]{2,1,0:T(8,128)(2,1)}), bf16[32,32,256]{2,1,0:T(8,128)(2,1)S(1)}, u32[]{:S(2)}, u32[]{:S(2)}) async-start(bf16[32,32,256]{2,1,0:T(8,128)(2,1)} %bitcast.60), calls=%async_computation.7 | async-start | bytes 1048576 | tf_op jit(solution)/shard_map/all_to_all | solution.py:72
  400.5 18.6 %all-to-all-start.8 = ((bf16[32,32,256]{2,1,0:T(8,128)(2,1)}), bf16[32,32,256]{2,1,0:T(8,128)(2,1)}, u32[]{:S(2)}, u32[]{:S(2)}) async-start(bf16[32,32,256]{2,1,0:T(8,128)(2,1)} %copy.115), calls=%async_computation.8 | async-start | bytes 1048576 | tf_op jit(solution)/shard_map/all_to_all | solution.py:87
  403.7 176.9 %reduce-scatter.7.cloned.1.call-start = ((), (), s32[]{:S(2)}) async-start(), calls=%async_computation.18 | async-start | bytes 6488064 | tf_op jit(solution)/shard_map/reduce_scatter | solution.py:64
  441.5 10.3 collective-permute-start.1
  470.5 251.8 %reduce-scatter.11.cloned.1.call-start = ((), (), s32[]{:S(2)}) async-start(), calls=%async_computation.22 | async-start | bytes 5947392 | tf_op jit(solution)/shard_map/reduce_scatter | solution.py:64
  478.6 396.7 %reduce-scatter.13.cloned.1.call-start = ((), (), s32[]{:S(2)}) async-start(), calls=%async_computation.24 | async-start | bytes 11894784
  492.2 521.9 %reduce-scatter.9.cloned.1.call-start = ((), (), s32[]{:S(2)}) async-start(), calls=%async_computation.20 | async-start | bytes 2162688 | tf_op jit(solution)/shard_map/reduce_scatter | solution.py:64
  497.3 546.2 %all-gather.18.cloned.1.call-start = ((), (), s32[]{:S(2)}) async-start(), calls=%async_computation.19 | async-start | bytes 1769472 | tf_op jit(solution)/shard_map/all_gather | solution.py:65
  580.6 489.8 %all-gather.22.cloned.1.call-start = ((), (), s32[]{:S(2)}) async-start(), calls=%async_computation.23 | async-start | bytes 1622016 | tf_op jit(solution)/shard_map/all_gather | solution.py:65
  722.3 154.9 %copy-start.44 = (bf16[4,2,256,256]{3,2,1,0:T(8,128)(2,1)S(1)}, bf16[4,2,256,256]{3,2,1,0:T(8,128)(2,1)}, u32[]{:S(2)}) copy-start(bf16[4,2,256,256]{3,2,1,0:T(8,128)(2,1)} %get-tuple-element.41) | copy-start | bytes 3145732
  722.3 382.2 %all-gather.20.cloned.1.call-start = ((), (), s32[]{:S(2)}) async-start(), calls=%async_computation.21 | async-start | bytes 3244032 | tf_op jit(solution)/shard_map/all_gather | solution.py:65
  889.3 28.0 %all-to-all-start.5 = ((bf16[2,256,1024]{1,0,2:T(2,128)(2,1)}), bf16[2,256,1024]{1,0,2:T(2,128)(2,1)S(1)}, u32[]{:S(2)}, u32[]{:S(2)}) async-start(bf16[2,256,1024]{1,0,2:T(2,128)(2,1)} %copy.106), calls=%async_computation.5 | async-start | bytes 2097152 | tf_op jit(solution)/shard_map/all_to_all | solution.py:119
  917.3 64.2 %all-to-all-start.9 = ((bf16[2,256,1024]{1,0,2:T(2,128)(2,1)}), bf16[2,256,1024]{1,0,2:T(2,128)(2,1)}, u32[]{:S(2)}, u32[]{:S(2)}) async-start(bf16[2,256,1024]{1,0,2:T(2,128)(2,1)} %copy.117), calls=%async_computation.9 | async-start | bytes 2097152 | tf_op jit(solution)/shard_map/all_to_all | solution.py:119
  (47 other events, 162.4 us)
Sparse Core Ops, SparseCore 0:
  11.5 88.6 all-gather.9
  103.0 55.8 all-gather.11
  162.3 109.0 all-gather.13
  274.1 65.6 all-gather.15
  470.6 109.9 reduce-scatter.6
  582.8 139.3 reduce-scatter.10
  724.7 150.4 reduce-scatter.12
  878.2 135.8 reduce-scatter.8
  1016.0 27.4 all-gather.17
  1045.2 25.1 all-gather.21
  1072.8 31.6 all-gather.19

commit v2 on v1

--- a/solution.py
+++ b/solution.py
@@ -3,6 +3,8 @@
 import jax
 import jax.numpy as jnp
 from jax import lax
+from jax.experimental import pallas as pl
+from jax.experimental.pallas import tpu as pltpu
 from jax.sharding import PartitionSpec as P
 
 SPAN = 64
@@ -13,6 +15,212 @@
 BOTH = ("seq", "head")
 f32 = jnp.float32
 bf16 = jnp.bfloat16
+
+
+MESH = pl.DeviceIdType.MESH
+
+
+def bits_of(count):
+    return [1 << k for k in range(count.bit_length() - 1)]
+
+def reduce_body(seq, head, plan, n_arrays, *refs):
+    grads, outs, scratch = refs[:n_arrays], refs[n_arrays : 2 * n_arrays], refs[2 * n_arrays :]
+    s, z = lax.axis_index("seq"), lax.axis_index("head")
+    seq_bits, head_bits = bits_of(seq), bits_of(head)
+    ns, nz = len(seq_bits), len(head_bits)
+    per = 1 + ns + nz
+    owns = scratch[: len(plan)]
+    recvs = [scratch[len(plan) + i * (ns + nz) : len(plan) + (i + 1) * (ns + nz)] for i in range(len(plan))]
+    load_sem, send_sem, recv_sem, zsend, zrecv, gsend, grecv, keep_sem = scratch[len(plan) * per :]
+
+    def flip(place, mask):
+        return place + mask - 2 * mask * (place // mask % 2)
+
+    def seq_peer(mask):
+        return {"seq": flip(s, mask), "head": z}
+
+    def head_peer(mask):
+        return {"seq": s, "head": flip(z, mask)}
+
+    barrier = pltpu.get_barrier_semaphore()
+    for mask in seq_bits:
+        pl.semaphore_signal(barrier, 1, device_id=seq_peer(mask), device_id_type=MESH)
+    for mask in head_bits:
+        pl.semaphore_signal(barrier, 1, device_id=head_peer(mask), device_id_type=MESH)
+    pl.semaphore_wait(barrier, ns + nz)
+
+    def masks(c):
+        rest = seq_bits[1:]
+        return seq_bits[:1] + (rest if c % 2 == 0 else rest[::-1])
+
+    def rows_of(c):
+        return plan[c][2]
+
+    def bit(c, k):
+        return s // masks(c)[k] % 2
+
+    def kept(c, k):
+        size = rows_of(c)
+        return sum((bit(c, j) * (size >> (j + 1)) for j in range(1, k + 1)), 0)
+
+    def aligned(x, size):
+        return pl.multiple_of(x, size) if not isinstance(x, int) else x
+
+    def seq_copy(c, k):
+        array, first, size = plan[c]
+        half = size >> (k + 1)
+        other = (1 - bit(c, k)) * half
+        if k == 0:
+            source = grads[array].at[:, pl.ds(aligned(first + other, half), half)]
+        else:
+            source = owns[c].at[:, pl.ds(aligned(kept(c, k - 1) + other, half), half)]
+        return pltpu.make_async_remote_copy(
+            source, recvs[c][k], send_sem.at[c, k], recv_sem.at[c, k],
+            device_id=seq_peer(masks(c)[k]), device_id_type=MESH)
+
+    def load(c):
+        array, first, size = plan[c]
+        half = size // 2
+        return pltpu.make_async_copy(
+            grads[array].at[:, pl.ds(aligned(first + bit(c, 0) * half, half), half)], owns[c], load_sem.at[c])
+
+    def quarters(k):
+        low = z % (1 << k)
+        return [low + (i << k) for i in range(head >> k)]
+
+    def head_copies(c, k):
+        size = rows_of(c) // seq
+        at = pl.ds(aligned(kept(c, ns - 1), size), size)
+        low = z % (1 << k)
+        b = z // (1 << k) % 2
+        copies = []
+        for i in range(head >> (k + 1)):
+            q = low + (1 - b) * (1 << k) + (i << (k + 1))
+            copies.append(pltpu.make_async_remote_copy(
+                owns[c].at[q, at], recvs[c][ns + k].at[i], zsend.at[c, k, i], zrecv.at[c, k, i],
+                device_id=head_peer(1 << k), device_id_type=MESH))
+        return copies
+
+    def add(c, k):
+        size = rows_of(c)
+        if k < ns:
+            many, rows, first = head, size >> (k + 1), kept(c, k)
+            place = lambda i: i
+        else:
+            j = k - ns
+            many, rows, first = head >> (j + 1), size // seq, kept(c, ns - 1)
+            place = lambda i: z % (1 << j) + (z // (1 << j) % 2) * (1 << j) + i * (1 << (j + 1))
+        tile = min(16, rows)
+        tiles = rows // tile
+        received = recvs[c][k]
+
+        def one(t, carry):
+            i, r = t // tiles, t % tiles * tile
+            here = pl.ds(pl.multiple_of(first + r, tile), tile)
+            q = place(i)
+            owns[c][q, here] = (
+                owns[c][q, here].astype(f32) + received[i, pl.ds(pl.multiple_of(r, tile), tile)].astype(f32)
+            ).astype(bf16)
+            return carry
+
+        lax.fori_loop(0, many * tiles, one, 0)
+
+    def result_row(c, upto):
+        array, first, size = plan[c]
+        return first + sum(bit(c, j) * (size >> (j + 1)) for j in range(upto))
+
+    def keep(c):
+        array, first, size = plan[c]
+        rows = size // seq
+        return pltpu.make_async_copy(
+            owns[c].at[z, pl.ds(aligned(kept(c, ns - 1), rows), rows)],
+            outs[array].at[pl.ds(aligned(result_row(c, ns), rows), rows)], keep_sem.at[c])
+
+    def gather_copy(c, j):
+        array, first, size = plan[c]
+        level = ns - j
+        rows = size >> level
+        at = pl.ds(aligned(result_row(c, level), rows), rows)
+        return pltpu.make_async_remote_copy(
+            outs[array].at[at], outs[array].at[at], gsend.at[c, j], grecv.at[c, j],
+            device_id=seq_peer(masks(c)[level - 1]), device_id_type=MESH)
+
+    count = len(plan)
+    for c in range(count):
+        seq_copy(c, 0).start()
+        load(c).start()
+
+    def advance(c, k):
+        if k == 0:
+            load(c).wait()
+        if k < ns:
+            seq_copy(c, k).wait_recv()
+            add(c, k)
+        elif k < ns + nz:
+            for copy in head_copies(c, k - ns):
+                copy.wait_recv()
+            add(c, k)
+        elif k == ns + nz:
+            keep(c).wait()
+        else:
+            gather_copy(c, k - ns - nz - 1).wait_recv()
+        n = k + 1
+        if n < ns:
+            seq_copy(c, n).start()
+        elif n < ns + nz:
+            for copy in head_copies(c, n - ns):
+                copy.start()
+        elif n == ns + nz:
+            keep(c).start()
+        elif n - ns - nz - 1 < ns:
+            gather_copy(c, n - ns - nz - 1).start()
+
+    stages = ns + nz + 1 + ns
+    pairs = count // 2
+    for t in range(pairs + stages - 1):
+        for k in reversed(range(stages)):
+            p = t - k
+            if 0 <= p < pairs:
+                advance(2 * p, k)
+                advance(2 * p + 1, k)
+    for c in range(count):
+        for k in range(ns):
+            seq_copy(c, k).wait_send()
+        for k in range(nz):
+            for copy in head_copies(c, k):
+                copy.wait_send()
+        for j in range(ns):
+            gather_copy(c, j).wait_send()
+
+def reduce_all(arrays, cuts, collective_id):
+    seq, head = lax.axis_size("seq"), lax.axis_size("head")
+    ns, nz = len(bits_of(seq)), len(bits_of(head))
+    plan = []
+    for a, (array, cut) in enumerate(zip(arrays, cuts)):
+        rows = array.shape[1] // cut
+        plan += [(a, i * rows, rows) for i in range(cut)]
+    scratch = []
+    for a, first, size in plan:
+        scratch.append(pltpu.VMEM((head, size // 2, arrays[a].shape[2]), bf16))
+    for a, first, size in plan:
+        columns = arrays[a].shape[2]
+        scratch += [pltpu.VMEM((head, size >> (k + 1), columns), bf16) for k in range(ns)]
+        scratch += [pltpu.VMEM((head >> (k + 1), size // seq, columns), bf16) for k in range(nz)]
+    count = len(plan)
+    dma = pltpu.SemaphoreType.DMA
+    scratch += [dma((count,)), dma((count, ns)), dma((count, ns)), dma((count, nz, head // 2)), dma((count, nz, head // 2)),
+                dma((count, ns)), dma((count, ns)), dma((count,))]
+    anywhere = pl.BlockSpec(memory_space=pl.ANY)
+    return pl.pallas_call(
+        partial(reduce_body, seq, head, plan, len(arrays)),
+        out_shape=[jax.ShapeDtypeStruct(a.shape[1:], bf16) for a in arrays],
+        in_specs=[anywhere] * len(arrays),
+        out_specs=[anywhere] * len(arrays),
+        scratch_shapes=scratch,
+        compiler_params=pltpu.CompilerParams(
+            collective_id=collective_id, has_side_effects=True, vmem_limit_bytes=60 * 2**20),
+        name="reduce_gradients",
+    )(*arrays)
 
 
 def shifted(block, distance):
@@ -57,12 +265,6 @@
     mine = lax.dynamic_slice_in_dim(weight, lax.axis_index("seq") * part, part, 0)
     every = lax.all_gather(mine, ("head", "seq"), axis=0, tiled=True)
     return every.reshape(lax.axis_size("head"), *weight.shape)
-
-
-def reduced(grad):
-    flat = grad.astype(bf16).reshape(-1, grad.shape[-1])
-    mine = lax.psum_scatter(flat, ("head", "seq"), scatter_dimension=0, tiled=True)
-    return lax.all_gather(mine, "seq", axis=0, tiled=True).astype(f32)
 
 
 def exchange(log_total, value, back):
@@ -196,16 +398,16 @@
     layer_out = to_features(layer_out.astype(bf16)).astype(f32)
 
     d_hidden = rounded(dot("std,hfd->hstf", upstream, w_low))
-    grad_down = reduced(dot("hstf,std->hfd", hidden, upstream))
+    grad_down = dot("std,hstf->hdf", upstream, hidden).astype(bf16)
     d_gate_up = jnp.concatenate(
         [d_hidden * up_val * silu_slope(gate_val), d_hidden * gate_act], axis=-1
     ).astype(bf16)
-    grad_pair = reduced(dot("std,hstf->hdf", normed_two, d_gate_up))
+    grad_pair = dot("std,hstf->hdf", normed_two, d_gate_up).astype(bf16)
     d_normed_two = dot("hstf,hdf->std", d_gate_up, w_pair)
     d_hidden_in = upstream.astype(f32) + norm_back(hidden_in, second_scale, mlp_gain, d_normed_two)
     grad_mlp_gain = jnp.sum(d_normed_two * hidden_in * second_scale, axis=(0, 1))
     d_mixer = d_hidden_in.astype(bf16)
-    grad_out = reduced(dot("hste,std->hed", gated, d_mixer))
+    grad_out = dot("std,hste->hde", d_mixer, gated)
     d_gated = rounded(dot("std,hed->hste", d_mixer, w_proj))
     d_normed_out = d_gated * gate_silu
     d_gate_rows = d_gated * normed_out * silu_slope(gate_rows)
@@ -242,7 +444,14 @@
         edge_back, ((0, 0), (0, 0), (mine - tap_count + 1, 0), (0, 0))
     )
     d_projected = jnp.concatenate([d_mixed, d_gate_rows], axis=-1).astype(bf16)
-    grad_mixer = reduced(dot("std,hste->hde", normed, d_projected))
+    grad_mixer = dot("std,hste->hde", normed, d_projected)
+    grad_mixer = jnp.concatenate([grad_mixer, grad_out], axis=2).astype(bf16)
+    grad_pair, grad_down, grad_mixer = (
+        a.astype(f32) for a in reduce_all((grad_pair, grad_down, grad_mixer), (4, 4, 4), 1)
+    )
+    grad_down = grad_down.T
+    mixer_width = conv_width + value_width
+    grad_out = grad_mixer[:, mixer_width:].T
     d_normed = dot("hste,hde->std", d_projected, w_mixer)
     tokens_grad = d_hidden_in + norm_back(resid, first_scale, attn_gain, d_normed)
     tokens_grad = to_features(tokens_grad.astype(bf16)).astype(f32)
@@ -264,7 +473,7 @@
         grad_mixer[:, :key_width],
         grad_mixer[:, key_width : 2 * key_width],
         grad_mixer[:, 2 * key_width : conv_width],
-        grad_mixer[:, conv_width:],
+        grad_mixer[:, conv_width:mixer_width],
         grad_taps[:, :key_width],
         grad_taps[:, key_width : 2 * key_width],
         grad_taps[:, 2 * key_width :],

time: 1120 us -> 785 us (0.70)
  waiting for transfers between devices: 669 us -> 163 us
  Pallas kernels: 0 us -> 166 us
  blocking collectives: 106 us -> 84.5 us
  other arithmetic: 72.1 us -> 83.8 us
    reduce_scatter x3 -> x0, waiting for transfers between devices: 253 us -> none  [reduced(): lax.psum_scatter(flat, ('head', 'seq'), scatter_dimension=0, tiled=True)]
    pallas_call x0 -> x1, Pallas kernels: none -> 166 us  [reduce_all(): pl.pallas_call(partial(reduce_body, seq, head, plan, len(arrays)), out_sh...]
    unnamed x12 -> x4, waiting for transfers between devices: 144 us -> 0.07 us
    all_gather x3 -> x0, waiting for transfers between devices: 67.7 us -> none  [reduced(): return lax.all_gather(mine, 'seq', axis=0, tiled=True).astype(f32)]
    all_to_all x2, waiting for transfers between devices: 33 us -> 17.1 us  [exchange(): lax.all_to_all(value.astype(bf16).reshape(count, part, width), BOTH, 0, 0...]
    psum x1, blocking collectives: 53.7 us -> 38.7 us  [local(): small = lax.psum(small.astype(bf16), BOTH).astype(f32)]
    all_gather x1 -> x0, blocking collectives: 14.7 us -> none  [reduced(): return lax.all_gather(mine, 'seq', axis=0, tiled=True).astype(f32)]
    all_to_all x2, waiting for transfers between devices: 22.5 us -> 8.38 us  [to_features(): return lax.all_to_all(array, 'head', 2, 1, tiled=True)]
  transfers between devices with their start and end apart: 23 -> 16, of which waited for: 17 -> 9; matrix products, arithmetic and copies ran while one was open for 15% -> 24% of each run, Pallas kernels for 0% -> 21%
where the time goes in v2:
time: 785 us; the launch traced here: 779 us
  Pallas kernels  166 us (21%)
  waiting for transfers between devices  163 us (21%)
  matrix products  120 us (15%)
  local copies, waits for them, and re-layouts  88.2 us (11%)
  blocking collectives  84.5 us (11%)
  other arithmetic  83.8 us (11%)
  starting transfers between devices  58.6 us (7%)
  between operations  14.9 us (2%)
    pallas_call x1, Pallas kernels, reduce_all(): pl.pallas_call(partial(reduce_body, seq, head, plan, len(arrays)), out_sh...  166 us
    dot_general x24, matrix products, dot(): jnp.einsum(spec, left.astype(bf16), right.astype(bf16), preferred_element...  115 us
    all_gather x4, waiting for transfers between devices, whole(): every = lax.all_gather(mine, ('head', 'seq'), axis=0, tiled=True)  72.9 us
    all_gather x1, blocking collectives, local(): lax.all_gather(jnp.concatenate([conv_query, conv_key, conv_value], axis=1...  45.8 us
    all_to_all x3, waiting for transfers between devices, to_tokens(): return lax.all_to_all(array, 'head', 1, 2, tiled=True)  45.5 us
    psum x1, blocking collectives, local(): small = lax.psum(small.astype(bf16), BOTH).astype(f32)  38.7 us
    unnamed x112, local copies, waits for them, and re-layouts  31 us
    all_to_all x2, waiting for transfers between devices, exchange(): ours = lax.all_to_all(total.astype(bf16), BOTH, 0, 0, tiled=True)  17.5 us
  transfers between devices with their start and end apart: 16, of which 9 were waited for; matrix products, arithmetic and copies ran while one was open for 24% of the time, Pallas kernels for 21%

profile of v2, /device:TPU:1, one launch (start us, length us, event | category | flops | bytes accessed | tf_op | source)
XLA Modules:
  0.0 779.2 jit_solution(7682126352697162110)
XLA Ops:
  19.6 5.6 all-to-all-start.1
  27.2 15.0 %all-to-all-done.1 = s16[2,1024,128]{2,0,1:T(2,128)(2,1)S(1)} async-done(((s16[2,1024,128]{2,0,1:T(2,128)(2,1)}), s16[2,1024,128]{2,0,1:T(2,128)(2,1)S(1)}, u32[]{:S(2)}, u32[]{:S(2)}) %all-to-all-start.1) | async-done | bytes 524320 | tf_op jit(solution)/shard_map/all_to_all | solution.py:318
  46.5 45.8 %all-gather.1 = f32[4,4,512]{2,1,0:T(4,128)S(1)} all-gather(f32[1,4,512]{2,1,0:T(4,128)S(1)} %maximum_bitcast_fusion.1), channel_id=2, replica_groups=mesh['seq'=8,'head'=4] {'head'}, dimensions={0}, use_global_device_ids=true | all-gather | bytes 40960 | tf_op jit(solution)/shard_map/all_gather | solution.py:333
  101.0 6.5 convert_bitcast_fusion.1
  112.4 10.1 %all-to-all-start.3 = ((f32[32,1,32]{2,1,0:T(1,128)}), f32[32,1,32]{2,1,0:T(1,128)S(1)}, u32[]{:S(2)}, u32[]{:S(2)}) async-start(f32[32,1,32]{2,1,0:T(1,128)} %bitcast.28), calls=%async_computation.3 | async-start | bytes 32768 | tf_op jit(solution)/shard_map/all_to_all | solution.py:275
  135.6 5.9 all-to-all-start.2
  144.8 17.1 %all-to-all-done.2 = bf16[32,32,256]{2,1,0:T(8,128)(2,1)} async-done(((bf16[32,32,256]{2,1,0:T(8,128)(2,1)}), bf16[32,32,256]{2,1,0:T(8,128)(2,1)}, u32[]{:S(2)}, u32[]{:S(2)}) %all-to-all-start.2) | async-done | bytes 524320 | tf_op jit(solution)/shard_map/all_to_all | solution.py:274
  161.9 4.2 all-to-all-start.6
  169.4 30.6 %all-to-all-done.6 = bf16[2,1024,256]{2,0,1:T(2,128)(2,1)} async-done(((bf16[2,1024,256]{2,0,1:T(2,128)(2,1)}), bf16[2,1024,256]{2,0,1:T(2,128)(2,1)}, u32[]{:S(2)}, u32[]{:S(2)}) %all-to-all-start.6) | async-done | bytes 1048608 | tf_op jit(solution)/shard_map/all_to_all | solution.py:318
  220.7 10.8 %all-to-all-done.4 = bf16[32,32,256]{2,1,0:T(8,128)(2,1)} async-done(((bf16[32,32,256]{2,1,0:T(8,128)(2,1)}), bf16[32,32,256]{2,1,0:T(8,128)(2,1)}, u32[]{:S(2)}, u32[]{:S(2)}) %all-to-all-start.4) | async-done | bytes 524320 | tf_op jit(solution)/shard_map/all_to_all | solution.py:289
  242.1 4.7 convert_reduce_fusion.1
  257.6 17.9 %all-gather.11.cloned.1.call-done = bf16[4096,1408]{1,0:T(8,128)(2,1)} async-done(((bf16[128,1408]{1,0:T(8,128)(2,1)}), bf16[4096,1408]{1,0:T(8,128)(2,1)}) %all-gather.11.cloned.1.call-update) | async-done | bytes 11534352 | tf_op jit(solution)/shard_map/all_gather | solution.py:266
  275.5 13.5 %convolution_bitcast_fusion = f32[4,2,256,1408]{2,3,1,0:T(8,128)} fusion(bf16[4,1024,1408,1]{2,1,3,0:T(8,128)(2,1)} %bitcast.333, bf16[2,256,1024,1]{2,1,0,3:T(8,128)(2,1)S(1)} %reshape.320), kind=kOutput, calls=%fused_computation.7 | convolution fusion | flops 5905580032 | bytes 24117248 | tf_op jit(solution)/shard_map/std,hdf->hstf/dot_general | solution.py:253
  289.1 55.0 %all-gather.13.cloned.1.call-done = bf16[2816,1024]{1,0:T(8,128)(2,1)} async-done(((bf16[88,1024]{1,0:T(8,128)(2,1)}), bf16[2816,1024]{1,0:T(8,128)(2,1)}) %all-gather.13.cloned.1.call-update) | async-done | bytes 5767184 | tf_op jit(solution)/shard_map/all_gather | solution.py:266
  344.1 11.8 %fusion.3 = (bf16[4,2,256,704]{2,3,1,0:T(8,128)(2,1)}, bf16[4,2,256,704]{2,3,1,0:T(8,128)(2,1)}, bf16[4,2,256,704]{2,3,1,0:T(8,128)(2,1)}) fusion(f32[4,2,256,1408]{2,3,1,0:T(8,128)} %convolution_bitcast_fusion, bf16[4,704,1024,1]{2,1,3,0:T(8,128)(2,1)} %bitcast.337, bf16[2,256,1024,1]{2,1,0,3:T(8,128)(2,1)S(1)} %copy-done.36), kind=kOutput, calls=%fused_computation.13 | convolution fusion | flops 2977300480 | bytes 27000832 | tf_op jit(solution)/shard_map/std,hfd->hstf/dot_general | solution.py:253
  355.8 13.9 %fusion.20 = (bf16[1024]{0:T(1024)(128)(2,1)S(1)}, f32[2,256]{1,0:T(2,128)S(1)}, f32[2,256,1024]{2,1,0:T(8,128)}, f32[2,256,1024,1]{2,1,0,3:T(8,128)}) fusion(f32[2,256]{1,0:T(2,128)S(1)} %get-tuple-element.153, f32[1024]{0:T(1024)S(1)} %copy-done.38, f32[2,256,1024]{2,1,0:T(8,128)} %reshape.300, f32[2,256,1024]{2,1,0:T(8,128)} %convert_reduce_fusion.1, ...), kind=kOutput, calls=%fused_computation.64 | convolution fusion | flops 5920782848 | bytes 25700352 | tf_op jit(solution)/shard_map/hstf,hdf->std/dot_general | solution.py:253
  393.2 7.8 bitcast_convert_fusion.2
  401.0 8.5 %copy.164 = bf16[4,704,1024]{1,2,0:T(8,128)(2,1)} copy(bf16[4,704,1024]{2,1,0:T(8,128)(2,1)} %bitcast_convert_fusion.2) | data formatting | bytes 11534336 | tf_op jit(solution)/shard_map/convert_element_type | solution.py:401
  409.4 11.5 %fusion.refs_0_ = bf16[4,1024,1408]{2,1,0:T(8,128)(2,1)} fusion(bf16[4,2,256,704]{2,3,1,0:T(8,128)(2,1)} %get-tuple-element.108, bf16[4,2,256,704]{2,3,1,0:T(8,128)(2,1)} %get-tuple-element.107, f32[2,256,1024]{2,1,0:T(8,128)} %get-tuple-element.101, f32[1024]{0:T(1024)S(1)} %copy-done.38, f32[2,256]{1,0:T(2,128)S(1)} %get-tuple-element.153), kind=kOutput, calls=%fused_computation.3 | convolution fusion | flops 5924454400 | bytes 19404800 | tf_op jit(solution)/shard_map/std,hstf->hdf/dot_general | solution.py:253
  423.9 6.5 all-to-all-start.8
  430.5 8.4 %convert_reduce_fusion = f32[2,256,1024]{2,1,0:T(8,128)} fusion(bf16[4,2,256,704]{2,3,1,0:T(8,128)(2,1)} %get-tuple-element.109, bf16[4,704,1024,1]{2,1,3,0:T(8,128)(2,1)} %bitcast.338), kind=kOutput, calls=%fused_computation.5 | convolution fusion | flops 2958557184 | bytes 10747904 | tf_op jit(solution)/shard_map/hstf,hfd->hstd/dot_general | solution.py:253
  438.9 6.7 all-to-all-done.8
  455.4 4.8 multiply_reduce_fusion.3
  460.2 6.7 broadcast_multiply_fusion.3
  467.8 6.3 pad_add_fusion
  482.8 7.2 fusion.18
  494.2 5.4 all-to-all-start.5
  499.6 7.5 fusion.1
  507.1 38.7 %psum.7 = bf16[10496]{0:T(1024)(128)(2,1)S(1)} all-reduce(bf16[10496]{0:T(1024)(128)(2,1)S(1)} %pad_maximum_fusion.10), channel_id=1, replica_groups=mesh['seq'=8,'head'=4] {'seq','head'}, use_global_device_ids=true, to_apply=%region_16.17 | all-reduce | flops 10496 | bytes 41984 | tf_op jit(solution)/shard_map/psum | solution.py:461
  546.4 7.8 pad_maximum_fusion.refs_2_
  554.2 165.8 %reduce_gradients.1 = (bf16[1024,1408]{1,0:T(8,128)(2,1)}, bf16[1024,704]{1,0:T(8,128)(2,1)}, bf16[1024,1024]{1,0:T(8,128)(2,1)}) custom-call(bf16[4,1024,1408]{2,1,0:T(8,128)(2,1)} %fusion.refs_0_, bf16[4,1024,704]{2,1,0:T(8,128)(2,1)} %bitcast.291, bf16[4,1024,1024]{2,1,0:T(8,128)(2,1)} %pad_maximum_fusion.refs_2_), custom_call_target="tpu_custom_call" | custom-call | tf_op jit(solution)/shard_map/reduce_gradients/pallas_call | solution.py:214
  758.8 8.4 %all-to-all-done.9 = bf16[2,256,1024]{1,0,2:T(2,128)(2,1)S(1)} async-done(((bf16[2,256,1024]{1,0,2:T(2,128)(2,1)}), bf16[2,256,1024]{1,0,2:T(2,128)(2,1)S(1)}, u32[]{:S(2)}, u32[]{:S(2)}) %all-to-all-start.9) | async-done | bytes 1048608 | tf_op jit(solution)/shard_map/all_to_all | solution.py:321
  (243 shorter events, 187.9 us)
Async XLA Ops:
  7.2 38.6 %copy-start = (bf16[704,1024]{1,0:T(8,128)(2,1)S(1)}, bf16[704,1024]{1,0:T(8,128)(2,1)}, u32[]{:S(2)}) copy-start(bf16[704,1024]{1,0:T(8,128)(2,1)} %param.33) | copy-start | bytes 4325380
  7.2 93.8 %all-gather.7.cloned.1.call-start = ((), (), s32[]{:S(2)}) async-start(), calls=%async_computation.10 | async-start | bytes 6488064 | tf_op jit(solution)/shard_map/all_gather | solution.py:266
  8.9 233.1 %all-gather.9.cloned.1.call-start = ((), (), s32[]{:S(2)}) async-start(), calls=%async_computation.11 | async-start | bytes 2162688 | tf_op jit(solution)/shard_map/all_gather | solution.py:266
  10.5 265.0 %all-gather.11.cloned.1.call-start = ((), (), s32[]{:S(2)}) async-start(), calls=%async_computation.12 | async-start | bytes 11894784 | tf_op jit(solution)/shard_map/all_gather | solution.py:266
  16.6 8.5 %copy-start.35 = (bf16[2,1024,256]{2,1,0:T(8,128)(2,1)S(1)}, bf16[2,1024,256]{2,1,0:T(8,128)(2,1)}, u32[]{:S(2)}) copy-start(bf16[2,1024,256]{2,1,0:T(8,128)(2,1)} %param.17) | copy-start | bytes 3145732
  19.5 26.9 %copy-start.41 = (f32[1024]{0:T(1024)S(1)}, f32[1024]{0:T(1024)}, u32[]{:S(2)}) copy-start(f32[1024]{0:T(1024)} %param.20) | copy-start | bytes 12292
  19.6 26.9 %copy-start.44 = (f32[4,256]{1,0:T(4,128)S(1)}, f32[4,256]{1,0:T(4,128)}, u32[]{:S(2)}) copy-start(f32[4,256]{1,0:T(4,128)} %param.27) | copy-start | bytes 12292
  19.6 26.9 %copy-start.46 = (f32[4,128]{1,0:T(4,128)S(1)}, f32[4,128]{1,0:T(4,128)}, u32[]{:S(2)}) copy-start(f32[4,128]{1,0:T(4,128)} %param.26) | copy-start | bytes 6148
  19.6 26.9 %copy-start.47 = (f32[4,128]{1,0:T(4,128)S(1)}, f32[4,128]{1,0:T(4,128)}, u32[]{:S(2)}) copy-start(f32[4,128]{1,0:T(4,128)} %param.25) | copy-start | bytes 6148
  19.6 22.6 %all-to-all-start.1 = ((s16[2,1024,128]{2,0,1:T(2,128)(2,1)}), s16[2,1024,128]{2,0,1:T(2,128)(2,1)S(1)}, u32[]{:S(2)}, u32[]{:S(2)}) async-start(s16[2,1024,128]{2,0,1:T(2,128)(2,1)} %copy_convert_fusion), calls=%async_computation.1 | async-start | bytes 1048576 | tf_op jit(solution)/shard_map/all_to_all | solution.py:318
  42.2 52.8 %all-to-all-start = ((bf16[2,1024,256]{2,0,1:T(2,128)(2,1)}), bf16[2,1024,256]{2,0,1:T(2,128)(2,1)S(1)}, u32[]{:S(2)}, u32[]{:S(2)}) async-start(bf16[2,1024,256]{2,0,1:T(2,128)(2,1)} %copy.138), calls=%async_computation | async-start | bytes 2097152 | tf_op jit(solution)/shard_map/all_to_all | solution.py:318
  45.7 298.4 %all-gather.13.cloned.1.call-start = ((), (), s32[]{:S(2)}) async-start(), calls=%async_computation.13 | async-start | bytes 5947392 | tf_op jit(solution)/shard_map/all_gather | solution.py:266
  98.1 9.4 %copy-start.39 = (f32[2,256]{1,0:T(2,128)}, f32[2,256]{1,0:T(2,128)S(1)}, u32[]{:S(2)}) copy-start(f32[2,256]{1,0:T(2,128)S(1)} %get-tuple-element.151) | copy-start | bytes 6148
  109.2 13.4 %collective-permute-start = (bf16[4,2,3,512]{3,2,1,0:T(4,128)(2,1)S(1)}, bf16[4,2,3,512]{3,2,1,0:T(4,128)(2,1)S(1)}, u32[]{:S(2)}, u32[]{:S(2)}) collective-permute-start(bf16[4,2,3,512]{3,2,1,0:T(4,128)(2,1)S(1)} %slice.194), channel_id=1, source_target_pairs={{0,1},{1,2},{2,3},{3,4},{4,5},{5,6},{6,7},{7,8},{8,9},{9,10},{10,1... | collective-permute-start | bytes 73736 | tf_op jit(solution)/shard_map/ppermute | solution.py:229
  112.4 23.2 %all-to-all-start.3 = ((f32[32,1,32]{2,1,0:T(1,128)}), f32[32,1,32]{2,1,0:T(1,128)S(1)}, u32[]{:S(2)}, u32[]{:S(2)}) async-start(f32[32,1,32]{2,1,0:T(1,128)} %bitcast.28), calls=%async_computation.3 | async-start | bytes 32768 | tf_op jit(solution)/shard_map/all_to_all | solution.py:275
  135.6 26.3 %all-to-all-start.2 = ((bf16[32,32,256]{2,1,0:T(8,128)(2,1)}), bf16[32,32,256]{2,1,0:T(8,128)(2,1)}, u32[]{:S(2)}, u32[]{:S(2)}) async-start(bf16[32,32,256]{2,1,0:T(8,128)(2,1)} %add_convert_fusion.2), calls=%async_computation.2 | async-start | bytes 1048576 | tf_op jit(solution)/shard_map/all_to_all | solution.py:274
  144.8 59.3 %copy-start.38 = (f32[1024]{0:T(1024)S(1)}, f32[1024]{0:T(1024)}, u32[]{:S(2)}) copy-start(f32[1024]{0:T(1024)} %param.30) | copy-start | bytes 12292
  161.9 38.1 %all-to-all-start.6 = ((bf16[2,1024,256]{2,0,1:T(2,128)(2,1)}), bf16[2,1024,256]{2,0,1:T(2,128)(2,1)}, u32[]{:S(2)}, u32[]{:S(2)}) async-start(bf16[2,1024,256]{2,0,1:T(2,128)(2,1)} %copy.152), calls=%async_computation.6 | async-start | bytes 2097152 | tf_op jit(solution)/shard_map/all_to_all | solution.py:318
  200.0 31.5 %all-to-all-start.4 = ((bf16[32,32,256]{2,1,0:T(8,128)(2,1)}), bf16[32,32,256]{2,1,0:T(8,128)(2,1)}, u32[]{:S(2)}, u32[]{:S(2)}) async-start(bf16[32,32,256]{2,1,0:T(8,128)(2,1)} %copy.146), calls=%async_computation.4 | async-start | bytes 1048576 | tf_op jit(solution)/shard_map/all_to_all | solution.py:289
  275.5 68.5 %copy-start.36 = (bf16[2,256,1024,1]{2,1,0,3:T(8,128)(2,1)S(1)}, bf16[2,256,1024,1]{2,1,0,3:T(8,128)(2,1)}, u32[]{:S(2)}) copy-start(bf16[2,256,1024,1]{2,1,0,3:T(8,128)(2,1)} %reshape.322) | copy-start | bytes 3145732
  355.8 13.9 %copy-start.15 = (bf16[2,256,1024]{2,1,0:T(8,128)(2,1)S(1)}, bf16[2,256,1024]{2,1,0:T(8,128)(2,1)}, u32[]{:S(2)}) copy-start(bf16[2,256,1024]{2,1,0:T(8,128)(2,1)} %all_to_all.73) | copy-start | bytes 3145732
  389.6 31.4 %all-to-all-start.7 = ((bf16[32,32,256]{2,1,0:T(8,128)(2,1)}), bf16[32,32,256]{2,1,0:T(8,128)(2,1)}, u32[]{:S(2)}, u32[]{:S(2)}) async-start(bf16[32,32,256]{2,1,0:T(8,128)(2,1)} %bitcast.311), calls=%async_computation.7 | async-start | bytes 1048576 | tf_op jit(solution)/shard_map/all_to_all | solution.py:274
  423.9 21.7 %all-to-all-start.8 = ((bf16[32,32,256]{2,1,0:T(8,128)(2,1)}), bf16[32,32,256]{2,1,0:T(8,128)(2,1)}, u32[]{:S(2)}, u32[]{:S(2)}) async-start(bf16[32,32,256]{2,1,0:T(8,128)(2,1)} %copy.159), calls=%async_computation.8 | async-start | bytes 1048576 | tf_op jit(solution)/shard_map/all_to_all | solution.py:289
  474.2 5.7 collective-permute-start.1
  482.7 7.3 copy-start.33
  482.7 7.3 copy-start.16
  482.7 7.3 copy-start.17
  482.8 7.3 copy-start.18
  482.8 7.3 copy-start.32
  482.8 7.3 copy-start.43
  494.2 243.5 %all-to-all-start.5 = ((bf16[2,256,1024]{1,0,2:T(2,128)(2,1)}), bf16[2,256,1024]{1,0,2:T(2,128)(2,1)}, u32[]{:S(2)}, u32[]{:S(2)}) async-start(bf16[2,256,1024]{1,0,2:T(2,128)(2,1)} %copy.150), calls=%async_computation.5 | async-start | bytes 2097152 | tf_op jit(solution)/shard_map/all_to_all | solution.py:321
  737.7 29.4 %all-to-all-start.9 = ((bf16[2,256,1024]{1,0,2:T(2,128)(2,1)}), bf16[2,256,1024]{1,0,2:T(2,128)(2,1)S(1)}, u32[]{:S(2)}, u32[]{:S(2)}) async-start(bf16[2,256,1024]{1,0,2:T(2,128)(2,1)} %copy.161), calls=%async_computation.9 | async-start | bytes 2097152 | tf_op jit(solution)/shard_map/all_to_all | solution.py:321
  (35 other events, 92.6 us)
Sparse Core Ops, SparseCore 0:
  11.5 86.8 all-gather.6
  101.2 59.9 all-gather.8
  164.6 110.8 all-gather.10
  278.2 65.7 all-gather.12

commit v3 on v1

v3 whole, which is shorter than its diff:
```python
from functools import partial

import jax
import jax.numpy as jnp
from jax import lax
from jax.experimental import pallas as pl
from jax.experimental.pallas import tpu as pltpu
from jax.sharding import PartitionSpec as P

SPAN = 64
KEY_HEAD = 128
HALO = 16
MESH = pl.DeviceIdType.MESH

epsilon = 1e-06
decay_unit = 2.0 ** (-17)
f32 = jnp.float32
bf16 = jnp.bfloat16

def flipped(place, mask):
    return place + mask - 2 * mask * (place // mask % 2)


def start_body(seq, n_weights, items, *refs):
    tokens, codes, cotangent = refs[:3]
    weights = refs[3 : 3 + n_weights]
    out_tokens, out_codes, out_cotangent = refs[3 + n_weights : 6 + n_weights]
    n_sem = 13
    gathered = refs[6 + n_weights : -n_sem]
    (tsend, trecv, csend, crecv, hsend, hrecv, stay, zsend, zrecv, ysend, yrecv, gsend, grecv) = refs[-n_sem:]
    s, z = lax.axis_index("seq"), lax.axis_index("head")
    heads = 4
    masks = [1, 2, 4]

    def peer(to_s, to_z):
        return {"seq": to_s, "head": to_z}

    barrier = pltpu.get_barrier_semaphore()

    def greet(to_s, to_z):
        pl.semaphore_signal(barrier, 1, device_id=peer(to_s, to_z), device_id_type=MESH)

    for d in range(1, heads):
        greet(s, (z + d) % heads)
    for mask in masks:
        greet(flipped(s, mask), z)

    @pl.when((z == 0) & (s > 0))
    def _():
        for q in range(heads):
            greet(s - 1, q)

    greeted = heads - 1 + len(masks)

    @pl.when(s < seq - 1)
    def _():
        pl.semaphore_wait(barrier, greeted + 1)

    @pl.when(s == seq - 1)
    def _():
        pl.semaphore_wait(barrier, greeted)

    seqs, rows, width = tokens.shape
    mine = rows // heads

    def remote(src, dst, send, recv, to_s, to_z):
        return pltpu.make_async_remote_copy(src, dst, send, recv, device_id=peer(to_s, to_z), device_id_type=MESH)

    def columns(ref, q):
        n = ref.shape[2] // heads
        return pl.ds(pl.multiple_of(q * n, n), n)

    def sends(target, act):
        here = pl.ds(target * mine, mine)
        if target == 0:
            src, dst = tokens.at[:, pl.ds(0, mine)], out_tokens.at[:, pl.ds(HALO, mine), columns(out_tokens, z)]
        else:
            src = tokens.at[:, pl.ds(target * mine - HALO, mine + HALO)]
            dst = out_tokens.at[:, :, columns(out_tokens, z)]
        triples = [
            (src, dst),
            (codes.at[:, here], out_codes.at[:, :, columns(out_codes, z)]),
            (cotangent.at[:, here], out_cotangent.at[:, :, columns(out_cotangent, z)]),
        ]

        @pl.when(z == target)
        def _():
            for i, (a, b) in enumerate(triples):
                copy = pltpu.make_async_copy(a, b, stay.at[i])
                if act == "start":
                    copy.start()
                else:
                    copy.wait()

        @pl.when(z != target)
        def _():
            for i, (a, b) in enumerate(triples):
                copy = remote(a, b, tsend.at[i, target], trecv.at[i, z], s, target)
                if act == "start":
                    copy.start()
                else:
                    copy.wait_send()

    def arrive(source):
        @pl.when(z != source)
        def _():
            here = pl.ds(0, mine)

            @pl.when(z == 0)
            def _():
                dst = out_tokens.at[:, pl.ds(HALO, mine), columns(out_tokens, source)]
                remote(tokens.at[:, here], dst, tsend.at[0, source], trecv.at[0, source], s, source).wait_recv()

            @pl.when(z != 0)
            def _():
                dst = out_tokens.at[:, :, columns(out_tokens, source)]
                remote(
                    tokens.at[:, pl.ds(0, mine + HALO)], dst, tsend.at[0, source], trecv.at[0, source], s, source
                ).wait_recv()

            for i, (a, b) in enumerate(((codes, out_codes), (cotangent, out_cotangent))):
                remote(
                    a.at[:, here], b.at[:, :, columns(b, source)], tsend.at[i + 1, source], trecv.at[i + 1, source],
                    s, source,
                ).wait_recv()

    def halo_copy(source, to_s):
        return remote(
            tokens.at[:, pl.ds(rows - HALO, HALO)], out_tokens.at[:, pl.ds(0, HALO), columns(out_tokens, source)],
            hsend, hrecv.at[source], to_s, 0,
        )

    @pl.when(s < seq - 1)
    def _():
        halo_copy(z, s + 1).start()

    def order(i):
        return [4, 2, 1] if i % 2 == 0 else [2, 4, 1]

    def span(i, j):
        weight, _, axis, first, count, _ = items[i]
        size = count if axis == 0 else weights[weight].shape[1]
        begin = first if axis == 0 else 0
        for k, mask in enumerate(reversed(order(i))):
            if k < len(masks) - j:
                size = size // 2
                begin = begin + (s // mask % 2) * size
        return pl.multiple_of(begin, size), size

    def piece(i, j):
        weight, _, axis, first, count, column = items[i]
        begin, size = span(i, j)
        wide = weights[weight].shape[1]
        if axis == 0:
            own = weights[weight].at[pl.ds(begin, size)]
            place = lambda ref, q: ref.at[q, pl.ds(begin, size), pl.ds(column, wide)]
        else:
            own = weights[weight].at[pl.ds(first, count), pl.ds(begin, size)]
            place = lambda ref, q: ref.at[q, pl.ds(first, count), pl.ds(begin, size)]
        return own, place

    def own_copy(i):
        weight, to, axis, first, count, column = items[i]
        wide = weights[weight].shape[1]
        return pltpu.make_async_copy(
            weights[weight].at[pl.ds(first, count)],
            gathered[to].at[z, pl.ds(first, count), pl.ds(column, wide)], stay.at[3 + i])

    def far_copy(i):
        own, place = piece(i, 0)
        return remote(own, place(gathered[items[i][1]], z), zsend.at[i], zrecv.at[i], s, flipped(z, 2))

    def near_copies(i):
        own, place = piece(i, 0)
        to = gathered[items[i][1]]
        far = flipped(z, 2)
        near = flipped(z, 1)
        return [
            remote(own, place(to, z), ysend.at[i, 0], yrecv.at[i, 0], s, near),
            remote(place(to, far), place(to, far), ysend.at[i, 1], yrecv.at[i, 1], s, near),
        ]

    def seq_copies(i, j):
        _, place = piece(i, j)
        to = gathered[items[i][1]]
        other = flipped(s, order(i)[j])
        return [
            remote(place(to, (z + d) % heads), place(to, (z + d) % heads), gsend.at[i, j, d - 1], grecv.at[i, j, d - 1],
                   other, z)
            for d in range(1, heads)
        ]

    count = len(items)
    for i in range(count):
        far_copy(i).start()
    for target in range(heads):
        sends(target, "start")
    for i in range(count):
        own_copy(i).start()

    def advance(i, k):
        if k == 0:
            far_copy(i).wait_recv()
        elif k == 1:
            for copy in near_copies(i):
                copy.wait_recv()
        else:
            for copy in seq_copies(i, k - 2):
                copy.wait_recv()
        if k == 0:
            for copy in near_copies(i):
                copy.start()
        elif k - 1 < len(masks):
            for copy in seq_copies(i, k - 1):
                copy.start()

    stages = 2 + len(masks)
    pairs = count // 2
    for t in range(pairs + stages - 1):
        for k in reversed(range(stages)):
            p = t - k
            if 0 <= p < pairs:
                advance(2 * p, k)
                advance(2 * p + 1, k)
    for source in range(heads):
        arrive(source)
    for target in range(heads):
        sends(target, "wait")

    @pl.when((z == 0) & (s > 0))
    def _():
        for q in range(heads):
            halo_copy(q, s - 1).wait_recv()

    @pl.when(s < seq - 1)
    def _():
        halo_copy(z, s + 1).wait_send()

    for i in range(count):
        own_copy(i).wait()
        far_copy(i).wait_send()
        for copy in near_copies(i):
            copy.wait_send()
        for j in range(len(masks)):
            for copy in seq_copies(i, j):
                copy.wait_send()


def start_all(tokens, codes, cotangent, weights, items, shapes, collective_id):
    seq, heads = lax.axis_size("seq"), lax.axis_size("head")
    seqs, rows, width = tokens.shape
    mine = rows // heads
    count = len(items)
    dma = pltpu.SemaphoreType.DMA
    anywhere = pl.BlockSpec(memory_space=pl.ANY)
    out_shape = [
        jax.ShapeDtypeStruct((seqs, mine + HALO, heads * width), tokens.dtype),
        jax.ShapeDtypeStruct((seqs, mine, heads * codes.shape[2]), codes.dtype),
        jax.ShapeDtypeStruct((seqs, mine, heads * width), cotangent.dtype),
    ] + [jax.ShapeDtypeStruct((heads, *shape), bf16) for shape in shapes]
    return pl.pallas_call(
        partial(start_body, seq, len(weights), items),
        out_shape=out_shape,
        in_specs=[anywhere] * (3 + len(weights)),
        out_specs=[anywhere] * len(out_shape),
        scratch_shapes=[
            dma((3, heads)), dma((3, heads)), dma((1,)), dma((1,)), dma, dma((heads,)), dma((3 + count,)),
            dma((count,)), dma((count,)), dma((count, 2)), dma((count, 2)), dma((count, 3, 3)), dma((count, 3, 3)),
        ],
        compiler_params=pltpu.CompilerParams(collective_id=collective_id, has_side_effects=True),
        name="start_exchange",
    )(tokens, codes, cotangent, *weights)


def exchange_body(count, heads, per_block, backward, value, logs, out, packed, got, ready, send, recv, bsend, brecv):
    me = lax.axis_index("seq") * heads + lax.axis_index("head")
    part = value.shape[0] // count
    tail = packed.shape[1] - part
    others = count - 1

    def peer(p):
        return {"seq": p // heads, "head": p % heads}

    barrier = pltpu.get_barrier_semaphore()

    def greet(d, carry):
        pl.semaphore_signal(barrier, 1, device_id=peer((me + d) % count), device_id_type=MESH)
        return carry

    lax.fori_loop(1, count, greet, 0)
    high = logs[...].astype(bf16)
    low = (logs[...] - high.astype(f32)).astype(bf16)

    def pack(p, carry):
        packed[p, pl.ds(0, part)] = value[pl.ds(pl.multiple_of(p * part, part), part)]
        return carry

    lax.fori_loop(0, count, pack, 0)
    parts_each = count * per_block // value.shape[0]
    for b in range(logs.shape[0]):
        both = jnp.concatenate([high[b : b + 1], low[b : b + 1], jnp.zeros((tail - 2, high.shape[1]), bf16)], axis=0)
        for i in range(parts_each):
            packed[b * parts_each + i, pl.ds(part, tail)] = both
    got[me] = packed[me]
    pl.semaphore_wait(barrier, others)

    def there(p):
        return pltpu.make_async_remote_copy(
            packed.at[p], got.at[me], send.at[p], recv.at[me], device_id=peer(p), device_id_type=MESH)

    def here(p):
        return pltpu.make_async_remote_copy(
            packed.at[p], got.at[p], send.at[p], recv.at[p], device_id=peer(p), device_id_type=MESH)

    def back(p):
        return pltpu.make_async_remote_copy(
            ready.at[p], out.at[pl.ds(pl.multiple_of(me * part, part), part)], bsend.at[p], brecv.at[me],
            device_id=peer(p), device_id_type=MESH)

    def home(p):
        return pltpu.make_async_remote_copy(
            ready.at[p], out.at[pl.ds(pl.multiple_of(p * part, part), part)], bsend.at[p], brecv.at[p],
            device_id=peer(p), device_id_type=MESH)

    def each(act):
        def one(d, carry):
            act((me + d) % count)
            return carry

        lax.fori_loop(1, count, one, 0)

    each(lambda p: there(p).start())

    def step(i, state):
        p = count - 1 - i if backward else i

        @pl.when(p != me)
        def _():
            here(p).wait_recv()

        ready[p] = state.astype(bf16)

        @pl.when(p != me)
        def _():
            back(p).start()

        decay = jnp.exp(got[p, pl.ds(part, 1)].astype(f32) + got[p, pl.ds(part + 1, 1)].astype(f32))
        return decay * state + got[p, pl.ds(0, part)].astype(f32)

    lax.fori_loop(0, count, step, jnp.zeros((part, value.shape[1]), f32))
    out[pl.ds(pl.multiple_of(me * part, part), part)] = ready[me]
    each(lambda p: home(p).wait_recv())
    each(lambda p: there(p).wait_send())
    each(lambda p: back(p).wait_send())


def exchange(value, logs, backward, collective_id):
    heads = lax.axis_size("head")
    count = lax.axis_size("seq") * heads
    rows, width = value.shape
    part = rows // count
    tail = 16
    dma = pltpu.SemaphoreType.DMA
    return pl.pallas_call(
        partial(exchange_body, count, heads, rows // logs.shape[0], backward),
        out_shape=jax.ShapeDtypeStruct((rows, width), bf16),
        in_specs=[pl.BlockSpec(memory_space=pltpu.VMEM)] * 2,
        out_specs=pl.BlockSpec(memory_space=pltpu.VMEM),
        scratch_shapes=[
            pltpu.VMEM((count, part + tail, width), bf16),
            pltpu.VMEM((count, part + tail, width), bf16),
            pltpu.VMEM((count, part, width), bf16),
            dma((count,)), dma((count,)), dma((count,)), dma((count,)),
        ],
        compiler_params=pltpu.CompilerParams(collective_id=collective_id, has_side_effects=True),
        name="exchange_states",
    )(value, logs)


def aligned(x, size):
    return x if isinstance(x, int) else pl.multiple_of(x, size)


def finish_body(seq, plan, n_arrays, *refs):
    heads = 4
    head_masks = [1, 2]
    nz = len(head_masks)
    seq_masks = [1 << k for k in range(seq.bit_length() - 1)]
    split, joined = seq_masks[:3], seq_masks[3:]
    ns, nj = len(split), len(joined)
    lay_out, tok_grad = refs[:2]
    grads = refs[2 : 2 + n_arrays]
    lay_full, tok_full, halos = refs[2 + n_arrays : 5 + n_arrays]
    outs = refs[5 + n_arrays : 5 + 2 * n_arrays]
    scratch = refs[5 + 2 * n_arrays :]
    s, z = lax.axis_index("seq"), lax.axis_index("head")
    count = len(plan)
    per = ns + nj + nz
    owns = scratch[:count]
    recvs = [scratch[count + i * per : count + (i + 1) * per] for i in range(count)]
    (load_sem, send_sem, recv_sem, jsend, jrecv, zsend, zrecv, gsend, grecv, keep_sem, asend, arecv, stay, hsend,
     hrecv) = scratch[count * (1 + per) :]

    def peer(to_s, to_z):
        return {"seq": to_s, "head": to_z}

    def remote(src, dst, send, recv, to_s, to_z):
        return pltpu.make_async_remote_copy(src, dst, send, recv, device_id=peer(to_s, to_z), device_id_type=MESH)

    barrier = pltpu.get_barrier_semaphore()

    def greet(to_s, to_z):
        pl.semaphore_signal(barrier, 1, device_id=peer(to_s, to_z), device_id_type=MESH)

    for mask in seq_masks:
        greet(flipped(s, mask), z)
    for d in range(1, heads):
        greet(s, (z + d) % heads)

    @pl.when(s < seq - 1)
    def _():
        greet(s + 1, 0)

    greeted = len(seq_masks) + heads - 1

    @pl.when((z == 0) & (s > 0))
    def _():
        pl.semaphore_wait(barrier, greeted + heads)

    @pl.when((z != 0) | (s == 0))
    def _():
        pl.semaphore_wait(barrier, greeted)

    seqs, mine, _ = lay_out.shape
    width = lay_full.shape[2]

    def features(q):
        return pl.ds(aligned(q * width, width), width)

    def rows_to(q):
        return pl.ds(aligned(q * mine, mine), mine)

    def back_copies(q, source):
        return [
            (lay_out.at[:, :, features(q)], lay_full.at[:, rows_to(source)]),
            (tok_grad.at[:, pl.ds(HALO, mine), features(q)], tok_full.at[:, rows_to(source)]),
        ]

    def back_send(d):
        q = (z + d) % heads
        return [remote(a, b, asend.at[i, q], arecv.at[i, z], s, q) for i, (a, b) in enumerate(back_copies(q, z))]

    def back_wait(d):
        q = (z + d) % heads
        return [remote(a, b, asend.at[i, q], arecv.at[i, q], s, q) for i, (a, b) in enumerate(back_copies(z, q))]

    def stay_copies():
        return [pltpu.make_async_copy(a, b, stay.at[i]) for i, (a, b) in enumerate(back_copies(z, z))]

    def halo_send(d):
        q = (z + d) % heads
        return remote(tok_grad.at[:, pl.ds(0, HALO), features(q)], halos.at[z], hsend.at[q], hrecv.at[z], s, q)

    def halo_wait(d):
        q = (z + d) % heads
        return remote(tok_grad.at[:, pl.ds(0, HALO), features(z)], halos.at[q], hsend.at[q], hrecv.at[q], s, q)

    def halo_own():
        return pltpu.make_async_copy(tok_grad.at[:, pl.ds(0, HALO), features(z)], halos.at[z], stay.at[2])

    def halo_cross(q):
        return remote(tok_grad.at[:, pl.ds(0, HALO), features(q)], halos.at[0], hsend.at[q], hrecv.at[0], s - 1, q)

    def halo_from_next():
        return remote(tok_grad.at[:, pl.ds(0, HALO), features(z)], halos.at[0], hsend.at[0], hrecv.at[0], s + 1, 0)

    def to_features(first):
        for copy in stay_copies():
            copy.start() if first else copy.wait()
        for d in range(1, heads):
            for copy in back_send(d):
                copy.start() if first else copy.wait_send()
            if not first:
                for copy in back_wait(d):
                    copy.wait_recv()

        @pl.when(z != 0)
        def _():
            halo_own().start() if first else halo_own().wait()
            for d in range(1, heads):
                halo_send(d).start() if first else halo_send(d).wait_send()

        @pl.when((z == 0) & (s > 0))
        def _():
            for q in range(heads):
                halo_cross(q).start() if first else halo_cross(q).wait_send()

        if not first:
            for d in range(1, heads):

                @pl.when((z + d) % heads != 0)
                def _():
                    halo_wait(d).wait_recv()

            @pl.when(s < seq - 1)
            def _():
                halo_from_next().wait_recv()

    def masks(c):
        return split[:1] + (split[1:] if c % 2 == 0 else split[:0:-1])

    def bit(c, k):
        return s // masks(c)[k] % 2

    def extent(c):
        array, axis, first, size = plan[c]
        return size if axis == 0 else grads[array].shape[2]

    def kept(c, k):
        size = extent(c)
        return sum((bit(c, j) * (size >> (j + 1)) for j in range(1, k + 1)), 0)

    def cut(c, begin, size):
        _, axis, _, rows = plan[c]
        part = pl.ds(aligned(begin, size), size)
        return (part, slice(None)) if axis == 0 else (slice(None), part)

    def in_array(c, begin, size):
        _, axis, first, rows = plan[c]
        if axis == 0:
            return pl.ds(aligned(first + begin, size), size), slice(None)
        return pl.ds(first, rows), pl.ds(aligned(begin, size), size)

    def load(c):
        half = extent(c) // 2
        rows, columns = in_array(c, bit(c, 0) * half, half)
        return pltpu.make_async_copy(grads[plan[c][0]].at[:, rows, columns], owns[c], load_sem.at[c])

    def seq_copy(c, k):
        half = extent(c) >> (k + 1)
        other = (1 - bit(c, k)) * half
        if k == 0:
            rows, columns = in_array(c, other, half)
            source = grads[plan[c][0]].at[:, rows, columns]
        else:
            rows, columns = cut(c, kept(c, k - 1) + other, half)
            source = owns[c].at[:, rows, columns]
        return remote(source, recvs[c][k], send_sem.at[c, k], recv_sem.at[c, k], flipped(s, masks(c)[k]), z)

    def final(c):
        size = extent(c) >> ns
        return cut(c, kept(c, ns - 1), size)

    def joined_copy(c, k):
        rows, columns = final(c)
        return remote(
            owns[c].at[:, rows, columns], recvs[c][ns + k], jsend.at[c, k], jrecv.at[c, k], flipped(s, joined[k]), z)

    def head_copies(c, k):
        rows, columns = final(c)
        mask = head_masks[k]
        low, b = z % mask, z // mask % 2
        return [
            remote(
                owns[c].at[low + (1 - b) * mask + i * 2 * mask, rows, columns], recvs[c][ns + nj + k].at[i],
                zsend.at[c, k, i], zrecv.at[c, k, i], s, flipped(z, mask))
            for i in range(heads // (2 * mask))
        ]

    def add(c, k):
        _, axis, _, rows = plan[c]
        if k < ns:
            begin, size = kept(c, k), extent(c) >> (k + 1)
        else:
            begin, size = kept(c, ns - 1), extent(c) >> ns
        if k < ns + nj:
            many, place = heads, lambda i: i
        else:
            mask = head_masks[k - ns - nj]
            many = heads // (2 * mask)
            place = lambda i: z % mask + z // mask % 2 * mask + i * 2 * mask
        n_rows = size if axis == 0 else rows
        tile = min(16, n_rows)
        tiles = n_rows // tile
        received = recvs[c][k]

        def one(t, carry):
            i, r = t // tiles, t % tiles * tile
            there = pl.ds(pl.multiple_of(r, tile), tile)
            if axis == 0:
                here, columns = pl.ds(pl.multiple_of(begin + r, tile), tile), slice(None)
            else:
                here, columns = there, pl.ds(aligned(begin, size), size)
            q = place(i)
            total = owns[c][q, here, columns].astype(f32) + received[i, there].astype(f32)
            owns[c][q, here, columns] = total.astype(bf16)
            return carry

        lax.fori_loop(0, many * tiles, one, 0)

    def held(c, level):
        size = extent(c)
        return in_array(c, sum(bit(c, j) * (size >> (j + 1)) for j in range(level)), size >> level)

    def keep(c):
        rows, columns = final(c)
        to_rows, to_columns = held(c, ns)
        return pltpu.make_async_copy(
            owns[c].at[z, rows, columns], outs[plan[c][0]].at[to_rows, to_columns], keep_sem.at[c])

    def gather_copy(c, j):
        level = ns - j
        rows, columns = held(c, level)
        array = outs[plan[c][0]].at[rows, columns]
        return remote(array, array, gsend.at[c, j], grecv.at[c, j], flipped(s, masks(c)[level - 1]), z)

    for c in range(count):
        seq_copy(c, 0).start()
        load(c).start()
    to_features(True)
    last = per + 1 + ns

    def copies(c, k):
        if k < ns:
            return [seq_copy(c, k)]
        if k < ns + nj:
            return [joined_copy(c, k - ns)]
        if k < per:
            return head_copies(c, k - ns - nj)
        return [gather_copy(c, k - per - 1)]

    def advance(c, k):
        if k == 0:
            load(c).wait()
        if k == per:
            keep(c).wait()
        else:
            for copy in copies(c, k):
                copy.wait_recv()
        if k < per:
            if ns < k + 1 <= ns + nj:
                joined_copy_done(c, k)
            add(c, k)
        n = k + 1
        if n == per:
            keep(c).start()
        elif n < last:
            for copy in copies(c, n):
                copy.start()

    def joined_copy_done(c, k):
        joined_copy(c, k - ns).wait_send()

    pairs = count // 2
    for t in range(pairs + last - 1):
        for k in reversed(range(last)):
            p = t - k
            if 0 <= p < pairs:
                advance(2 * p, k)
                advance(2 * p + 1, k)
    to_features(False)
    for c in range(count):
        for k in range(last):
            if k != per and not ns <= k < ns + nj:
                for copy in copies(c, k):
                    copy.wait_send()


def finish_all(lay_out, tok_grad, arrays, plan, collective_id):
    seq, heads = lax.axis_size("seq"), lax.axis_size("head")
    nj = max(0, seq.bit_length() - 4)
    ns, nz = 3, 2
    seqs, mine, features = lay_out.shape
    width = features // heads
    owns, recvs = [], []
    for a, axis, first, rows in plan:
        columns = arrays[a].shape[2]
        cut = lambda k: (rows >> k, columns) if axis == 0 else (rows, columns >> k)
        owns.append(pltpu.VMEM((heads, *cut(1)), bf16))
        recvs += [pltpu.VMEM((heads, *cut(k + 1)), bf16) for k in range(ns)]
        recvs += [pltpu.VMEM((heads, *cut(ns)), bf16) for k in range(nj)]
        recvs += [pltpu.VMEM((heads >> (k + 1), *cut(ns)), bf16) for k in range(nz)]
    count = len(plan)
    dma = pltpu.SemaphoreType.DMA
    sems = [
        dma((count,)), dma((count, ns)), dma((count, ns)), dma((count, max(nj, 1))), dma((count, max(nj, 1))),
        dma((count, nz, heads // 2)), dma((count, nz, heads // 2)), dma((count, ns)), dma((count, ns)), dma((count,)),
        dma((2, heads)), dma((2, heads)), dma((3,)), dma((heads,)), dma((heads,)),
    ]
    anywhere = pl.BlockSpec(memory_space=pl.ANY)
    out_shape = [jax.ShapeDtypeStruct((seqs, heads * mine, width), bf16)] * 2
    out_shape += [jax.ShapeDtypeStruct((heads, seqs, HALO, width), bf16)]
    out_shape += [jax.ShapeDtypeStruct(a.shape[1:], bf16) for a in arrays]
    return pl.pallas_call(
        partial(finish_body, seq, plan, len(arrays)),
        out_shape=out_shape,
        in_specs=[anywhere] * (2 + len(arrays)),
        out_specs=[anywhere] * len(out_shape),
        scratch_shapes=owns + recvs + sems,
        compiler_params=pltpu.CompilerParams(
            collective_id=collective_id, has_side_effects=True, vmem_limit_bytes=60 * 2**20),
        name="finish_sums",
    )(lay_out, tok_grad, *arrays)


def row_scale(values):
    return lax.rsqrt(jnp.mean(values * values, axis=-1, keepdims=True) + epsilon)


def silu_slope(values):
    logistic = jax.nn.sigmoid(values)
    return logistic * (1.0 + values * (1.0 - logistic))


def norm_back(values, inverse, weights, upstream):
    weighted = weights * upstream
    return inverse * weighted - values * inverse**3 * jnp.mean(
        weighted * values, axis=-1, keepdims=True
    )


def rounded(values):
    return values.astype(bf16).astype(f32)


def dot(spec, left, right):
    return jnp.einsum(spec, left.astype(bf16), right.astype(bf16), preferred_element_type=f32)


def cumulated(spec, values, count):
    at = jnp.arange(count)
    lower = (at[:, None] >= at[None, :]).astype(f32)
    return jnp.einsum(spec, lower, values, precision=lax.Precision.HIGHEST, preferred_element_type=f32)


def whole(weights):
    seq = lax.axis_size("seq")
    parts = []
    for w in weights:
        part = w.shape[0] // seq
        parts.append(lax.dynamic_slice_in_dim(w, lax.axis_index("seq") * part, part, 0))
    mine = jnp.concatenate(parts, axis=0)
    every = lax.all_gather(mine, ("head", "seq"), axis=0, tiled=True)
    every = every.reshape(lax.axis_size("head"), seq, *mine.shape)
    out, at = [], 0
    for w, p in zip(weights, parts):
        out.append(every[:, :, at : at + p.shape[0]].reshape(-1, *w.shape))
        at += p.shape[0]
    return out


def chunks(array, rows, count):
    return [(array, 0, i * (rows // count), rows // count) for i in range(count)]


def local(
    tokens,
    decay_codes,
    cotangent,
    attn_gain,
    w_query,
    w_key,
    w_value,
    w_out_gate,
    conv_query,
    conv_key,
    conv_value,
    out_gain,
    w_out,
    mlp_gain,
    w_gate,
    w_up,
    w_down,
):
    seqs, rows, own_width = tokens.shape
    heads = lax.axis_size("head")
    place = lax.axis_index("seq") * heads + lax.axis_index("head")
    mine = rows // heads
    width = own_width * heads
    key_width = w_query.shape[1]
    value_width = w_value.shape[1]
    conv_width = 2 * key_width + value_width
    mixer_width = conv_width + value_width

    half = width // 2
    items = [
        (0, 0, 0, 0, width, 0),
        (1, 0, 0, 0, width, key_width),
        (2, 0, 0, 0, half, 2 * key_width),
        (2, 0, 0, half, half, 2 * key_width),
        (3, 0, 0, 0, half, conv_width),
        (3, 0, 0, half, half, conv_width),
        (4, 1, 0, 0, w_out.shape[0] // 2, 0),
        (4, 1, 0, w_out.shape[0] // 2, w_out.shape[0] // 2, 0),
    ]
    tokens_ext, codes, upstream, w_mixer, w_proj = start_all(
        tokens,
        decay_codes.astype(jnp.int16),
        cotangent,
        (w_query, w_key, w_value, w_out_gate, w_out),
        items,
        ((width, mixer_width), w_out.shape),
        1,
    )
    (w_gate_all,) = whole((w_gate,))
    (w_up_all,) = whole((w_up,))
    (w_low,) = whole((w_down,))
    taps = lax.all_gather(jnp.concatenate([conv_query, conv_key, conv_value], axis=1), "head")

    first_rows = (jnp.arange(mine + HALO) < HALO) & (place == 0)
    resid_ext = jnp.where(first_rows[None, :, None], 0, tokens_ext).astype(f32)
    first_scale = row_scale(resid_ext)
    normed = (resid_ext * first_scale * attn_gain).astype(bf16)
    projected = dot("std,hde->hste", normed, w_mixer).astype(bf16)
    gate_rows = projected[:, :, HALO:, conv_width:].astype(f32)
    extended = projected[..., :conv_width].astype(f32)
    tap_count = taps.shape[1]
    lead = HALO - tap_count + 1
    conv_sum = sum(
        taps[:, j, None, None, :] * extended[:, :, lead + j : lead + j + mine] for j in range(tap_count)
    )
    activated = jax.nn.silu(conv_sum)
    blocks = mine // SPAN

    def spanned(values):
        return values.reshape(heads, seqs, blocks, SPAN, values.shape[-1])

    query = spanned(activated[..., :key_width])
    keyed = spanned(activated[..., key_width : 2 * key_width])
    valued = spanned(activated[..., 2 * key_width :])
    log_decay = -codes.astype(f32) * decay_unit
    log_decay = jnp.moveaxis(log_decay.reshape(seqs, blocks, SPAN, heads, key_width), 3, 0)
    cumul = cumulated("tu,hanuk->hantk", log_decay, SPAN)
    span_log = cumul[:, :, :, -1]
    running = cumulated("mn,hank->hamk", span_log, blocks)
    carry_decay = jnp.exp(running - span_log)
    log_total = running[:, :, -1].reshape(-1, key_width)
    positions = jnp.arange(SPAN)
    causal = positions[:, None] >= positions[None, :]
    grow = jnp.exp(cumul)
    shrink = jnp.exp(-cumul)
    to_end = jnp.exp(span_log[:, :, :, None] - cumul)
    scale = key_width ** (-0.5)
    query_exp = query * scale * grow
    keyed_exp = keyed * shrink
    keyed_end = keyed * to_end
    update = dot("hantk,hantv->hanvk", keyed_end, valued)
    span_decay = jnp.exp(span_log)
    starts = [jnp.zeros_like(update[:, :, 0])]
    for n in range(blocks):
        starts.append(span_decay[:, :, n, None, :] * starts[n] + update[:, :, n])
    local_end = starts.pop()
    flat = (-1, key_width)
    incoming = exchange(local_end.astype(bf16).reshape(flat), log_total, False, 2)
    incoming = incoming.reshape(local_end.shape).astype(f32)
    scores = jnp.where(causal, dot("hantk,hanuk->hantu", query_exp, keyed_exp), 0.0)
    inner = dot("hantu,hanuv->hantv", scores, valued)
    states = jnp.stack(starts, 2) + carry_decay[:, :, :, None, :] * incoming[:, :, None]
    core_rows = (inner + dot("hantk,hanvk->hantv", query_exp, states)).reshape(heads, seqs, mine, value_width)
    out_scale = row_scale(core_rows)
    normed_out = core_rows * out_scale * out_gain
    gate_silu = jax.nn.silu(gate_rows)
    gated = (normed_out * gate_silu).astype(bf16)
    resid = resid_ext[:, HALO:]
    hidden_in = resid + jnp.sum(rounded(dot("hste,hed->hstd", gated, w_proj)), axis=0)
    second_scale = row_scale(hidden_in)
    normed_two = (hidden_in * second_scale * mlp_gain).astype(bf16)
    gate_val = dot("std,hdf->hstf", normed_two, w_gate_all)
    up_val = dot("std,hdf->hstf", normed_two, w_up_all)
    gate_act = jax.nn.silu(gate_val)
    hidden = (gate_act * up_val).astype(bf16)
    layer_out = hidden_in + jnp.sum(rounded(dot("hstf,hfd->hstd", hidden, w_low)), axis=0)

    d_hidden = rounded(dot("std,hfd->hstf", upstream, w_low))
    grad_down = dot("hstf,std->hfd", hidden, upstream)
    d_gate = (d_hidden * up_val * silu_slope(gate_val)).astype(bf16)
    d_up = (d_hidden * gate_act).astype(bf16)
    grad_gate = dot("std,hstf->hdf", normed_two, d_gate)
    grad_up = dot("std,hstf->hdf", normed_two, d_up)
    d_normed_two = dot("hstf,hdf->std", d_gate, w_gate_all) + dot("hstf,hdf->std", d_up, w_up_all)
    d_hidden_in = upstream.astype(f32) + norm_back(hidden_in, second_scale, mlp_gain, d_normed_two)
    grad_mlp_gain = jnp.sum(d_normed_two * hidden_in * second_scale, axis=(0, 1))
    d_mixer = d_hidden_in.astype(bf16)
    grad_out = dot("hste,std->hed", gated, d_mixer)
    d_gated = rounded(dot("std,hed->hste", d_mixer, w_proj))
    d_normed_out = d_gated * gate_silu
    d_gate_rows = d_gated * normed_out * silu_slope(gate_rows)
    grad_out_gain = jnp.sum(d_normed_out * core_rows * out_scale, axis=(0, 1, 2))
    d_core = spanned(norm_back(core_rows, out_scale, out_gain, d_normed_out))

    d_states = dot("hantk,hantv->hanvk", query_exp, d_core)
    own_grad = jnp.sum(carry_decay[:, :, :, None, :] * d_states, axis=2)
    leaving = exchange(own_grad.astype(bf16).reshape(flat), log_total, True, 3)
    d_ends = [leaving.reshape(own_grad.shape).astype(f32)]
    for n in range(blocks - 1, 0, -1):
        d_ends.append(span_decay[:, :, n, None, :] * d_ends[-1] + d_states[:, :, n])
    d_ends = jnp.stack(d_ends[::-1], 2)
    d_scores = jnp.where(causal, dot("hantv,hanuv->hantu", d_core, valued), 0.0)
    d_query = dot("hantu,hanuk->hantk", d_scores, keyed_exp) + dot("hantv,hanvk->hantk", d_core, states)
    d_query = d_query * scale * grow
    d_keyed = dot("hantu,hantk->hanuk", d_scores, query_exp) * shrink
    d_keyed = d_keyed + dot("hanuv,hanvk->hanuk", valued, d_ends) * to_end
    d_valued = dot("hantu,hantv->hanuv", scores, d_core) + dot("hanuk,hanvk->hanuv", keyed_end, d_ends)
    d_activated = jnp.concatenate(
        [a.reshape(heads, seqs, mine, -1) for a in (d_query, d_keyed, d_valued)], axis=-1
    )
    d_conv = d_activated * silu_slope(conv_sum)
    tap_grads = []
    d_extended = jnp.zeros(extended.shape, f32)
    for j in range(tap_count):
        tap_grads.append(jnp.sum(d_conv * extended[:, :, lead + j : lead + j + mine], axis=(1, 2)))
        d_extended = d_extended + jnp.pad(
            taps[:, j, None, None, :] * d_conv, ((0, 0), (0, 0), (lead + j, tap_count - 1 - j), (0, 0))
        )
    grad_taps = jnp.stack(tap_grads, 1)
    d_gate_ext = jnp.pad(d_gate_rows, ((0, 0), (0, 0), (HALO, 0), (0, 0)))
    d_projected = jnp.concatenate([d_extended, d_gate_ext], axis=-1).astype(bf16)
    grad_mixer = dot("std,hste->hde", normed, d_projected)
    d_normed = dot("hste,hde->std", d_projected, w_mixer)
    grad_attn_gain = jnp.sum(d_normed * resid_ext * first_scale, axis=(0, 1))
    tokens_grad = norm_back(resid_ext, first_scale, attn_gain, d_normed)
    tokens_grad = tokens_grad + jnp.pad(d_hidden_in, ((0, 0), (HALO, 0), (0, 0)))

    small = jnp.concatenate(
        [
            grad_attn_gain.reshape(heads, -1),
            grad_mlp_gain.reshape(heads, -1),
            jnp.broadcast_to(grad_out_gain, (heads, value_width)),
            grad_taps.reshape(heads, -1),
        ],
        axis=1,
    )
    small_rows = 256
    lanes = -(-small.shape[1] // (small_rows * 128)) * 128
    small = jnp.pad(small, ((0, 0), (0, small_rows * lanes - small.shape[1]))).reshape(heads, small_rows, lanes)
    arrays = [a.astype(bf16) for a in (grad_gate, grad_up, grad_down, grad_out, grad_mixer, small)]
    ff = w_gate.shape[1]
    plan = (
        chunks(0, width, 4)
        + chunks(1, width, 4)
        + [(2, 1, 0, ff // 2), (2, 1, ff // 2, ff // 2)]
        + chunks(3, w_out.shape[0], 2)
        + chunks(4, width, 4)
        + chunks(5, small_rows, 2)
    )
    layer_out, tokens_grad, halos, *sums = finish_all(
        layer_out.astype(bf16), tokens_grad.astype(bf16), arrays, plan, 4
    )
    grad_gate, grad_up, grad_down, grad_out, grad_mixer, small = (a.astype(f32) for a in sums)
    layer_out = layer_out.astype(f32)
    last = lax.axis_index("seq") == lax.axis_size("seq") - 1
    halos = jnp.where(last & (jnp.arange(heads) == 0)[:, None, None, None], 0, halos).astype(f32)
    halos = jnp.moveaxis(jnp.roll(halos, -1, axis=0), 0, 1)
    halos = jnp.pad(halos, ((0, 0), (0, 0), (mine - HALO, 0), (0, 0))).reshape(tokens_grad.shape)
    tokens_grad = tokens_grad.astype(f32) + halos
    small = small.reshape(-1)
    at = 2 * own_width + value_width
    grad_taps = small[at : at + tap_count * conv_width].reshape(tap_count, conv_width)
    return (
        layer_out,
        tokens_grad,
        small[:own_width],
        grad_mixer[:, :key_width],
        grad_mixer[:, key_width : 2 * key_width],
        grad_mixer[:, 2 * key_width : conv_width],
        grad_mixer[:, conv_width:],
        grad_taps[:, :key_width],
        grad_taps[:, key_width : 2 * key_width],
        grad_taps[:, 2 * key_width :],
        small[2 * own_width : at],
        grad_out,
        small[own_width : 2 * own_width],
        grad_gate,
        grad_up,
        grad_down,
    )


def solution(mesh):
    in_specs = (
        P(None, "seq", "head"),
        P(None, "seq", "head"),
        P(None, "seq", "head"),
        P(),
        P(None, "head"),
        P(None, "head"),
        P(None, "head"),
        P(None, "head"),
        P(None, "head"),
        P(None, "head"),
        P(None, "head"),
        P(),
        P("head", None),
        P(),
        P(None, "head"),
        P(None, "head"),
        P("head", None),
    )
    out_specs = (
        P(None, "seq", "head"),
        P(None, "seq", "head"),
        P("head"),
        P(None, "head"),
        P(None, "head"),
        P(None, "head"),
        P(None, "head"),
        P(None, "head"),
        P(None, "head"),
        P(None, "head"),
        P(),
        P("head", None),
        P("head"),
        P(None, "head"),
        P(None, "head"),
        P("head", None),
    )
    return jax.shard_map(local, mesh=mesh, in_specs=in_specs, out_specs=out_specs, check_vma=False)
```

time: 1120 us -> 669 us (0.60)
  waiting for transfers between devices: 669 us -> 21.4 us
  Pallas kernels: 0 us -> 381 us
  blocking collectives: 106 us -> 17.5 us
  starting transfers between devices: 50.4 us -> 0.12 us
  other arithmetic: 72.1 us -> 51.6 us
  local copies, waits for them, and re-layouts: 82.8 us -> 69.3 us
  matrix products: 121 us -> 108 us
    pallas_call x0 -> x4, Pallas kernels: none -> 381 us  [the longest x1 173 us: finish_all(): pl.pallas_call(partial(finish_body, seq, plan, len(arrays)), out_shape=ou...]
    reduce_scatter x3 -> x0, waiting for transfers between devices: 253 us -> none  [reduced(): lax.psum_scatter(flat, ('head', 'seq'), scatter_dimension=0, tiled=True)]
    unnamed x12 -> x3, waiting for transfers between devices: 144 us -> 0.05 us
    all_to_all x10 -> x0, waiting for transfers between devices: 121 us -> none  [the longest x3 44.7 us: to_tokens(): return lax.all_to_all(array, 'head', 1, 2, tiled=True)]
    all_gather x3 -> x0, waiting for transfers between devices: 67.7 us -> none  [reduced(): return lax.all_gather(mine, 'seq', axis=0, tiled=True).astype(f32)]
    all_gather x4 -> x3, waiting for transfers between devices: 83.4 us -> 21.4 us  [whole(): every = lax.all_gather(mine, ('head', 'seq'), axis=0, tiled=True)]
    psum x1 -> x0, blocking collectives: 53.7 us -> none  [local(): small = lax.psum(small.astype(bf16), BOTH).astype(f32)]
    all_to_all x10 -> x0, starting transfers between devices: 42.7 us -> none  [the longest x3 13.2 us: to_tokens(): return lax.all_to_all(array, 'head', 1, 2, tiled=True)]
  transfers between devices with their start and end apart: 23 -> 3, of which waited for: 17 -> 1; matrix products, arithmetic and copies ran while one was open for 15% -> 12% of each run, Pallas kernels for 0% -> 26%
where the time goes in v3:
time: 669 us; the launch traced here: 664 us
  Pallas kernels  381 us (57%)
  matrix products  108 us (16%)
  local copies, waits for them, and re-layouts  69.3 us (10%)
  other arithmetic  51.6 us (8%)
  waiting for transfers between devices  21.4 us (3%)
  blocking collectives  17.5 us (3%)
  between operations  15.2 us (2%)
    pallas_call x1, Pallas kernels, finish_all(): pl.pallas_call(partial(finish_body, seq, plan, len(arrays)), out_shape=ou...  173 us
    pallas_call x1, Pallas kernels, start_all(): pl.pallas_call(partial(start_body, seq, len(weights), items), out_shape=o...  118 us
    dot_general x27, matrix products, dot(): jnp.einsum(spec, left.astype(bf16), right.astype(bf16), preferred_element...  106 us
    pallas_call x2, Pallas kernels, exchange(): pl.pallas_call(partial(exchange_body, count, heads, rows // logs.shape[0]...  89.3 us
    another operation x2, local copies, waits for them, and re-layouts, whole(): out.append(every[:, :, at:at + p.shape[0]].reshape(-1, *w.shape))  21.5 us
    all_gather x3, waiting for transfers between devices, whole(): every = lax.all_gather(mine, ('head', 'seq'), axis=0, tiled=True)  21.4 us
    unnamed x141, local copies, waits for them, and re-layouts  18.1 us
    all_gather x1, blocking collectives, local(): lax.all_gather(jnp.concatenate([conv_query, conv_key, conv_value], axis=1...  17.5 us
  transfers between devices with their start and end apart: 3, of which 1 were waited for; matrix products, arithmetic and copies ran while one was open for 12% of the time, Pallas kernels for 26%

profile of v3, /device:TPU:1, one launch (start us, length us, event | category | flops | bytes accessed | tf_op | source)
XLA Modules:
  0.0 663.5 jit_solution(9484349001168977598)
XLA Ops:
  13.6 118.4 %start_exchange.1 = (bf16[2,272,1024]{2,1,0:T(8,128)(2,1)}, s16[2,256,512]{2,1,0:T(8,128)(2,1)}, bf16[2,256,1024]{2,1,0:T(8,128)(2,1)}, bf16[4,1024,768]{2,1,0:T(8,128)(2,1)}, bf16[4,256,1024]{2,1,0:T(8,128)(2,1)}) custom-call(bf16[2,1024,256]{2,1,0:T(8,128)(2,1)} %refs_0_.1, s16[2,1024,128]{2,1,0:T(8,128)(2,1)} %convert_element_type.241.refs_1_, ...), custom_call_target="tpu_custom_call" | custom-call | tf_op jit(solution)/shard_map/start_exchange/pallas_call | solution.py:261
  137.0 17.5 %all-gather.1 = f32[4,4,512]{2,1,0:T(4,128)S(1)} all-gather(f32[1,4,512]{2,1,0:T(4,128)S(1)} %maximum_bitcast_fusion.1), channel_id=2, replica_groups=mesh['seq'=8,'head'=4] {'head'}, dimensions={0}, use_global_device_ids=true | all-gather | bytes 40960 | tf_op jit(solution)/shard_map/all_gather | solution.py:808
  155.2 6.8 %convert_bitcast_fusion = bf16[4,2,272,768]{3,2,1,0:T(8,128)(2,1)S(1)} fusion(bf16[4,1024,768]{2,1,0:T(8,128)(2,1)} %get-tuple-element.31, f32[1024]{0:T(1024)S(1)} %copy-done.49, f32[2,272]{1,0:T(2,128)S(1)} %get-tuple-element.169, bf16[2,272,1024]{2,1,0:T(8,128)(2,1)S(1)} %copy-done.18, pred[272]{0:T(512)(128)(4,1)S(1)} %fusion.87), kind=kOutput, calls=%fused_computation.50 | convolution fusion | flops 3427008512 | bytes 10754448 | tf_op jit(solution)/shard_map/std,hde->hste/dot_general | solution.py:727
  163.9 3.9 fusion.24
  173.5 53.9 %exchange_states.2 = bf16[2048,128]{1,0:T(8,128)(2,1)} custom-call(bf16[2048,128]{1,0:T(8,128)(2,1)} %fusion.74.value, f32[8,128]{1,0:T(8,128)} %bitcast.345), custom_call_target="tpu_custom_call" | custom-call | tf_op jit(solution)/shard_map/exchange_states/pallas_call | solution.py:364
  242.1 10.9 %reshape_reshape.9 = bf16[4,1024,704]{1,0,2:T(4,128)(2,1)} reshape(bf16[4096,704]{0,1:T(8,128)(2,1)} %all-gather.6.cloned.1.call-done) | data formatting | bytes 11534336 | tf_op jit(solution)/shard_map/reshape;reshape | solution.py:747
  253.1 10.5 %reshape_reshape.10 = bf16[4,1024,704]{1,0,2:T(4,128)(2,1)} reshape(bf16[4096,704]{0,1:T(8,128)(2,1)} %all-gather.8.cloned.1.call-done) | data formatting | bytes 11534336 | tf_op jit(solution)/shard_map/reshape;reshape | solution.py:747
  263.6 11.9 %fusion.21 = f32[4,704,2,256]{3,1,2,0:T(8,128)} fusion(bf16[2,256,1024,1]{2,1,0,3:T(8,128)(2,1)S(1)} %fusion.68, bf16[4,1024,704,1]{1,0,2,3:T(4,128)(2,1)} %bitcast.321), kind=kOutput, calls=%fused_computation.34 | convolution fusion | flops 2952790016 | bytes 12582912 | tf_op jit(solution)/shard_map/std,hdf->hstf/dot_general | solution.py:727
  275.5 7.5 %fusion.17 = f32[4,704,2,256]{3,1,2,0:T(8,128)} fusion(bf16[2,256,1024,1]{2,1,0,3:T(8,128)(2,1)} %copy-done.42, bf16[4,1024,704,1]{1,0,2,3:T(4,128)(2,1)S(1)} %bitcast.324), kind=kOutput, calls=%fused_computation.30 | convolution fusion | flops 2952790016 | bytes 12582912 | tf_op jit(solution)/shard_map/std,hdf->hstf/dot_general | solution.py:727
  282.9 21.4 %all-gather.10.cloned.1.call-done = bf16[2816,1024]{1,0:T(8,128)(2,1)} async-done(((bf16[88,1024]{1,0:T(8,128)(2,1)}), bf16[2816,1024]{1,0:T(8,128)(2,1)}) %all-gather.10.cloned.1.call-update) | async-done | bytes 5767184 | tf_op jit(solution)/shard_map/all_gather | solution.py:743
  304.3 9.7 %fusion.7 = (bf16[4,2,256,704]{2,3,1,0:T(8,128)(2,1)S(1)}, bf16[4,2,256,704]{2,3,1,0:T(8,128)(2,1)S(1)}, bf16[4,2,256,704]{2,3,1,0:T(8,128)(2,1)S(1)}) fusion(f32[4,704,2,256]{3,1,2,0:T(8,128)} %fusion.17, f32[4,704,2,256]{3,1,2,0:T(8,128)} %fusion.21, bf16[4,704,1024,1]{2,1,3,0:T(8,128)(2,1)} %bitcast.356, bf16[2,256,1024]{2,1,0:T(8,128)(2,1)S(1)} %copy-done.35), kind=kOutput, calls=%fused_computation.16 | convolution fusion | flops 2977300480 | bytes 27000832 | tf_op jit(solution)/shard_map/std,hfd->hstf/dot_general | solution.py:727
  314.1 9.0 %fusion.15 = f32[2,256,1024,1]{2,1,0,3:T(8,128)S(1)} fusion(bf16[4,2,256,704]{2,3,1,0:T(8,128)(2,1)S(1)} %get-tuple-element.128, bf16[4,1024,704,1]{1,0,2,3:T(4,128)(2,1)} %bitcast.323), kind=kOutput, calls=%fused_computation.28 | convolution fusion | flops 2952790016 | bytes 10747904 | tf_op jit(solution)/shard_map/hstf,hdf->std/dot_general | solution.py:727
  323.1 7.3 %multiply_reduce_fusion.5 = (bf16[1024]{0:T(1024)(128)(2,1)S(1)}, f32[2,256]{1,0:T(2,128)S(1)}, f32[2,256,1024]{2,1,0:T(8,128)S(1)}) fusion(f32[2,256,1024]{2,1,0:T(8,128)S(1)} %copy-done.6, f32[2,256]{1,0:T(2,128)S(1)} %get-tuple-element.171, f32[1024]{0:T(1024)S(1)} %copy-done.47, f32[2,256,1024,1]{2,1,0,3:T(8,128)S(1)} %fusion.15, ...), kind=kOutput, calls=%fused_computation.100 | convolution fusion | flops 2956458496 | bytes 14952448 | tf_op jit(solution)/shard_map/hstf,hdf->std/dot_general | solution.py:727
  330.5 3.9 convert_reduce_fusion
  345.2 3.8 multiply_reduce_fusion.4
  349.0 35.4 %exchange_states.3 = bf16[2048,128]{1,0:T(8,128)(2,1)} custom-call(bf16[2048,128]{1,0:T(8,128)(2,1)} %bitcast.331, f32[8,128]{1,0:T(8,128)} %bitcast.346), custom_call_target="tpu_custom_call" | custom-call | tf_op jit(solution)/shard_map/exchange_states/pallas_call | solution.py:364
  394.3 3.5 multiply_reduce_fusion.3
  397.9 5.6 broadcast_multiply_fusion.3
  403.4 4.7 add_convert_fusion
  408.2 8.0 %fusion.37 = (bf16[1024]{0:T(1024)(128)(2,1)S(1)}, f32[2,272]{1,0:T(2,128)S(1)}, f32[2,272,1024,1]{2,1,0,3:T(8,128)}) fusion(f32[2,272]{1,0:T(2,128)S(1)} %get-tuple-element.169, bf16[2,272,1024]{2,1,0:T(8,128)(2,1)S(1)} %copy-done.19, pred[272]{0:T(512)(128)(4,1)S(1)} %fusion.87, f32[1024]{0:T(1024)S(1)} %copy-done.49, ...), kind=kOutput, calls=%fused_computation.68 | convolution fusion | flops 3437033984 | bytes 12921360 | tf_op jit(solution)/shard_map/hste,hde->std/dot_general | solution.py:727
  416.2 7.7 %fusion.1.refs_6_ = bf16[4,1024,768]{2,1,0:T(8,128)(2,1)} fusion(bf16[4,2,256,256]{3,2,1,0:T(8,128)(2,1)S(1)} %copy-done.44, bf16[4,2,272,512]{3,2,1,0:T(8,128)(2,1)S(1)} %add_convert_fusion, f32[1024]{0:T(1024)S(1)} %copy-done.49, f32[2,272]{1,0:T(2,128)S(1)} %get-tuple-element.169, bf16[2,272,1024]{2,1,0:T(8,128)(2,1)S(1)} %copy-done.19, ...), kind=kOutput, calls=%fused_computation.8 | convolution fusion | flops 3438510080 | bytes 10688912 | tf_op jit(solution)/shard_map/std,hste->hde/dot_general | solution.py:727
  423.9 4.9 bitcast_convert_fusion.2
  428.8 2.6 bitcast_convert_fusion.4.refs_5_
  431.5 5.2 bitcast_convert_fusion.3
  436.7 5.0 bitcast_convert_fusion.1.refs_4_
  442.6 8.5 %copy.92 = bf16[4,704,1024]{1,2,0:T(8,128)(2,1)} copy(bf16[4,704,1024]{2,1,0:T(8,128)(2,1)} %bitcast_convert_fusion.2) | data formatting | bytes 11534336 | tf_op jit(solution)/shard_map/convert_element_type | solution.py:936
  451.1 8.4 %copy.91 = bf16[4,704,1024]{1,2,0:T(8,128)(2,1)} copy(bf16[4,704,1024]{2,1,0:T(8,128)(2,1)} %bitcast_convert_fusion.3) | data formatting | bytes 11534336 | tf_op jit(solution)/shard_map/convert_element_type | solution.py:936
  459.5 3.3 fusion.34.refs_1_
  462.8 173.1 %finish_sums.1 = (bf16[2,1024,256]{2,1,0:T(8,128)(2,1)}, bf16[2,1024,256]{2,1,0:T(8,128)(2,1)}, bf16[4,2,16,256]{3,2,1,0:T(8,128)(2,1)}, bf16[1024,704]{1,0:T(8,...) custom-call(bf16[2,256,1024]{2,1,0:T(8,128)(2,1)} %get-tuple-element, ...), custom_call_target="tpu_custom_call" | custom-call | tf_op jit(solution)/shard_map/finish_sums/pallas_call | solution.py:694
  636.9 2.8 fusion.101
  644.7 3.0 copy.96
  647.7 3.1 copy.97
  (224 shorter events, 67.2 us)
Async XLA Ops:
  7.2 5.5 copy-start.41
  7.2 234.9 %all-gather.6.cloned.1.call-start = ((), (), s32[]{:S(2)}) async-start(), calls=%async_computation | async-start | bytes 5947392 | tf_op jit(solution)/shard_map/all_gather | solution.py:743
  9.3 243.8 %all-gather.8.cloned.1.call-start = ((), (), s32[]{:S(2)}) async-start(), calls=%async_computation.1 | async-start | bytes 5947392 | tf_op jit(solution)/shard_map/all_gather | solution.py:743
  11.0 293.3 %all-gather.10.cloned.1.call-start = ((), (), s32[]{:S(2)}) async-start(), calls=%async_computation.2 | async-start | bytes 5947392 | tf_op jit(solution)/shard_map/all_gather | solution.py:743
  134.5 20.6 %copy-start.49 = (f32[1024]{0:T(1024)S(1)}, f32[1024]{0:T(1024)}, u32[]{:S(2)}) copy-start(f32[1024]{0:T(1024)} %param.20) | copy-start | bytes 12292
  136.5 32.6 %copy-start.3 = (f32[4,2,4,64,128]{4,3,2,1,0:T(8,128)}, f32[4,2,4,64,128]{4,3,2,1,0:T(8,128)S(1)}, u32[]{:S(2)}) copy-start(f32[4,2,4,64,128]{4,3,2,1,0:T(8,128)S(1)} %convolution_bitcast_fusion) | copy-start | bytes 3145732
  163.9 3.9 copy-start.2
  169.6 58.9 %copy-start.14 = (bf16[4,2,4,64,128]{4,3,2,1,0:T(8,128)(2,1)}, bf16[4,2,4,64,128]{4,3,2,1,0:T(8,128)(2,1)S(1)}, u32[]{:S(2)}) copy-start(bf16[4,2,4,64,128]{4,3,2,1,0:T(8,128)(2,1)S(1)} %get-tuple-element.152) | copy-start | bytes 1572868
  169.6 58.9 %copy-start.26 = (bf16[4,2,4,64,128]{4,3,2,1,0:T(8,128)(2,1)}, bf16[4,2,4,64,128]{4,3,2,1,0:T(8,128)(2,1)S(1)}, u32[]{:S(2)}) copy-start(bf16[4,2,4,64,128]{4,3,2,1,0:T(8,128)(2,1)S(1)} %get-tuple-element.146) | copy-start | bytes 1572868
  242.1 21.5 %copy-start.42 = (bf16[2,256,1024,1]{2,1,0,3:T(8,128)(2,1)}, bf16[2,256,1024,1]{2,1,0,3:T(8,128)(2,1)S(1)}, u32[]{:S(2)}) copy-start(bf16[2,256,1024,1]{2,1,0,3:T(8,128)(2,1)S(1)} %fusion.68) | copy-start | bytes 3145732
  263.6 11.9 %copy-start.23 = (bf16[4,1024,704]{1,0,2:T(4,128)(2,1)S(1)}, bf16[4,1024,704]{1,0,2:T(4,128)(2,1)}, u32[]{:S(2)}) copy-start(bf16[4,1024,704]{1,0,2:T(4,128)(2,1)} %reshape_reshape.10) | copy-start | bytes 17301508
  275.5 28.8 %copy-start.35 = (bf16[2,256,1024]{2,1,0:T(8,128)(2,1)S(1)}, bf16[2,256,1024]{2,1,0:T(8,128)(2,1)}, u32[]{:S(2)}) copy-start(bf16[2,256,1024]{2,1,0:T(8,128)(2,1)} %get-tuple-element.34) | copy-start | bytes 3145732
  314.0 9.1 %copy-start.59 = (bf16[4,2,256,704]{2,3,1,0:T(8,128)(2,1)}, bf16[4,2,256,704]{2,3,1,0:T(8,128)(2,1)S(1)}, u32[]{:S(2)}) copy-start(bf16[4,2,256,704]{2,3,1,0:T(8,128)(2,1)S(1)} %get-tuple-element.128) | copy-start | bytes 8650756
  314.0 9.0 %copy-start.57 = (bf16[4,2,256,704]{2,3,1,0:T(8,128)(2,1)}, bf16[4,2,256,704]{2,3,1,0:T(8,128)(2,1)S(1)}, u32[]{:S(2)}) copy-start(bf16[4,2,256,704]{2,3,1,0:T(8,128)(2,1)S(1)} %get-tuple-element.126) | copy-start | bytes 8650756
  314.1 16.4 %copy-start.61 = (bf16[4,2,256,704]{2,3,1,0:T(8,128)(2,1)}, bf16[4,2,256,704]{2,3,1,0:T(8,128)(2,1)S(1)}, u32[]{:S(2)}) copy-start(bf16[4,2,256,704]{2,3,1,0:T(8,128)(2,1)S(1)} %get-tuple-element.127) | copy-start | bytes 8650756
  314.1 9.0 %copy-start.6 = (f32[2,256,1024]{2,1,0:T(8,128)S(1)}, f32[2,256,1024]{2,1,0:T(8,128)}, u32[]{:S(2)}) copy-start(f32[2,256,1024]{2,1,0:T(8,128)} %copy-done.5) | copy-start | bytes 6291460
  314.1 16.4 %slice-start.2 = ((s8[5767168]{0:T(1024)(128)(4,1)}), s8[4194304]{0:T(1024)(128)(4,1)S(1)}, s32[]{:S(2)}) async-start(s8[5767168]{0:T(1024)(128)(4,1)} %bitcast.357), calls=%async_computation.5 | async-start | bytes 8388608
  323.1 7.4 %slice-start.3 = ((s8[5767168]{0:T(1024)(128)(4,1)}), s8[1572864]{0:T(1024)(128)(4,1)S(1)}, s32[]{:S(2)}) async-start(s8[5767168]{0:T(1024)(128)(4,1)} %bitcast.357), calls=%async_computation.6 | async-start | bytes 3145728
  334.4 4.3 copy-start.56
  336.0 5.3 copy-start.20
  403.4 4.7 copy-start.19
  403.4 4.7 copy-start.44
  416.2 7.7 %copy-start.43 = (bf16[2,256,1024,1]{2,1,0,3:T(8,128)(2,1)S(1)}, bf16[2,256,1024,1]{2,1,0,3:T(8,128)(2,1)}, u32[]{:S(2)}) copy-start(bf16[2,256,1024,1]{2,1,0,3:T(8,128)(2,1)} %copy-done.42) | copy-start | bytes 3145732
  416.2 7.7 %copy-start.60 = (bf16[4,2,256,704]{2,3,1,0:T(8,128)(2,1)S(1)}, bf16[4,2,256,704]{2,3,1,0:T(8,128)(2,1)}, u32[]{:S(2)}) copy-start(bf16[4,2,256,704]{2,3,1,0:T(8,128)(2,1)} %copy-done.59) | copy-start | bytes 8650756
  423.9 4.9 copy-start.21
  423.9 4.9 copy-start.38
  431.5 5.2 copy-start.36
  431.5 5.2 copy-start.62
  451.1 8.4 %copy-start.48 = (f32[2,272]{1,0:T(2,128)S(1)}, f32[2,272]{1,0:T(2,128)}, u32[]{:S(2)}) copy-start(f32[2,272]{1,0:T(2,128)} %get-tuple-element.168) | copy-start | bytes 6532
  462.8 173.1 %copy-start.54 = (pred[4]{0:T(512)(128)(4,1)S(1)}, pred[4]{0:T(512)(128)(4,1)}, u32[]{:S(2)}) copy-start(pred[4]{0:T(512)(128)(4,1)} %compare_and_fusion) | copy-start | bytes 16
  636.9 3.9 copy-start.46
  650.8 4.0 copy-start.39
  (38 other events, 83.2 us)
Sparse Core Ops, SparseCore 0:
  11.5 127.4 all-gather.5
  142.4 92.2 all-gather.7
  238.1 66.1 all-gather.9

commit v4 on v3

--- a/solution.py
+++ b/solution.py
@@ -21,13 +21,48 @@
     return place + mask - 2 * mask * (place // mask % 2)
 
 
-def start_body(seq, n_weights, items, *refs):
-    tokens, codes, cotangent = refs[:3]
+def over_seq(items, gathered, gsend, grecv, s, z):
+    heads = 4
+
+    def order(i):
+        return [4, 2, 1] if items[i][0] % 2 == 0 else [2, 4, 1]
+
+    def span(i, j):
+        _, _, to, axis, first, count, _, _ = items[i]
+        size = count if axis == 0 else gathered[to].shape[2]
+        begin = first if axis == 0 else 0
+        for mask in order(i)[: j - 4 : -1] if j < 3 else []:
+            size = size // 2
+            begin = begin + (s // mask % 2) * size
+        return pl.multiple_of(begin, size), size
+
+    def seq_copies(i, j):
+        _, _, to, axis, first, count, column, _ = items[i]
+        begin, size = span(i, j)
+        copies = []
+        for d in range(1, heads):
+            q = (z + d) % heads
+            if axis == 0:
+                place = gathered[to].at[q, pl.ds(begin, size), pl.ds(column, items[i][7])]
+            else:
+                place = gathered[to].at[q, pl.ds(first, count), pl.ds(begin, size)]
+            copies.append(pltpu.make_async_remote_copy(
+                place, place, gsend.at[i, j, d - 1], grecv.at[i, j, d - 1],
+                device_id={"seq": flipped(s, order(i)[j]), "head": z}, device_id_type=MESH))
+        return copies
+
+    return span, seq_copies
+
+
+def start_body(seq, n_weights, items, steps, *refs):
+    tokens, codes, taps = refs[:3]
     weights = refs[3 : 3 + n_weights]
-    out_tokens, out_codes, out_cotangent = refs[3 + n_weights : 6 + n_weights]
-    n_sem = 13
-    gathered = refs[6 + n_weights : -n_sem]
-    (tsend, trecv, csend, crecv, hsend, hrecv, stay, zsend, zrecv, ysend, yrecv, gsend, grecv) = refs[-n_sem:]
+    out_tokens, out_codes, out_taps = refs[3 + n_weights : 6 + n_weights]
+    n_sem = 11
+    n_items = len(items)
+    gathered = refs[6 + n_weights : -n_sem - n_items]
+    held = refs[-n_sem - n_items : -n_sem]
+    (tsend, trecv, hsend, hrecv, stay, zsend, zrecv, ysend, yrecv, gsend, grecv) = refs[-n_sem:]
     s, z = lax.axis_index("seq"), lax.axis_index("head")
     heads = 4
     masks = [1, 2, 4]
@@ -80,7 +115,7 @@
         triples = [
             (src, dst),
             (codes.at[:, here], out_codes.at[:, :, columns(out_codes, z)]),
-            (cotangent.at[:, here], out_cotangent.at[:, :, columns(out_cotangent, z)]),
+            (taps, out_taps.at[z]),
         ]
 
         @pl.when(z == target)
@@ -118,11 +153,10 @@
                     tokens.at[:, pl.ds(0, mine + HALO)], dst, tsend.at[0, source], trecv.at[0, source], s, source
                 ).wait_recv()
 
-            for i, (a, b) in enumerate(((codes, out_codes), (cotangent, out_cotangent))):
-                remote(
-                    a.at[:, here], b.at[:, :, columns(b, source)], tsend.at[i + 1, source], trecv.at[i + 1, source],
-                    s, source,
-                ).wait_recv()
+            for i, (a, b) in enumerate(
+                ((codes.at[:, here], out_codes.at[:, :, columns(out_codes, source)]), (taps, out_taps.at[source]))
+            ):
+                remote(a, b, tsend.at[i + 1, source], trecv.at[i + 1, source], s, source).wait_recv()
 
     def halo_copy(source, to_s):
         return remote(
@@ -134,21 +168,10 @@
     def _():
         halo_copy(z, s + 1).start()
 
-    def order(i):
-        return [4, 2, 1] if i % 2 == 0 else [2, 4, 1]
-
-    def span(i, j):
-        weight, _, axis, first, count, _ = items[i]
-        size = count if axis == 0 else weights[weight].shape[1]
-        begin = first if axis == 0 else 0
-        for k, mask in enumerate(reversed(order(i))):
-            if k < len(masks) - j:
-                size = size // 2
-                begin = begin + (s // mask % 2) * size
-        return pl.multiple_of(begin, size), size
+    span, seq_copies = over_seq(items, gathered, gsend, grecv, s, z)
 
     def piece(i, j):
-        weight, _, axis, first, count, column = items[i]
+        _, weight, _, axis, first, count, column, _ = items[i]
         begin, size = span(i, j)
         wide = weights[weight].shape[1]
         if axis == 0:
@@ -159,20 +182,23 @@
             place = lambda ref, q: ref.at[q, pl.ds(first, count), pl.ds(begin, size)]
         return own, place
 
-    def own_copy(i):
-        weight, to, axis, first, count, column = items[i]
+    def own_load(i):
+        _, weight, _, _, first, count, _, _ = items[i]
+        return pltpu.make_async_copy(weights[weight].at[pl.ds(first, count)], held[i], stay.at[3 + i])
+
+    def own_store(i):
+        _, weight, to, _, first, count, column, _ = items[i]
         wide = weights[weight].shape[1]
         return pltpu.make_async_copy(
-            weights[weight].at[pl.ds(first, count)],
-            gathered[to].at[z, pl.ds(first, count), pl.ds(column, wide)], stay.at[3 + i])
+            held[i], gathered[to].at[z, pl.ds(first, count), pl.ds(column, wide)], stay.at[3 + i])
 
     def far_copy(i):
         own, place = piece(i, 0)
-        return remote(own, place(gathered[items[i][1]], z), zsend.at[i], zrecv.at[i], s, flipped(z, 2))
+        return remote(own, place(gathered[items[i][2]], z), zsend.at[i], zrecv.at[i], s, flipped(z, 2))
 
     def near_copies(i):
         own, place = piece(i, 0)
-        to = gathered[items[i][1]]
+        to = gathered[items[i][2]]
         far = flipped(z, 2)
         near = flipped(z, 1)
         return [
@@ -180,48 +206,34 @@
             remote(place(to, far), place(to, far), ysend.at[i, 1], yrecv.at[i, 1], s, near),
         ]
 
-    def seq_copies(i, j):
-        _, place = piece(i, j)
-        to = gathered[items[i][1]]
-        other = flipped(s, order(i)[j])
-        return [
-            remote(place(to, (z + d) % heads), place(to, (z + d) % heads), gsend.at[i, j, d - 1], grecv.at[i, j, d - 1],
-                   other, z)
-            for d in range(1, heads)
-        ]
-
     count = len(items)
+
+    def stage(i, k):
+        if k == 0:
+            return [far_copy(i)]
+        return near_copies(i) if k == 1 else seq_copies(i, k - 2)
+
+    stages = 2 + len(masks)
+    pairs = (max(item[0] for item in items) + 2) // 2
+    for t in range(pairs + stages):
+        for k in reversed(range(stages + 1)):
+            for i in range(count):
+                if items[i][0] // 2 != t - k or k > 2 + steps[i]:
+                    continue
+                if k > 0:
+                    for copy in stage(i, k - 1):
+                        copy.wait_recv()
+                if k < 2 + steps[i]:
+                    for copy in stage(i, k):
+                        copy.start()
+        if t == 0:
+            for target in range(heads):
+                sends(target, "start")
+            for i in range(count):
+                own_load(i).start()
     for i in range(count):
-        far_copy(i).start()
-    for target in range(heads):
-        sends(target, "start")
-    for i in range(count):
-        own_copy(i).start()
-
-    def advance(i, k):
-        if k == 0:
-            far_copy(i).wait_recv()
-        elif k == 1:
-            for copy in near_copies(i):
-                copy.wait_recv()
-        else:
-            for copy in seq_copies(i, k - 2):
-                copy.wait_recv()
-        if k == 0:
-            for copy in near_copies(i):
-                copy.start()
-        elif k - 1 < len(masks):
-            for copy in seq_copies(i, k - 1):
-                copy.start()
-
-    stages = 2 + len(masks)
-    pairs = count // 2
-    for t in range(pairs + stages - 1):
-        for k in reversed(range(stages)):
-            p = t - k
-            if 0 <= p < pairs:
-                advance(2 * p, k)
-                advance(2 * p + 1, k)
+        own_load(i).wait()
+        own_store(i).start()
     for source in range(heads):
         arrive(source)
     for target in range(heads):
@@ -237,16 +249,16 @@
         halo_copy(z, s + 1).wait_send()
 
     for i in range(count):
-        own_copy(i).wait()
+        own_store(i).wait()
         far_copy(i).wait_send()
         for copy in near_copies(i):
             copy.wait_send()
-        for j in range(len(masks)):
+        for j in range(steps[i]):
             for copy in seq_copies(i, j):
                 copy.wait_send()
 
 
-def start_all(tokens, codes, cotangent, weights, items, shapes, collective_id):
+def start_all(tokens, codes, taps, weights, items, steps, shapes, collective_id):
     seq, heads = lax.axis_size("seq"), lax.axis_size("head")
     seqs, rows, width = tokens.shape
     mine = rows // heads
@@ -256,23 +268,30 @@
     out_shape = [
         jax.ShapeDtypeStruct((seqs, mine + HALO, heads * width), tokens.dtype),
         jax.ShapeDtypeStruct((seqs, mine, heads * codes.shape[2]), codes.dtype),
-        jax.ShapeDtypeStruct((seqs, mine, heads * width), cotangent.dtype),
+        jax.ShapeDtypeStruct((heads, *taps.shape), taps.dtype),
     ] + [jax.ShapeDtypeStruct((heads, *shape), bf16) for shape in shapes]
     return pl.pallas_call(
-        partial(start_body, seq, len(weights), items),
+        partial(start_body, seq, len(weights), items, steps),
         out_shape=out_shape,
         in_specs=[anywhere] * (3 + len(weights)),
         out_specs=[anywhere] * len(out_shape),
-        scratch_shapes=[
-            dma((3, heads)), dma((3, heads)), dma((1,)), dma((1,)), dma, dma((heads,)), dma((3 + count,)),
+        scratch_shapes=[pltpu.VMEM((item[5], weights[item[1]].shape[1]), bf16) for item in items]
+        + [
+            dma((3, heads)), dma((3, heads)), dma, dma((heads,)), dma((3 + count,)),
             dma((count,)), dma((count,)), dma((count, 2)), dma((count, 2)), dma((count, 3, 3)), dma((count, 3, 3)),
         ],
-        compiler_params=pltpu.CompilerParams(collective_id=collective_id, has_side_effects=True),
+        compiler_params=pltpu.CompilerParams(
+            collective_id=collective_id, has_side_effects=True, vmem_limit_bytes=24 * 2**20),
         name="start_exchange",
-    )(tokens, codes, cotangent, *weights)
-
-
-def exchange_body(count, heads, per_block, backward, value, logs, out, packed, got, ready, send, recv, bsend, brecv):
+    )(tokens, codes, taps, *weights)
+
+
+def exchange_body(count, heads, per_block, backward, items, n_more, *refs):
+    value, logs = refs[:2]
+    out = refs[2 + n_more]
+    gathered = refs[3 + n_more : 3 + 2 * n_more]
+    packed, got, ready, send, recv, bsend, brecv, gsend, grecv = refs[3 + 2 * n_more :]
+    _, seq_copies = over_seq(items, gathered, gsend, grecv, lax.axis_index("seq"), lax.axis_index("head"))
     me = lax.axis_index("seq") * heads + lax.axis_index("head")
     part = value.shape[0] // count
     tail = packed.shape[1] - part
@@ -330,6 +349,9 @@
         lax.fori_loop(1, count, one, 0)
 
     each(lambda p: there(p).start())
+    for i in range(len(items)):
+        for copy in seq_copies(i, 1):
+            copy.start()
 
     def step(i, state):
         p = count - 1 - i if backward else i
@@ -349,32 +371,48 @@
 
     lax.fori_loop(0, count, step, jnp.zeros((part, value.shape[1]), f32))
     out[pl.ds(pl.multiple_of(me * part, part), part)] = ready[me]
+    for i in range(len(items)):
+        for copy in seq_copies(i, 1):
+            copy.wait_recv()
+        for copy in seq_copies(i, 2):
+            copy.start()
     each(lambda p: home(p).wait_recv())
     each(lambda p: there(p).wait_send())
     each(lambda p: back(p).wait_send())
-
-
-def exchange(value, logs, backward, collective_id):
+    for i in range(len(items)):
+        for copy in seq_copies(i, 2):
+            copy.wait()
+        for copy in seq_copies(i, 1):
+            copy.wait_send()
+
+
+def exchange(value, logs, backward, collective_id, items=(), gathered=()):
     heads = lax.axis_size("head")
     count = lax.axis_size("seq") * heads
     rows, width = value.shape
     part = rows // count
     tail = 16
     dma = pltpu.SemaphoreType.DMA
+    more = len(gathered)
+    anywhere, near = pl.BlockSpec(memory_space=pl.ANY), pl.BlockSpec(memory_space=pltpu.VMEM)
     return pl.pallas_call(
-        partial(exchange_body, count, heads, rows // logs.shape[0], backward),
-        out_shape=jax.ShapeDtypeStruct((rows, width), bf16),
-        in_specs=[pl.BlockSpec(memory_space=pltpu.VMEM)] * 2,
-        out_specs=pl.BlockSpec(memory_space=pltpu.VMEM),
+        partial(exchange_body, count, heads, rows // logs.shape[0], backward, items, more),
+        out_shape=[jax.ShapeDtypeStruct((rows, width), bf16)]
+        + [jax.ShapeDtypeStruct(a.shape, a.dtype) for a in gathered],
+        in_specs=[near] * 2 + [anywhere] * more,
+        out_specs=[near] + [anywhere] * more,
+        input_output_aliases={2 + i: 1 + i for i in range(more)},
         scratch_shapes=[
             pltpu.VMEM((count, part + tail, width), bf16),
             pltpu.VMEM((count, part + tail, width), bf16),
             pltpu.VMEM((count, part, width), bf16),
             dma((count,)), dma((count,)), dma((count,)), dma((count,)),
+            dma((max(len(items), 1), 3, 3)), dma((max(len(items), 1), 3, 3)),
         ],
-        compiler_params=pltpu.CompilerParams(collective_id=collective_id, has_side_effects=True),
+        compiler_params=pltpu.CompilerParams(
+            collective_id=collective_id, has_side_effects=True, vmem_limit_bytes=16 * 2**20),
         name="exchange_states",
-    )(value, logs)
+    )(value, logs, *gathered)
 
 
 def aligned(x, size):
@@ -733,20 +771,12 @@
     return jnp.einsum(spec, lower, values, precision=lax.Precision.HIGHEST, preferred_element_type=f32)
 
 
-def whole(weights):
+def whole(weight):
     seq = lax.axis_size("seq")
-    parts = []
-    for w in weights:
-        part = w.shape[0] // seq
-        parts.append(lax.dynamic_slice_in_dim(w, lax.axis_index("seq") * part, part, 0))
-    mine = jnp.concatenate(parts, axis=0)
+    part = weight.shape[0] // seq
+    mine = lax.dynamic_slice_in_dim(weight, lax.axis_index("seq") * part, part, 0)
     every = lax.all_gather(mine, ("head", "seq"), axis=0, tiled=True)
-    every = every.reshape(lax.axis_size("head"), seq, *mine.shape)
-    out, at = [], 0
-    for w, p in zip(weights, parts):
-        out.append(every[:, :, at : at + p.shape[0]].reshape(-1, *w.shape))
-        at += p.shape[0]
-    return out
+    return every.reshape(lax.axis_size("head"), *weight.shape)
 
 
 def chunks(array, rows, count):
@@ -782,30 +812,26 @@
     conv_width = 2 * key_width + value_width
     mixer_width = conv_width + value_width
 
-    half = width // 2
-    items = [
-        (0, 0, 0, 0, width, 0),
-        (1, 0, 0, 0, width, key_width),
-        (2, 0, 0, 0, half, 2 * key_width),
-        (2, 0, 0, half, half, 2 * key_width),
-        (3, 0, 0, 0, half, conv_width),
-        (3, 0, 0, half, half, conv_width),
-        (4, 1, 0, 0, w_out.shape[0] // 2, 0),
-        (4, 1, 0, w_out.shape[0] // 2, w_out.shape[0] // 2, 0),
-    ]
-    tokens_ext, codes, upstream, w_mixer, w_proj = start_all(
+    half, ff = width // 2, w_gate.shape[1]
+    out_half, ff_half = w_out.shape[0] // 2, ff // 2
+    items = [(0, 0, 0, 0, 0, width, 0, key_width), (1, 1, 0, 0, 0, width, key_width, key_width)]
+    items += [(i, 2, 0, 0, i * half, half, 2 * key_width, value_width) for i in range(2)]
+    items += [(i, 3, 0, 0, i * half, half, conv_width, value_width) for i in range(2)]
+    items += [(i, 4, 1, 0, i * out_half, out_half, 0, width) for i in range(2)]
+    pair = [(2 + 2 * a + i, 5 + a, 2 + a, 1, i * ff_half, ff_half, 0, width) for a in range(2) for i in range(2)]
+    tokens_ext, codes, taps, w_mixer, w_proj, w_gate_all, w_up_all = start_all(
         tokens,
         decay_codes.astype(jnp.int16),
-        cotangent,
-        (w_query, w_key, w_value, w_out_gate, w_out),
-        items,
-        ((width, mixer_width), w_out.shape),
+        jnp.concatenate([conv_query, conv_key, conv_value], axis=1),
+        (w_query, w_key, w_value, w_out_gate, w_out, w_gate.T, w_up.T),
+        items + pair,
+        [3] * len(items) + [1] * len(pair),
+        ((width, mixer_width), w_out.shape, w_down.shape, w_down.shape),
         1,
     )
-    (w_gate_all,) = whole((w_gate,))
-    (w_up_all,) = whole((w_up,))
-    (w_low,) = whole((w_down,))
-    taps = lax.all_gather(jnp.concatenate([conv_query, conv_key, conv_value], axis=1), "head")
+    w_low = whole(w_down)
+    upstream, codes = lax.optimization_barrier((cotangent, codes))
+    upstream = lax.all_to_all(upstream, "head", 1, 2, tiled=True)
 
     first_rows = (jnp.arange(mine + HALO) < HALO) & (place == 0)
     resid_ext = jnp.where(first_rows[None, :, None], 0, tokens_ext).astype(f32)
@@ -851,7 +877,10 @@
         starts.append(span_decay[:, :, n, None, :] * starts[n] + update[:, :, n])
     local_end = starts.pop()
     flat = (-1, key_width)
-    incoming = exchange(local_end.astype(bf16).reshape(flat), log_total, False, 2)
+    pair = [(item[0], 0, item[2] - 2, *item[3:]) for item in pair]
+    incoming, w_gate_all, w_up_all = exchange(
+        local_end.astype(bf16).reshape(flat), log_total, False, 2, pair, (w_gate_all, w_up_all)
+    )
     incoming = incoming.reshape(local_end.shape).astype(f32)
     scores = jnp.where(causal, dot("hantk,hanuk->hantu", query_exp, keyed_exp), 0.0)
     inner = dot("hantu,hanuv->hantv", scores, valued)
@@ -865,8 +894,8 @@
     hidden_in = resid + jnp.sum(rounded(dot("hste,hed->hstd", gated, w_proj)), axis=0)
     second_scale = row_scale(hidden_in)
     normed_two = (hidden_in * second_scale * mlp_gain).astype(bf16)
-    gate_val = dot("std,hdf->hstf", normed_two, w_gate_all)
-    up_val = dot("std,hdf->hstf", normed_two, w_up_all)
+    gate_val = dot("std,hfd->hstf", normed_two, w_gate_all)
+    up_val = dot("std,hfd->hstf", normed_two, w_up_all)
     gate_act = jax.nn.silu(gate_val)
     hidden = (gate_act * up_val).astype(bf16)
     layer_out = hidden_in + jnp.sum(rounded(dot("hstf,hfd->hstd", hidden, w_low)), axis=0)
@@ -875,9 +904,9 @@
     grad_down = dot("hstf,std->hfd", hidden, upstream)
     d_gate = (d_hidden * up_val * silu_slope(gate_val)).astype(bf16)
     d_up = (d_hidden * gate_act).astype(bf16)
-    grad_gate = dot("std,hstf->hdf", normed_two, d_gate)
-    grad_up = dot("std,hstf->hdf", normed_two, d_up)
-    d_normed_two = dot("hstf,hdf->std", d_gate, w_gate_all) + dot("hstf,hdf->std", d_up, w_up_all)
+    grad_gate = dot("hstf,std->hfd", d_gate, normed_two)
+    grad_up = dot("hstf,std->hfd", d_up, normed_two)
+    d_normed_two = dot("hstf,hfd->std", d_gate, w_gate_all) + dot("hstf,hfd->std", d_up, w_up_all)
     d_hidden_in = upstream.astype(f32) + norm_back(hidden_in, second_scale, mlp_gain, d_normed_two)
     grad_mlp_gain = jnp.sum(d_normed_two * hidden_in * second_scale, axis=(0, 1))
     d_mixer = d_hidden_in.astype(bf16)
@@ -890,7 +919,7 @@
 
     d_states = dot("hantk,hantv->hanvk", query_exp, d_core)
     own_grad = jnp.sum(carry_decay[:, :, :, None, :] * d_states, axis=2)
-    leaving = exchange(own_grad.astype(bf16).reshape(flat), log_total, True, 3)
+    (leaving,) = exchange(own_grad.astype(bf16).reshape(flat), log_total, True, 3)
     d_ends = [leaving.reshape(own_grad.shape).astype(f32)]
     for n in range(blocks - 1, 0, -1):
         d_ends.append(span_decay[:, :, n, None, :] * d_ends[-1] + d_states[:, :, n])
@@ -934,11 +963,8 @@
     lanes = -(-small.shape[1] // (small_rows * 128)) * 128
     small = jnp.pad(small, ((0, 0), (0, small_rows * lanes - small.shape[1]))).reshape(heads, small_rows, lanes)
     arrays = [a.astype(bf16) for a in (grad_gate, grad_up, grad_down, grad_out, grad_mixer, small)]
-    ff = w_gate.shape[1]
     plan = (
-        chunks(0, width, 4)
-        + chunks(1, width, 4)
-        + [(2, 1, 0, ff // 2), (2, 1, ff // 2, ff // 2)]
+        [(a, 1, i * (ff // 2), ff // 2) for a in range(3) for i in range(2)]
         + chunks(3, w_out.shape[0], 2)
         + chunks(4, width, 4)
         + chunks(5, small_rows, 2)
@@ -970,8 +996,8 @@
         small[2 * own_width : at],
         grad_out,
         small[own_width : 2 * own_width],
-        grad_gate,
-        grad_up,
+        grad_gate.T,
+        grad_up.T,
         grad_down,
     )
 

time: 669 us -> 592 us (0.88)
  waiting for transfers between devices: 21.4 us -> 0.02 us
  matrix products: 108 us -> 89 us
  blocking collectives: 17.5 us -> 0 us
  local copies, waits for them, and re-layouts: 69.3 us -> 53.6 us
  Pallas kernels: 381 us -> 368 us
  starting transfers between devices: 0.12 us -> 7.66 us
    another operation x2 -> x0, local copies, waits for them, and re-layouts: 21.5 us -> none  [whole(): out.append(every[:, :, at:at + p.shape[0]].reshape(-1, *w.shape))]
    all_gather x3 -> x1, waiting for transfers between devices: 21.4 us -> 0.01 us  [whole(): every = lax.all_gather(mine, ('head', 'seq'), axis=0, tiled=True)]
    unnamed x141 -> x177, local copies, waits for them, and re-layouts: 18.1 us -> 37.2 us
    dot_general x27, matrix products: 106 us -> 87 us  [dot(): jnp.einsum(spec, left.astype(bf16), right.astype(bf16), preferred_element...]
    all_gather x1 -> x0, blocking collectives: 17.5 us -> none  [local(): lax.all_gather(jnp.concatenate([conv_query, conv_key, conv_value], axis=1...]
    convert_element_type x2 -> x0, local copies, waits for them, and re-layouts: 16.9 us -> none  [local(): a.astype(bf16)]
    all_to_all x0 -> x1, starting transfers between devices: none -> 7.63 us  [local(): upstream = lax.all_to_all(upstream, 'head', 1, 2, tiled=True)]
    pallas_call x1, Pallas kernels: 118 us -> 111 us  [start_all(): pl.pallas_call(partial(start_body, seq, len(weights), items, steps), out_...]
  transfers between devices with their start and end apart: 3 -> 2, of which waited for: 1 -> 0; matrix products, arithmetic and copies ran while one was open for 12% -> 8% of each run, Pallas kernels for 26% -> 28%
where the time goes in v4:
time: 592 us; the launch traced here: 587 us
  Pallas kernels  368 us (62%)
  matrix products  89 us (15%)
  local copies, waits for them, and re-layouts  53.6 us (9%)
  other arithmetic  53.1 us (9%)
  between operations  15.4 us (3%)
  starting transfers between devices  7.66 us (1%)
    pallas_call x1, Pallas kernels, finish_all(): pl.pallas_call(partial(finish_body, seq, plan, len(arrays)), out_shape=ou...  173 us
    pallas_call x1, Pallas kernels, start_all(): pl.pallas_call(partial(start_body, seq, len(weights), items, steps), out_...  111 us
    dot_general x27, matrix products, dot(): jnp.einsum(spec, left.astype(bf16), right.astype(bf16), preferred_element...  87 us
    pallas_call x2, Pallas kernels, exchange(): pl.pallas_call(partial(exchange_body, count, heads, rows // logs.shape[0]...  84.2 us
    unnamed x177, local copies, waits for them, and re-layouts  37.2 us
  transfers between devices with their start and end apart: 2, of which 0 were waited for; matrix products, arithmetic and copies ran while one was open for 8% of the time, Pallas kernels for 28%

profile of v4, /device:TPU:1, one launch (start us, length us, event | category | flops | bytes accessed | tf_op | source)
XLA Modules:
  0.0 587.0 jit_solution(13447362770929402234)
XLA Ops:
  17.9 111.3 %start_exchange.1 = (bf16[2,272,1024]{2,1,0:T(8,128)(2,1)S(1)}, s16[2,256,512]{2,1,0:T(8,128)(2,1)S(1)}, f32[4,4,512]{2,1,0:T(4,128)S(1)}, bf16[4,1024,768]{2,1,...) custom-call(bf16[2,1024,256]{2,1,0:T(8,128)(2,1)S(1)} %copy-done.8, ...), custom_call_target="tpu_custom_call" | custom-call | tf_op jit(solution)/shard_map/start_exchange/pallas_call | solution.py:273
  129.2 2.4 copy-done.2
  131.6 2.4 copy-done.4
  134.8 2.6 copy-done.16
  140.8 7.6 %all-to-all-start = ((bf16[2,1024,256]{2,0,1:T(2,128)(2,1)}), bf16[2,1024,256]{2,0,1:T(2,128)(2,1)}, u32[]{:S(2)}, u32[]{:S(2)}) async-start(bf16[2,1024,256]{2,0,1:T(2,128)(2,1)} %copy.59), calls=%async_computation | async-start | bytes 2097152 | tf_op jit(solution)/shard_map/all_to_all | solution.py:834
  153.1 6.8 %convert_bitcast_fusion = bf16[4,2,272,768]{3,2,1,0:T(8,128)(2,1)S(1)} fusion(bf16[4,1024,768]{2,1,0:T(8,128)(2,1)} %copy-done.16, f32[1024]{0:T(1024)S(1)} %copy-done.63, f32[2,272]{1,0:T(2,128)S(1)} %get-tuple-element.119, bf16[2,272,1024]{2,1,0:T(8,128)(2,1)S(1)} %get-tuple-element.37, pred[272]{0:T(512)(128)(4,1)S(1)} %fusion.85), kind=kOutput, calls=%fused_computation.50 | convolution fusion | flops 3427008512 | bytes 10754448 | tf_op jit(solution)/shard_map/std,hde->hste/dot_general | solution.py:765
  161.8 3.9 fusion.24
  171.8 51.0 %exchange_states.2 = (bf16[2048,128]{1,0:T(8,128)(2,1)S(1)}, bf16[4,704,1024]{2,1,0:T(8,128)(2,1)S(1)}, bf16[4,704,1024]{2,1,0:T(8,128)(2,1)S(1)}) custom-call(bf16[2048,128]{1,0:T(8,128)(2,1)S(1)} %fusion.72.refs_0_, f32[8,128]{1,0:T(8,128)S(1)} %bitcast.335, bf16[4,704,1024]{2,1,0:T(8,128)(2,1)S(1)} %bitcast.319, ...), custom_call_target="tpu_custom_call", output_to_operand_aliasing={{1}: (2, {}), {2}: (3, {})} | custom-call | tf_op jit(solution)/shard_map/exchange_states/pallas_call | solution.py:398
  222.8 2.4 copy-done.5
  230.2 2.6 multiply_convert_fusion.1
  237.4 5.0 fusion.12
  242.4 5.0 fusion.8
  252.0 2.7 all_to_all.16
  254.7 11.4 %fusion.15 = (bf16[4,2,256,704]{2,3,1,0:T(8,128)(2,1)S(1)}, bf16[4,2,256,704]{2,3,1,0:T(8,128)(2,1)}, bf16[4,2,256,704]{2,3,1,0:T(8,128)(2,1)S(1)}) fusion(f32[4,704,2,256]{3,1,2,0:T(8,128)} %fusion.8, f32[4,704,2,256]{3,1,2,0:T(8,128)} %fusion.12, bf16[4,704,1024,1]{2,1,3,0:T(8,128)(2,1)} %bitcast.377, bf16[2,256,1024,1]{2,1,0,3:T(8,128)(2,1)} %reshape.236), kind=kOutput, calls=%fused_computation.24 | convolution fusion | flops 2977300480 | bytes 27000832 | tf_op jit(solution)/shard_map/std,hfd->hstf/dot_general | solution.py:765
  266.1 7.3 %fusion.6 = f32[2,256,1024,1]{2,1,0,3:T(8,128)S(1)} fusion(bf16[4,2,256,704]{2,3,1,0:T(8,128)(2,1)S(1)} %get-tuple-element.78, bf16[4,704,1024]{2,1,0:T(8,128)(2,1)} %copy-done.5), kind=kOutput, calls=%fused_computation.13 | convolution fusion | flops 2952790016 | bytes 10747904 | tf_op jit(solution)/shard_map/hstf,hfd->std/dot_general | solution.py:765
  273.6 3.5 multiply_reduce_fusion.5
  277.1 3.9 convert_reduce_fusion
  284.6 2.6 fusion.54
  287.2 2.8 fusion.51
  291.8 33.2 %exchange_states.3 = bf16[2048,128]{1,0:T(8,128)(2,1)S(1)} custom-call(bf16[2048,128]{1,0:T(8,128)(2,1)S(1)} %bitcast.331, f32[8,128]{1,0:T(8,128)S(1)} %bitcast.336), custom_call_target="tpu_custom_call" | custom-call | tf_op jit(solution)/shard_map/exchange_states/pallas_call | solution.py:398
  335.0 4.9 multiply_reduce_fusion.3
  339.9 7.0 %broadcast_multiply_fusion.3 = (f32[4,2,256,512]{3,2,1,0:T(8,128)}, f32[4,2,256,512]{3,2,1,0:T(8,128)}, f32[4,2,256,512]{3,2,1,0:T(8,128)}, f32[4,2,256,512]{3,2,1,0:T(8,128)}) fusion(f32[4,2,256,512]{3,2,1,0:T(8,128)S(1)} %get-tuple-element.68, f32[4,512]{1,0:T(4,128)S(1)} %get-tuple-element.133, f32[4,512]{1,0:T(4,128)S(1)} %get-tuple-element.130, ...), kind=kLoop, calls=%fused_computation.113 | loop fusion | flops 4194304 | bytes 21004288 | tf_op jit(solution)/shard_map/mul | solution.py:942
  346.9 7.0 %add_convert_fusion = bf16[4,2,272,512]{3,2,1,0:T(8,128)(2,1)S(1)} fusion(f32[4,2,256,512]{3,2,1,0:T(8,128)} %get-tuple-element.85, f32[4,2,256,512]{3,2,1,0:T(8,128)} %get-tuple-element.86, f32[4,2,256,512]{3,2,1,0:T(8,128)} %get-tuple-element.87, f32[4,2,256,512]{3,2,1,0:T(8,128)} %get-tuple-element.84), kind=kLoop, calls=%fused_computation.36 | loop fusion | flops 4456448 | bytes 19005440 | tf_op jit(solution)/shard_map/convert.23
  354.0 5.9 fusion.37
  359.9 7.9 %fusion.1.refs_6_ = bf16[4,1024,768]{2,1,0:T(8,128)(2,1)} fusion(bf16[4,2,256,256]{3,2,1,0:T(8,128)(2,1)S(1)} %copy-done.58, bf16[4,2,272,512]{3,2,1,0:T(8,128)(2,1)S(1)} %add_convert_fusion, f32[1024]{0:T(1024)S(1)} %copy-done.63, f32[2,272]{1,0:T(2,128)S(1)} %get-tuple-element.119, bf16[2,272,1024]{2,1,0:T(8,128)(2,1)S(1)} %get-tuple-element.37, ...), kind=kOutput, calls=%fused_computation.8 | convolution fusion | flops 3438510080 | bytes 10688912 | tf_op jit(solution)/shard_map/std,hste->hde/dot_general | solution.py:765
  367.8 2.6 bitcast_convert_fusion.4.refs_5_
  370.4 4.9 bitcast_convert_fusion.2.refs_3_
  375.3 5.0 bitcast_convert_fusion.3.refs_2_
  380.3 4.9 bitcast_convert_fusion.1.refs_4_
  386.8 3.3 fusion.34.refs_1_
  390.1 172.7 %finish_sums.1 = (bf16[2,1024,256]{2,1,0:T(8,128)(2,1)}, bf16[2,1024,256]{2,1,0:T(8,128)(2,1)}, bf16[4,2,16,256]{3,2,1,0:T(8,128)(2,1)}, bf16[704,1024]{1,0:T(8,...) custom-call(bf16[2,256,1024]{2,1,0:T(8,128)(2,1)} %get-tuple-element, ...), custom_call_target="tpu_custom_call" | custom-call | tf_op jit(solution)/shard_map/finish_sums/pallas_call | solution.py:732
  563.7 2.8 fusion.99
  (261 shorter events, 72.3 us)
Async XLA Ops:
  7.2 4.1 copy-start.6
  7.2 4.1 copy-start.9
  7.2 247.5 %all-gather.2.cloned.1.call-start = ((), (), s32[]{:S(2)}) async-start(), calls=%async_computation.1 | async-start | bytes 5947392 | tf_op jit(solution)/shard_map/all_gather | solution.py:778
  17.9 120.9 %copy-start.54 = (bf16[2,1024,256]{2,1,0:T(8,128)(2,1)S(1)}, bf16[2,1024,256]{2,1,0:T(8,128)(2,1)}, u32[]{:S(2)}) copy-start(bf16[2,1024,256]{2,1,0:T(8,128)(2,1)} %param.19) | copy-start | bytes 3145732
  138.7 9.7 %copy-start.13 = (s16[2,256,512]{2,1,0:T(8,128)(2,1)S(1)}, s16[2,256,512]{2,1,0:T(8,128)(2,1)}, u32[]{:S(2)}) copy-start(s16[2,256,512]{2,1,0:T(8,128)(2,1)} %copy-done.12) | copy-start | bytes 1572868
  140.8 106.7 %all-to-all-start = ((bf16[2,1024,256]{2,0,1:T(2,128)(2,1)}), bf16[2,1024,256]{2,0,1:T(2,128)(2,1)}, u32[]{:S(2)}, u32[]{:S(2)}) async-start(bf16[2,1024,256]{2,0,1:T(2,128)(2,1)} %copy.59), calls=%async_computation | async-start | bytes 2097152 | tf_op jit(solution)/shard_map/all_to_all | solution.py:834
  148.7 4.4 copy-start.63
  151.9 14.4 %copy-start.25 = (f32[4,2,4,64,128]{4,3,2,1,0:T(8,128)}, f32[4,2,4,64,128]{4,3,2,1,0:T(8,128)S(1)}, u32[]{:S(2)}) copy-start(f32[4,2,4,64,128]{4,3,2,1,0:T(8,128)S(1)} %convolution_bitcast_fusion) | copy-start | bytes 3145732
  161.8 3.9 copy-start.20
  165.9 62.6 %copy-start.30 = (bf16[4,2,256,256]{3,2,1,0:T(8,128)(2,1)}, bf16[4,2,256,256]{3,2,1,0:T(8,128)(2,1)S(1)}, u32[]{:S(2)}) copy-start(bf16[4,2,256,256]{3,2,1,0:T(8,128)(2,1)S(1)} %slice.269) | copy-start | bytes 3145732
  166.8 58.5 %copy-start.38 = (bf16[4,2,4,64,128]{4,3,2,1,0:T(8,128)(2,1)}, bf16[4,2,4,64,128]{4,3,2,1,0:T(8,128)(2,1)S(1)}, u32[]{:S(2)}) copy-start(bf16[4,2,4,64,128]{4,3,2,1,0:T(8,128)(2,1)S(1)} %get-tuple-element.96) | copy-start | bytes 1572868
  166.8 59.6 %copy-start.32 = (bf16[4,2,4,64,128]{4,3,2,1,0:T(8,128)(2,1)}, bf16[4,2,4,64,128]{4,3,2,1,0:T(8,128)(2,1)S(1)}, u32[]{:S(2)}) copy-start(bf16[4,2,4,64,128]{4,3,2,1,0:T(8,128)(2,1)S(1)} %get-tuple-element.102) | copy-start | bytes 1572868
  166.9 4.0 slice-start.6
  167.7 4.1 slice-start.7
  235.8 6.6 %slice-start.8 = ((s8[5767168]{0:T(1024)(128)(4,1)}), s8[4194304]{0:T(1024)(128)(4,1)S(1)}, s32[]{:S(2)}) async-start(s8[5767168]{0:T(1024)(128)(4,1)} %bitcast.326), calls=%async_computation.10 | async-start | bytes 8388608
  236.1 6.4 %copy-start.55 = (bf16[2,256,1024,1]{2,1,0,3:T(8,128)(2,1)}, bf16[2,256,1024,1]{2,1,0,3:T(8,128)(2,1)S(1)}, u32[]{:S(2)}) copy-start(bf16[2,256,1024,1]{2,1,0,3:T(8,128)(2,1)S(1)} %fusion.68) | copy-start | bytes 3145732
  237.4 5.0 slice-start.9
  252.0 21.5 %slice-start.4 = ((s8[5767168]{0:T(1024)(128)(4,1)}), s8[1572864]{0:T(1024)(128)(4,1)S(1)}, s32[]{:S(2)}) async-start(s8[5767168]{0:T(1024)(128)(4,1)} %bitcast.322), calls=%async_computation.6 | async-start | bytes 3145728
  254.7 18.8 %slice-start.5 = ((s8[5767168]{0:T(1024)(128)(4,1)}), s8[4194304]{0:T(1024)(128)(4,1)S(1)}, s32[]{:S(2)}) async-start(s8[5767168]{0:T(1024)(128)(4,1)} %bitcast.322), calls=%async_computation.7 | async-start | bytes 8388608
  266.1 7.4 %copy-start.66 = (bf16[4,2,256,704]{2,3,1,0:T(8,128)(2,1)}, bf16[4,2,256,704]{2,3,1,0:T(8,128)(2,1)S(1)}, u32[]{:S(2)}) copy-start(bf16[4,2,256,704]{2,3,1,0:T(8,128)(2,1)S(1)} %get-tuple-element.78) | copy-start | bytes 8650756
  266.1 7.4 %copy-start.43 = (bf16[4,2,256,704]{2,3,1,0:T(8,128)(2,1)}, bf16[4,2,256,704]{2,3,1,0:T(8,128)(2,1)S(1)}, u32[]{:S(2)}) copy-start(bf16[4,2,256,704]{2,3,1,0:T(8,128)(2,1)S(1)} %get-tuple-element.76) | copy-start | bytes 8650756
  266.1 7.4 %copy-start.22 = (f32[2,256,1024]{2,1,0:T(8,128)S(1)}, f32[2,256,1024]{2,1,0:T(8,128)}, u32[]{:S(2)}) copy-start(f32[2,256,1024]{2,1,0:T(8,128)} %copy-done.21) | copy-start | bytes 6291460
  266.1 10.9 %slice-start.14 = ((s8[5767168]{0:T(1024)(128)(4,1)}), s8[4194304]{0:T(1024)(128)(4,1)S(1)}, s32[]{:S(2)}) async-start(s8[5767168]{0:T(1024)(128)(4,1)} %bitcast.378), calls=%async_computation.16 | async-start | bytes 8388608
  335.0 19.0 %slice-start.10 = ((s8[6291456]{0:T(1024)(128)(4,1)}), s8[4194304]{0:T(1024)(128)(4,1)S(1)}, s32[]{:S(2)}) async-start(s8[6291456]{0:T(1024)(128)(4,1)} %bitcast.337), calls=%async_computation.12 | async-start | bytes 8388608
  339.9 14.1 %slice-start.11 = ((s8[6291456]{0:T(1024)(128)(4,1)}), s8[2097152]{0:T(1024)(128)(4,1)S(1)}, s32[]{:S(2)}) async-start(s8[6291456]{0:T(1024)(128)(4,1)} %bitcast.337), calls=%async_computation.13 | async-start | bytes 4194304
  346.9 7.1 %copy-start.58 = (bf16[4,2,256,256]{3,2,1,0:T(8,128)(2,1)S(1)}, bf16[4,2,256,256]{3,2,1,0:T(8,128)(2,1)}, u32[]{:S(2)}) copy-start(bf16[4,2,256,256]{3,2,1,0:T(8,128)(2,1)} %get-tuple-element.80) | copy-start | bytes 3145732
  359.9 7.9 %copy-start.51 = (bf16[4,2,256,256]{3,2,1,0:T(8,128)(2,1)S(1)}, bf16[4,2,256,256]{3,2,1,0:T(8,128)(2,1)}, u32[]{:S(2)}) copy-start(bf16[4,2,256,256]{3,2,1,0:T(8,128)(2,1)} %copy-done.50) | copy-start | bytes 3145732
  370.4 4.9 copy-start.44
  375.3 5.0 copy-start.57
  375.3 5.0 copy-start.69
  380.3 6.5 %copy-start.62 = (f32[2,272]{1,0:T(2,128)S(1)}, f32[2,272]{1,0:T(2,128)}, u32[]{:S(2)}) copy-start(f32[2,272]{1,0:T(2,128)} %get-tuple-element.118) | copy-start | bytes 6532
  390.1 172.7 %copy-start.65 = (pred[4]{0:T(512)(128)(4,1)S(1)}, pred[4]{0:T(512)(128)(4,1)}, u32[]{:S(2)}) copy-start(pred[4]{0:T(512)(128)(4,1)} %compare_and_fusion) | copy-start | bytes 16
  (56 other events, 118.0 us)
Sparse Core Ops, SparseCore 0:
  11.5 108.4 all-gather.1

commit v5 on v4

v5 whole, which is shorter than its diff:
```python
from functools import partial

import jax
import jax.numpy as jnp
from jax import lax
from jax.experimental import pallas as pl
from jax.experimental.pallas import tpu as pltpu
from jax.sharding import PartitionSpec as P

SPAN = 64
HALO = 16
MESH = pl.DeviceIdType.MESH

epsilon = 1e-06
decay_unit = 2.0 ** (-17)
f32 = jnp.float32
bf16 = jnp.bfloat16

def row_scale(values):
    return lax.rsqrt(jnp.mean(values * values, axis=-1, keepdims=True) + epsilon)


def silu_slope(values):
    logistic = jax.nn.sigmoid(values)
    return logistic * (1.0 + values * (1.0 - logistic))


def norm_back(values, inverse, weights, upstream):
    weighted = weights * upstream
    return inverse * weighted - values * inverse**3 * jnp.mean(
        weighted * values, axis=-1, keepdims=True
    )


def rounded(values):
    return values.astype(bf16).astype(f32)


def whole(weight):
    seq = lax.axis_size("seq")
    part = weight.shape[0] // seq
    mine = lax.dynamic_slice_in_dim(weight, lax.axis_index("seq") * part, part, 0)
    every = lax.all_gather(mine, ("head", "seq"), axis=0, tiled=True)
    return every.reshape(lax.axis_size("head"), *weight.shape)


def flipped(place, mask):
    return place + mask - 2 * mask * (place // mask % 2)


def over_seq(items, gathered, gsend, grecv, s, z):
    heads = 4

    def order(i):
        return [4, 2, 1] if items[i][0] % 2 == 0 else [2, 4, 1]

    def span(i, j):
        _, _, to, axis, first, count, _, _ = items[i]
        size = count if axis == 0 else gathered[to].shape[2]
        begin = first if axis == 0 else 0
        for mask in order(i)[: j - 4 : -1] if j < 3 else []:
            size = size // 2
            begin = begin + (s // mask % 2) * size
        return pl.multiple_of(begin, size), size

    def seq_copies(i, j):
        _, _, to, axis, first, count, column, _ = items[i]
        begin, size = span(i, j)
        copies = []
        for d in range(1, heads):
            q = (z + d) % heads
            if axis == 0:
                place = gathered[to].at[q, pl.ds(begin, size), pl.ds(column, items[i][7])]
            else:
                place = gathered[to].at[q, pl.ds(first, count), pl.ds(begin, size)]
            copies.append(pltpu.make_async_remote_copy(
                place, place, gsend.at[i, j, d - 1], grecv.at[i, j, d - 1],
                device_id={"seq": flipped(s, order(i)[j]), "head": z}, device_id_type=MESH))
        return copies

    return span, seq_copies


def start_body(seq, n_weights, items, steps, *refs):
    tokens, codes, taps = refs[:3]
    weights = refs[3 : 3 + n_weights]
    out_tokens, out_codes, out_taps = refs[3 + n_weights : 6 + n_weights]
    n_sem = 11
    n_items = len(items)
    gathered = refs[6 + n_weights : -n_sem - n_items]
    held = refs[-n_sem - n_items : -n_sem]
    (tsend, trecv, hsend, hrecv, stay, zsend, zrecv, ysend, yrecv, gsend, grecv) = refs[-n_sem:]
    s, z = lax.axis_index("seq"), lax.axis_index("head")
    heads = 4
    masks = [1, 2, 4]

    def peer(to_s, to_z):
        return {"seq": to_s, "head": to_z}

    barrier = pltpu.get_barrier_semaphore()

    def greet(to_s, to_z):
        pl.semaphore_signal(barrier, 1, device_id=peer(to_s, to_z), device_id_type=MESH)

    for d in range(1, heads):
        greet(s, (z + d) % heads)
    for mask in masks:
        greet(flipped(s, mask), z)

    @pl.when((z == 0) & (s > 0))
    def _():
        for q in range(heads):
            greet(s - 1, q)

    greeted = heads - 1 + len(masks)

    @pl.when(s < seq - 1)
    def _():
        pl.semaphore_wait(barrier, greeted + 1)

    @pl.when(s == seq - 1)
    def _():
        pl.semaphore_wait(barrier, greeted)

    seqs, rows, width = tokens.shape
    mine = rows // heads

    def remote(src, dst, send, recv, to_s, to_z):
        return pltpu.make_async_remote_copy(src, dst, send, recv, device_id=peer(to_s, to_z), device_id_type=MESH)

    def columns(ref, q):
        n = ref.shape[2] // heads
        return pl.ds(pl.multiple_of(q * n, n), n)

    def sends(target, act):
        here = pl.ds(target * mine, mine)
        if target == 0:
            src, dst = tokens.at[:, pl.ds(0, mine)], out_tokens.at[:, pl.ds(HALO, mine), columns(out_tokens, z)]
        else:
            src = tokens.at[:, pl.ds(target * mine - HALO, mine + HALO)]
            dst = out_tokens.at[:, :, columns(out_tokens, z)]
        triples = [
            (src, dst),
            (codes.at[:, here], out_codes.at[:, :, columns(out_codes, z)]),
            (taps, out_taps.at[z]),
        ]

        @pl.when(z == target)
        def _():
            for i, (a, b) in enumerate(triples):
                copy = pltpu.make_async_copy(a, b, stay.at[i])
                if act == "start":
                    copy.start()
                else:
                    copy.wait()

        @pl.when(z != target)
        def _():
            for i, (a, b) in enumerate(triples):
                copy = remote(a, b, tsend.at[i, target], trecv.at[i, z], s, target)
                if act == "start":
                    copy.start()
                else:
                    copy.wait_send()

    def arrive(source):
        @pl.when(z != source)
        def _():
            here = pl.ds(0, mine)

            @pl.when(z == 0)
            def _():
                dst = out_tokens.at[:, pl.ds(HALO, mine), columns(out_tokens, source)]
                remote(tokens.at[:, here], dst, tsend.at[0, source], trecv.at[0, source], s, source).wait_recv()

            @pl.when(z != 0)
            def _():
                dst = out_tokens.at[:, :, columns(out_tokens, source)]
                remote(
                    tokens.at[:, pl.ds(0, mine + HALO)], dst, tsend.at[0, source], trecv.at[0, source], s, source
                ).wait_recv()

            for i, (a, b) in enumerate(
                ((codes.at[:, here], out_codes.at[:, :, columns(out_codes, source)]), (taps, out_taps.at[source]))
            ):
                remote(a, b, tsend.at[i + 1, source], trecv.at[i + 1, source], s, source).wait_recv()

    def halo_copy(source, to_s):
        return remote(
            tokens.at[:, pl.ds(rows - HALO, HALO)], out_tokens.at[:, pl.ds(0, HALO), columns(out_tokens, source)],
            hsend, hrecv.at[source], to_s, 0,
        )

    @pl.when(s < seq - 1)
    def _():
        halo_copy(z, s + 1).start()

    span, seq_copies = over_seq(items, gathered, gsend, grecv, s, z)

    def piece(i, j):
        _, weight, _, axis, first, count, column, _ = items[i]
        begin, size = span(i, j)
        wide = weights[weight].shape[1]
        if axis == 0:
            own = weights[weight].at[pl.ds(begin, size)]
            place = lambda ref, q: ref.at[q, pl.ds(begin, size), pl.ds(column, wide)]
        else:
            own = weights[weight].at[pl.ds(first, count), pl.ds(begin, size)]
            place = lambda ref, q: ref.at[q, pl.ds(first, count), pl.ds(begin, size)]
        return own, place

    def own_load(i):
        _, weight, _, _, first, count, _, _ = items[i]
        return pltpu.make_async_copy(weights[weight].at[pl.ds(first, count)], held[i], stay.at[3 + i])

    def own_store(i):
        _, weight, to, _, first, count, column, _ = items[i]
        wide = weights[weight].shape[1]
        return pltpu.make_async_copy(
            held[i], gathered[to].at[z, pl.ds(first, count), pl.ds(column, wide)], stay.at[3 + i])

    def far_copy(i):
        own, place = piece(i, 0)
        return remote(own, place(gathered[items[i][2]], z), zsend.at[i], zrecv.at[i], s, flipped(z, 2))

    def near_copies(i):
        own, place = piece(i, 0)
        to = gathered[items[i][2]]
        far = flipped(z, 2)
        near = flipped(z, 1)
        return [
            remote(own, place(to, z), ysend.at[i, 0], yrecv.at[i, 0], s, near),
            remote(place(to, far), place(to, far), ysend.at[i, 1], yrecv.at[i, 1], s, near),
        ]

    count = len(items)

    def stage(i, k):
        if k == 0:
            return [far_copy(i)]
        return near_copies(i) if k == 1 else seq_copies(i, k - 2)

    stages = 2 + len(masks)
    pairs = (max(item[0] for item in items) + 2) // 2
    for t in range(pairs + stages):
        for k in reversed(range(stages + 1)):
            for i in range(count):
                if items[i][0] // 2 != t - k or k > 2 + steps[i]:
                    continue
                if k > 0:
                    for copy in stage(i, k - 1):
                        copy.wait_recv()
                if k < 2 + steps[i]:
                    for copy in stage(i, k):
                        copy.start()
        if t == 0:
            for target in range(heads):
                sends(target, "start")
            for i in range(count):
                own_load(i).start()
    for i in range(count):
        own_load(i).wait()
        own_store(i).start()
    for source in range(heads):
        arrive(source)
    for target in range(heads):
        sends(target, "wait")

    @pl.when((z == 0) & (s > 0))
    def _():
        for q in range(heads):
            halo_copy(q, s - 1).wait_recv()

    @pl.when(s < seq - 1)
    def _():
        halo_copy(z, s + 1).wait_send()

    for i in range(count):
        own_store(i).wait()
        far_copy(i).wait_send()
        for copy in near_copies(i):
            copy.wait_send()
        for j in range(steps[i]):
            for copy in seq_copies(i, j):
                copy.wait_send()


def start_all(tokens, codes, taps, weights, items, steps, shapes, collective_id):
    seq, heads = lax.axis_size("seq"), lax.axis_size("head")
    seqs, rows, width = tokens.shape
    mine = rows // heads
    count = len(items)
    dma = pltpu.SemaphoreType.DMA
    anywhere = pl.BlockSpec(memory_space=pl.ANY)
    out_shape = [
        jax.ShapeDtypeStruct((seqs, mine + HALO, heads * width), tokens.dtype),
        jax.ShapeDtypeStruct((seqs, mine, heads * codes.shape[2]), codes.dtype),
        jax.ShapeDtypeStruct((heads, *taps.shape), taps.dtype),
    ] + [jax.ShapeDtypeStruct((heads, *shape), bf16) for shape in shapes]
    return pl.pallas_call(
        partial(start_body, seq, len(weights), items, steps),
        out_shape=out_shape,
        in_specs=[anywhere] * (3 + len(weights)),
        out_specs=[pl.BlockSpec(memory_space=pltpu.HBM)] * len(out_shape),
        scratch_shapes=[pltpu.VMEM((item[5], weights[item[1]].shape[1]), bf16) for item in items]
        + [
            dma((3, heads)), dma((3, heads)), dma, dma((heads,)), dma((3 + count,)),
            dma((count,)), dma((count,)), dma((count, 2)), dma((count, 2)), dma((count, 3, 3)), dma((count, 3, 3)),
        ],
        compiler_params=pltpu.CompilerParams(
            collective_id=collective_id, has_side_effects=True, vmem_limit_bytes=24 * 2**20),
        name="start_exchange",
    )(tokens, codes, taps, *weights)


def states_exchange(heads, count, per_block, backward, value, logs, out, scratch):
    packed, got, ready, send, recv, bsend, brecv = scratch
    me = lax.axis_index("seq") * heads + lax.axis_index("head")
    part = value.shape[0] // count
    tail = packed.shape[1] - part

    def peer(p):
        return {"seq": p // heads, "head": p % heads}

    def each(act):
        def one(d, carry):
            act((me + d) % count)
            return carry

        lax.fori_loop(1, count, one, 0)

    def greet():
        barrier = pltpu.get_barrier_semaphore()
        each(lambda p: pl.semaphore_signal(barrier, 1, device_id=peer(p), device_id_type=MESH))

    def pack():
        high = logs[...].astype(bf16)
        low = (logs[...] - high.astype(f32)).astype(bf16)

        def one(p, carry):
            packed[p, pl.ds(0, part)] = value[pl.ds(pl.multiple_of(p * part, part), part)]
            return carry

        lax.fori_loop(0, count, one, 0)
        parts_each = count * per_block // value.shape[0]
        zeros = jnp.zeros((tail - 2, high.shape[1]), bf16)
        for b in range(logs.shape[0]):
            both = jnp.concatenate([high[b : b + 1], low[b : b + 1], zeros], axis=0)
            for i in range(parts_each):
                packed[b * parts_each + i, pl.ds(part, tail)] = both
        got[me] = packed[me]

    def there(p, to):
        return pltpu.make_async_remote_copy(
            packed.at[p], got.at[to], send.at[p], recv.at[to], device_id=peer(p), device_id_type=MESH)

    def back(p, to):
        return pltpu.make_async_remote_copy(
            ready.at[p], out.at[pl.ds(pl.multiple_of(to * part, part), part)], bsend.at[p], brecv.at[to],
            device_id=peer(p), device_id_type=MESH)

    def begin():
        each(lambda p: there(p, me).start())

    def add_up():
        def step(i, state):
            p = count - 1 - i if backward else i

            @pl.when(p != me)
            def _():
                there(p, p).wait_recv()

            ready[p] = state.astype(bf16)

            @pl.when(p != me)
            def _():
                back(p, me).start()

            decay = jnp.exp(got[p, pl.ds(part, 1)].astype(f32) + got[p, pl.ds(part + 1, 1)].astype(f32))
            return decay * state + got[p, pl.ds(0, part)].astype(f32)

        lax.fori_loop(0, count, step, jnp.zeros((part, value.shape[1]), f32))
        out[pl.ds(pl.multiple_of(me * part, part), part)] = ready[me]

    def end():
        each(lambda p: back(p, p).wait_recv())
        each(lambda p: there(p, me).wait_send())
        each(lambda p: back(p, me).wait_send())

    return greet, pack, begin, add_up, end


def states_scratch(count, rows, width):
    part, tail = rows // count, 16
    dma = pltpu.SemaphoreType.DMA
    return [
        pltpu.VMEM((count, part + tail, width), bf16),
        pltpu.VMEM((count, part + tail, width), bf16),
        pltpu.VMEM((count, part, width), bf16),
        dma((count,)), dma((count,)), dma((count,)), dma((count,)),
    ]


def exchange_body(count, heads, per_block, items, n_more, *refs):
    value, logs = refs[:2]
    out = refs[2 + n_more]
    gathered = refs[3 + n_more : 3 + 2 * n_more]
    *scratch, gsend, grecv = refs[3 + 2 * n_more :]
    _, seq_copies = over_seq(items, gathered, gsend, grecv, lax.axis_index("seq"), lax.axis_index("head"))
    greet, pack, begin, add_up, end = states_exchange(heads, count, per_block, False, value, logs, out, scratch)
    greet()
    pack()
    pl.semaphore_wait(pltpu.get_barrier_semaphore(), count - 1)
    begin()
    for i in range(len(items)):
        for copy in seq_copies(i, 1):
            copy.start()
    add_up()
    for i in range(len(items)):
        for copy in seq_copies(i, 1):
            copy.wait_recv()
        for copy in seq_copies(i, 2):
            copy.start()
    end()
    for i in range(len(items)):
        for copy in seq_copies(i, 2):
            copy.wait()
        for copy in seq_copies(i, 1):
            copy.wait_send()


def exchange(value, logs, collective_id, items, gathered):
    heads = lax.axis_size("head")
    count = lax.axis_size("seq") * heads
    rows, width = value.shape
    more = len(gathered)
    dma = pltpu.SemaphoreType.DMA
    far, near = pl.BlockSpec(memory_space=pltpu.HBM), pl.BlockSpec(memory_space=pltpu.VMEM)
    return pl.pallas_call(
        partial(exchange_body, count, heads, rows // logs.shape[0], items, more),
        out_shape=[jax.ShapeDtypeStruct((rows, width), bf16)]
        + [jax.ShapeDtypeStruct(a.shape, a.dtype) for a in gathered],
        in_specs=[near] * 2 + [far] * more,
        out_specs=[near] + [far] * more,
        input_output_aliases={2 + i: 1 + i for i in range(more)},
        scratch_shapes=states_scratch(count, rows, width) + [dma((len(items), 3, 3)), dma((len(items), 3, 3))],
        compiler_params=pltpu.CompilerParams(
            collective_id=collective_id, has_side_effects=True, vmem_limit_bytes=16 * 2**20),
        name="exchange_states",
    )(value, logs, *gathered)


def aligned(x, size):
    return x if isinstance(x, int) else pl.multiple_of(x, size)


def sums_body(seq, plan, sources, shapes, n_given, n_left, n_right, lead, states, *refs):
    heads = 4
    nz = 1
    seq_masks = [1 << k for k in range(seq.bit_length() - 1)]
    split, joined = seq_masks[:3], seq_masks[3:]
    ns, nj = len(split), len(joined)
    refs = list(refs)

    def take(n):
        taken = refs[:n]
        del refs[:n]
        return taken

    value, logs = take(2) if states else (None, None)
    (act,) = take(1)
    given, lefts, rights = take(n_given), take(n_left), take(n_right)
    (new_state,) = take(1) if states else (None,)
    (act_full,) = take(1)
    (halos,) = take(1) if lead else (None,)
    n_arrays, count = len(sources), len(plan)
    outs = take(n_arrays)
    per = ns + nj + nz
    owns = take(count)
    recvs = [take(per) for _ in range(count)]
    staged = {c: take(1)[0] for c in range(count) if not isinstance(sources[plan[c][0]], int)}
    state_scratch = take(7) if states else None
    (load_sem, send_sem, recv_sem, jsend, jrecv, zsend, zrecv, gsend, grecv, keep_sem, asend, arecv, stay, hsend,
     hrecv) = refs
    s, z = lax.axis_index("seq"), lax.axis_index("head")

    def peer(to_s, to_z):
        return {"seq": to_s, "head": to_z}

    def remote(src, dst, send, recv, to_s, to_z):
        return pltpu.make_async_remote_copy(src, dst, send, recv, device_id=peer(to_s, to_z), device_id_type=MESH)

    seqs, rows_here, _ = act.shape
    mine = rows_here - lead
    width = act_full.shape[2]

    def features(q):
        return pl.ds(aligned(q * width, width), width)

    def rows_to(q):
        return pl.ds(aligned(q * mine, mine), mine)

    def back_copy(d, waits):
        q = (z + d) % heads
        to, of = (z, q) if waits else (q, z)
        return remote(
            act.at[:, pl.ds(lead, mine), features(to)], act_full.at[:, rows_to(of)], asend.at[q], arecv.at[of], s, q)

    def stay_copy():
        return pltpu.make_async_copy(
            act.at[:, pl.ds(lead, mine), features(z)], act_full.at[:, rows_to(z)], stay.at[0])

    def halo_copy(to_s, q, to, of):
        return remote(act.at[:, pl.ds(0, lead), features(to)], halos.at[of], hsend.at[q], hrecv.at[of], to_s, q)

    def halo_own():
        return pltpu.make_async_copy(act.at[:, pl.ds(0, lead), features(z)], halos.at[z], stay.at[1])

    def to_features(first):
        stay_copy().start() if first else stay_copy().wait()
        for d in range(1, heads):
            back_copy(d, False).start() if first else back_copy(d, False).wait_send()
            if not first:
                back_copy(d, True).wait_recv()
        if not lead:
            return

        @pl.when(z != 0)
        def _():
            halo_own().start() if first else halo_own().wait()
            for d in range(1, heads):
                q = (z + d) % heads
                halo_copy(s, q, q, z).start() if first else halo_copy(s, q, q, z).wait_send()

        @pl.when((z == 0) & (s > 0))
        def _():
            for q in range(heads):
                halo_copy(s - 1, q, q, 0).start() if first else halo_copy(s - 1, q, q, 0).wait_send()

        if not first:
            for d in range(1, heads):
                q = (z + d) % heads

                @pl.when(q != 0)
                def _():
                    halo_copy(s, q, z, q).wait_recv()

            @pl.when(s < seq - 1)
            def _():
                halo_copy(s + 1, 0, z, 0).wait_recv()

    def masks(c):
        return split[:1] + (split[1:] if c % 2 == 0 else split[:0:-1])

    def bit(c, k):
        return s // masks(c)[k] % 2

    def extent(c):
        array, axis, first, size = plan[c]
        return size if axis == 0 else shapes[array][1]

    def kept(c, k):
        size = extent(c)
        return sum((bit(c, j) * (size >> (j + 1)) for j in range(1, k + 1)), 0)

    def cut(c, begin, size):
        part = pl.ds(aligned(begin, size), size)
        return (part, slice(None)) if plan[c][1] == 0 else (slice(None), part)

    def in_array(c, begin, size):
        _, axis, first, rows = plan[c]
        if axis == 0:
            return pl.ds(aligned(first + begin, size), size), slice(None)
        return pl.ds(first, rows), pl.ds(aligned(begin, size), size)

    def load(c):
        half = extent(c) // 2
        rows, columns = in_array(c, bit(c, 0) * half, half)
        return pltpu.make_async_copy(given[sources[plan[c][0]]].at[:, rows, columns], owns[c], load_sem.at[c])

    def product(c):
        left_at, right_at, natural = sources[plan[c][0]]
        left, right = lefts[left_at], rights[right_at]
        half = extent(c) // 2

        def one(q, carry):
            for to, b in ((staged[c], 1 - bit(c, 0)), (owns[c], bit(c, 0))):
                rows, columns = in_array(c, b * half, half)
                total = None
                for i in range(left.shape[1]):
                    b_ = right[q if right.shape[0] > 1 else 0, i, :, columns]
                    if natural:
                        term = dot_tn(left[q if left.shape[0] > 1 else 0, i, :, rows], b_)
                    else:
                        term = dot_nn(left[q if left.shape[0] > 1 else 0, i, rows, :], b_)
                    total = term if total is None else total + term
                to[q] = total.astype(bf16)
            return carry

        lax.fori_loop(0, heads, one, 0)

    def seq_copy(c, k):
        half = extent(c) >> (k + 1)
        other = (1 - bit(c, k)) * half
        if k == 0 and c in staged:
            source = staged[c]
        elif k == 0:
            rows, columns = in_array(c, other, half)
            source = given[sources[plan[c][0]]].at[:, rows, columns]
        else:
            rows, columns = cut(c, kept(c, k - 1) + other, half)
            source = owns[c].at[:, rows, columns]
        return remote(source, recvs[c][k], send_sem.at[c, k], recv_sem.at[c, k], flipped(s, masks(c)[k]), z)

    def final(c):
        return cut(c, kept(c, ns - 1), extent(c) >> ns)

    def joined_copy(c, k):
        rows, columns = final(c)
        return remote(
            owns[c].at[:, rows, columns], recvs[c][ns + k], jsend.at[c, k], jrecv.at[c, k], flipped(s, joined[k]), z)

    def head_copy(c, d, waits):
        rows, columns = final(c)
        q = (z + d) % heads
        to, of = (z, q) if waits else (q, z)
        return remote(
            owns[c].at[to, rows, columns], recvs[c][ns + nj].at[of], zsend.at[c, q], zrecv.at[c, of], s, q)

    def add(c, k):
        axis, rows = plan[c][1], plan[c][3]
        if k < ns:
            begin, size = kept(c, k), extent(c) >> (k + 1)
        else:
            begin, size = kept(c, ns - 1), extent(c) >> ns
        received = recvs[c][k]
        tall = size if axis == 0 else rows
        wide = shapes[plan[c][0]][1] if axis == 0 else size
        tile = tall
        while tile * wide > 98304 and tile % 32 == 0:
            tile //= 2
        tiles = tall // tile

        def places(r):
            there = pl.ds(pl.multiple_of(r, tile), tile)
            if axis == 0:
                return there, pl.ds(pl.multiple_of(begin + r, tile), tile), slice(None)
            return there, there, pl.ds(aligned(begin, size), size)

        def one(t, carry):
            i = t // tiles
            there, here, columns = places(t % tiles * tile)
            owns[c][i, here, columns] = owns[c][i, here, columns] + received[i, there]
            return carry

        def last_one(t, carry):
            there, here, columns = places(t * tile)
            total = owns[c][z, here, columns].astype(f32)
            for d in range(1, heads):
                total = total + received[(z + d) % heads, there].astype(f32)
            owns[c][z, here, columns] = total.astype(bf16)
            return carry

        if k < ns + nj:
            lax.fori_loop(0, heads * tiles, one, 0)
        else:
            lax.fori_loop(0, tiles, last_one, 0)

    def held(c, level):
        size = extent(c)
        return in_array(c, sum(bit(c, j) * (size >> (j + 1)) for j in range(level)), size >> level)

    def keep(c):
        rows, columns = final(c)
        to_rows, to_columns = held(c, ns)
        return pltpu.make_async_copy(
            owns[c].at[z, rows, columns], outs[plan[c][0]].at[to_rows, to_columns], keep_sem.at[c])

    def gather_copy(c, j):
        level = ns - j
        rows, columns = held(c, level)
        array = outs[plan[c][0]].at[rows, columns]
        source = owns[c].at[z, *final(c)] if j == 0 else array
        return remote(source, array, gsend.at[c, j], grecv.at[c, j], flipped(s, masks(c)[level - 1]), z)

    barrier = pltpu.get_barrier_semaphore()
    if states:
        everyone = seq * heads
        greet, pack, begin, add_up, end = states_exchange(
            heads, everyone, value.shape[0] // logs.shape[0], True, value, logs, new_state, state_scratch)
        greet()
        pack()
        pl.semaphore_wait(barrier, everyone - 1)
        begin()
    else:

        def greet(to_s, to_z):
            pl.semaphore_signal(barrier, 1, device_id=peer(to_s, to_z), device_id_type=MESH)

        for mask in seq_masks:
            greet(flipped(s, mask), z)
        for d in range(1, heads):
            greet(s, (z + d) % heads)
        greeted = len(seq_masks) + heads - 1

        @pl.when(s < seq - 1)
        def _():
            greet(s + 1, 0)

        @pl.when((z == 0) & (s > 0))
        def _():
            pl.semaphore_wait(barrier, greeted + heads)

        @pl.when((z != 0) | (s == 0))
        def _():
            pl.semaphore_wait(barrier, greeted)

    last = per + ns

    def copies(c, k, waits=False):
        if k < ns:
            return [seq_copy(c, k)]
        if k < ns + nj:
            return [joined_copy(c, k - ns)]
        if k < per:
            return [head_copy(c, d, waits) for d in range(1, heads)]
        return [gather_copy(c, k - per)]

    def advance(c, k):
        if k == 0 and c not in staged:
            load(c).wait()
        if k == per:
            keep(c).wait()
        for copy in copies(c, k, True):
            copy.wait_recv()
        if ns <= k < ns + nj:
            joined_copy(c, k - ns).wait_send()
        if k < per:
            add(c, k)
        if k + 1 == per:
            keep(c).start()
        if k + 1 < last:
            for copy in copies(c, k + 1):
                copy.start()

    def begin_chunk(c):
        if c in staged:
            product(c)
        else:
            load(c).start()
        seq_copy(c, 0).start()

    pairs = count // 2
    for t in range(pairs + last):
        for k in reversed(range(last)):
            p = t - 1 - k
            if 0 <= p < pairs:
                advance(2 * p, k)
                advance(2 * p + 1, k)
        if t < pairs:
            begin_chunk(2 * t)
            begin_chunk(2 * t + 1)
        if t == 0:
            to_features(True)
        if t == 1 and states:
            add_up()
    to_features(False)
    for c in range(count):
        for k in range(last):
            if not ns <= k < ns + nj:
                for copy in copies(c, k):
                    copy.wait_send()
    if states:
        end()


def sums(act, lead, plan, sources, shapes, given, lefts, rights, collective_id, states=()):
    seq, heads = lax.axis_size("seq"), lax.axis_size("head")
    nj = max(0, seq.bit_length() - 4)
    ns = 3
    seqs, rows_here, features = act.shape
    width = features // heads
    owns, recvs, staged = [], [], []
    for a, axis, first, rows in plan:
        columns = shapes[a][1]
        cut = lambda k: (rows >> k, columns) if axis == 0 else (rows, columns >> k)
        owns.append(pltpu.VMEM((heads, *cut(1)), bf16))
        recvs += [pltpu.VMEM((heads, *cut(k + 1)), bf16) for k in range(ns)]
        recvs += [pltpu.VMEM((heads, *cut(ns)), bf16) for k in range(nj)]
        recvs.append(pltpu.VMEM((heads, *cut(ns)), bf16))
        if not isinstance(sources[a], int):
            staged.append(pltpu.VMEM((heads, *cut(1)), bf16))
    count = len(plan)
    dma = pltpu.SemaphoreType.DMA
    sems = [
        dma((count,)), dma((count, ns)), dma((count, ns)), dma((count, max(nj, 1))), dma((count, max(nj, 1))),
        dma((count, heads)), dma((count, heads)), dma((count, ns)), dma((count, ns)), dma((count,)),
        dma((heads,)), dma((heads,)), dma((2,)), dma((heads,)), dma((heads,)),
    ]
    anywhere, near = pl.BlockSpec(memory_space=pl.ANY), pl.BlockSpec(memory_space=pltpu.VMEM)
    out_shape = [jax.ShapeDtypeStruct((seqs, heads * (rows_here - lead), width), bf16)]
    if lead:
        out_shape += [jax.ShapeDtypeStruct((heads, seqs, lead, width), bf16)]
    out_shape += [jax.ShapeDtypeStruct(shape, bf16) for shape in shapes]
    out_specs = [anywhere] * len(out_shape)
    state_scratch = []
    if states:
        out_shape.insert(0, jax.ShapeDtypeStruct(states[0].shape, bf16))
        out_specs.insert(0, near)
        state_scratch = states_scratch(seq * heads, *states[0].shape)
    return pl.pallas_call(
        partial(sums_body, seq, plan, sources, shapes, len(given), len(lefts), len(rights), lead, bool(states)),
        out_shape=out_shape,
        in_specs=[near] * len(states) + [anywhere] * (1 + len(given)) + [near] * (len(lefts) + len(rights)),
        out_specs=out_specs,
        scratch_shapes=owns + recvs + staged + state_scratch + sems,
        compiler_params=pltpu.CompilerParams(
            collective_id=collective_id, has_side_effects=True, vmem_limit_bytes=60 * 2**20),
        name="sum_gradients",
    )(*states, act, *given, *lefts, *rights)


def dot_nt(a, b):
    return lax.dot_general(a, b, (((1,), (1,)), ((), ())), preferred_element_type=f32)


def dot_tn(a, b):
    return lax.dot_general(a, b, (((0,), (0,)), ((), ())), preferred_element_type=f32)


def mlp_body(per_head, hid, gain, cot, w_gate, w_up, w_low, lay, d_hid, normed, hidden, d_gate, d_up, d_gain, acc, part, dx):
    step = pl.program_id(0)

    @pl.when(step == 0)
    def _():
        values = hid[...]
        normed[...] = (values * row_scale(values) * gain[...]).astype(bf16)
        acc[...] = values
        dx[...] = jnp.zeros_like(dx)

    g = dot_nt(w_gate[0], normed[...])
    u = dot_nt(w_up[0], normed[...])
    dh = rounded(dot_nt(w_low[0], cot[...]))
    logistic = jax.nn.sigmoid(g)
    act = g * logistic
    h = (act * u).astype(bf16)
    dg = (dh * u * (logistic * (1.0 + g * (1.0 - logistic)))).astype(bf16)
    du = (dh * act).astype(bf16)
    hidden[0] = h
    d_gate[0] = dg
    d_up[0] = du
    term = dot_tn(h, w_low[0])
    first = step % per_head == 0

    @pl.when(first)
    def _():
        part[...] = term

    @pl.when(jnp.logical_not(first))
    def _():
        part[...] += term

    @pl.when(step % per_head == per_head - 1)
    def _():
        acc[...] += rounded(part[...])

    dx[...] += dot_tn(dg, w_gate[0]) + dot_tn(du, w_up[0])

    @pl.when(step == pl.num_programs(0) - 1)
    def _():
        lay[...] = acc[...].astype(bf16)
        values, upstream = hid[...], dx[...]
        scale = row_scale(values)
        d_gain[...] = jnp.sum(upstream * values * scale, axis=0, keepdims=True)
        d_hid[...] = cot[...].astype(f32) + norm_back(values, scale, gain[...], upstream)


def mlp(hidden_in, gain, upstream, w_gate, w_up, w_low):
    tokens, width = hidden_in.shape
    heads, units, _ = w_gate.shape
    per_head = 2
    block = units // per_head
    weights = pl.BlockSpec((1, block, width), lambda i: (i // per_head, i % per_head, 0))
    units_out = pl.BlockSpec((1, block, tokens), lambda i: (i // per_head, i % per_head, 0))
    all_of = lambda *shape: pl.BlockSpec(shape, lambda i: (0, 0))
    units_shape = jax.ShapeDtypeStruct((heads, units, tokens), bf16)
    token_shape = lambda kind: jax.ShapeDtypeStruct((tokens, width), kind)
    return pl.pallas_call(
        partial(mlp_body, per_head),
        grid=(heads * per_head,),
        in_specs=[all_of(tokens, width), all_of(1, width), all_of(tokens, width), weights, weights, weights],
        out_specs=[all_of(tokens, width)] * 3 + [units_out] * 3 + [all_of(1, width)],
        out_shape=[token_shape(bf16), token_shape(f32), token_shape(bf16)]
        + [units_shape] * 3
        + [jax.ShapeDtypeStruct((1, width), f32)],
        scratch_shapes=[pltpu.VMEM((tokens, width), f32)] * 3,
        compiler_params=pltpu.CompilerParams(vmem_limit_bytes=56 * 2**20),
        name="feed_forward",
    )(hidden_in, gain.reshape(1, width), upstream, w_gate, w_up, w_low)


def rows_after(values, count):
    if count == 0:
        return values
    return jnp.concatenate([values[count:], jnp.zeros((count, values.shape[1]), values.dtype)], axis=0)


def short_conv(pre, taps, rows):
    lead = HALO - taps.shape[0] + 1
    return sum(taps[j : j + 1] * pre[lead + j : lead + j + rows] for j in range(taps.shape[0]))


def spans(values):
    return [values[n * SPAN : (n + 1) * SPAN] for n in range(values.shape[0] // SPAN)]


def lower(count):
    row = lax.broadcasted_iota(jnp.int32, (count, count), 0)
    column = lax.broadcasted_iota(jnp.int32, (count, count), 1)
    return row, column


def causal_scores(left, right):
    row, column = lower(SPAN)
    return jnp.where(row >= column, dot_nt(left, right), 0.0).astype(bf16)


def dot_nn(a, b):
    return jnp.dot(a, b, preferred_element_type=f32)


def without_first(values, first):
    row = lax.broadcasted_iota(jnp.int32, values.shape, 0)
    return jnp.where((row < HALO) & (first > 0), 0.0, values.astype(f32))


def forward_one_body(first, tokens, gain, w, taps, codes, normed, pre, q_exp, k_exp, k_end, value, decay, starts, ends, logs, kept):
    h, i = pl.program_id(0), pl.program_id(1)

    @pl.when(h == 0)
    def _():
        values = without_first(tokens[0], first[0])
        kept[i] = (values * row_scale(values) * gain[...]).astype(bf16)

    normed[0] = kept[i]
    projected = dot_nn(kept[i], w[0]).astype(bf16)
    pre[0, 0] = projected
    rows = codes.shape[1]
    key = codes.shape[2]
    wide = taps.shape[2]
    act = jax.nn.silu(short_conv(projected[:, :wide].astype(f32), taps[0], rows))
    whole_codes = codes[0].astype(jnp.int32)
    high = whole_codes // 128
    row, column = lower(rows)
    within = ((row >= column) & (row // SPAN == column // SPAN)).astype(bf16)
    total = 128.0 * dot_nn(within, high.astype(bf16)) + dot_nn(within, (whole_codes - 128 * high).astype(bf16))
    log = total * -decay_unit
    decay[0, 0] = log
    grow = jnp.exp(log)
    q_exp[0, 0] = (act[:, :key] * key**-0.5 * grow).astype(bf16)
    k_exp[0, 0] = (act[:, key : 2 * key] * jnp.exp(-log)).astype(bf16)
    value[0, 0] = act[:, 2 * key :].astype(bf16)
    state = jnp.zeros((wide - 2 * key, key), f32)
    sums_log = jnp.zeros((1, key), f32)
    for n, part in enumerate(spans(log)):
        at = pl.ds(n * SPAN, SPAN)
        last = part[SPAN - 1 :]
        k_end[0, 0, at] = (act[n * SPAN : (n + 1) * SPAN, key : 2 * key] * jnp.exp(last - part)).astype(bf16)
        starts[0, 0, n] = state.astype(bf16)
        state = jnp.exp(last) * state + dot_tn(value[0, 0, at], k_end[0, 0, at])
        sums_log = sums_log + last
    ends[0, 0] = state.astype(bf16)
    logs[0, 0] = sums_log


def forward_one(first, tokens, gain, w, taps, codes):
    heads, width, columns = w.shape
    seqs, tall, _ = tokens.shape
    rows = tall - HALO
    tap_count, wide = taps.shape[1:]
    key = codes.shape[2] // heads
    wide_value = wide - 2 * key
    blocks = rows // SPAN
    per = lambda *shape: pl.BlockSpec((1, 1, *shape), lambda h, i: (h, i) + (0,) * len(shape))
    shape = lambda kind, *rest: jax.ShapeDtypeStruct((heads, seqs, *rest), kind)
    return pl.pallas_call(
        forward_one_body,
        grid=(heads, seqs),
        in_specs=[
            pl.BlockSpec(memory_space=pltpu.SMEM),
            pl.BlockSpec((1, tall, width), lambda h, i: (i, 0, 0)),
            pl.BlockSpec((1, width), lambda h, i: (0, 0)),
            pl.BlockSpec((1, width, columns), lambda h, i: (h, 0, 0)),
            pl.BlockSpec((1, tap_count, wide), lambda h, i: (h, 0, 0)),
            pl.BlockSpec((1, rows, key), lambda h, i: (i, 0, h)),
        ],
        out_specs=[
            pl.BlockSpec((1, tall, width), lambda h, i: (i, 0, 0)),
            per(tall, columns), per(rows, key), per(rows, key), per(rows, key), per(rows, wide_value), per(rows, key),
            per(blocks, wide_value, key), per(wide_value, key), per(1, key),
        ],
        out_shape=[
            jax.ShapeDtypeStruct((seqs, tall, width), bf16),
            shape(bf16, tall, columns), shape(bf16, rows, key), shape(bf16, rows, key), shape(bf16, rows, key),
            shape(bf16, rows, wide_value), shape(f32, rows, key), shape(bf16, blocks, wide_value, key),
            shape(bf16, wide_value, key), shape(f32, 1, key),
        ],
        scratch_shapes=[pltpu.VMEM((seqs, tall, width), bf16)],
        compiler_params=pltpu.CompilerParams(vmem_limit_bytes=48 * 2**20),
        name="attention_spans",
    )(first, tokens, gain.reshape(1, -1), w, taps, codes)


def forward_two_body(first, tokens, pre, q_exp, k_exp, value, decay, starts, incoming, out_gain, w_out, core, states, gated, hidden_in):
    h = pl.program_id(1)
    wide_value = value.shape[3]
    carry = jnp.ones((1, q_exp.shape[3]), f32)
    entering = incoming[0, 0].astype(f32)
    parts = []
    for n in range(starts.shape[2]):
        at = pl.ds(n * SPAN, SPAN)
        state = (starts[0, 0, n].astype(f32) + carry * entering).astype(bf16)
        states[0, 0, n] = state
        q = q_exp[0, 0, at]
        scores = causal_scores(q, k_exp[0, 0, at])
        parts.append(dot_nn(scores, value[0, 0, at]) + dot_nt(q, state))
        carry = carry * jnp.exp(decay[0, 0, pl.ds((n + 1) * SPAN - 1, 1)])
    out = jnp.concatenate(parts, axis=0)
    core[0, 0] = out
    gate = pre[0, 0, pl.ds(HALO, out.shape[0]), pl.ds(pre.shape[3] - wide_value, wide_value)].astype(f32)
    gated[0, 0] = (out * row_scale(out) * out_gain[...] * jax.nn.silu(gate)).astype(bf16)
    term = rounded(dot_nn(gated[0, 0], w_out[0]))

    @pl.when(h == 0)
    def _():
        hidden_in[0] = without_first(tokens[0], first[0])[HALO:] + term

    @pl.when(h > 0)
    def _():
        hidden_in[0] += term


def head_spec(*shape):
    return pl.BlockSpec((1, 1, *shape), lambda i, h: (h, i) + (0,) * len(shape))


def forward_two(first, tokens, pre, q_exp, k_exp, value, decay, starts, incoming, out_gain, w_out):
    heads, seqs, rows, key = q_exp.shape
    wide_value, width = w_out.shape[1:]
    blocks = rows // SPAN
    tall = rows + HALO
    per = head_spec
    shape = lambda kind, *rest: jax.ShapeDtypeStruct((heads, seqs, *rest), kind)
    return pl.pallas_call(
        forward_two_body,
        grid=(seqs, heads),
        in_specs=[
            pl.BlockSpec(memory_space=pltpu.SMEM),
            pl.BlockSpec((1, tall, width), lambda i, h: (i, 0, 0)),
            per(tall, pre.shape[3]), per(rows, key), per(rows, key), per(rows, wide_value), per(rows, key),
            per(blocks, wide_value, key), per(wide_value, key),
            pl.BlockSpec((1, wide_value), lambda i, h: (0, 0)),
            pl.BlockSpec((1, wide_value, width), lambda i, h: (h, 0, 0)),
        ],
        out_specs=[
            per(rows, wide_value), per(blocks, wide_value, key), per(rows, wide_value),
            pl.BlockSpec((1, rows, width), lambda i, h: (i, 0, 0)),
        ],
        out_shape=[
            shape(f32, rows, wide_value), shape(bf16, blocks, wide_value, key), shape(bf16, rows, wide_value),
            jax.ShapeDtypeStruct((seqs, rows, width), f32),
        ],
        compiler_params=pltpu.CompilerParams(vmem_limit_bytes=48 * 2**20),
        name="attention_outputs",
    )(first, tokens, pre, q_exp, k_exp, value, decay, starts, incoming, out_gain.reshape(1, -1), w_out)


def backward_one_body(d_hidden_in, w_out, core, pre, out_gain, q_exp, decay, d_mixer, d_core, d_gate, d_states, own_grad, d_gain):
    i, h = pl.program_id(0), pl.program_id(1)
    wide_value = core.shape[3]

    @pl.when(h == 0)
    def _():
        d_mixer[0] = d_hidden_in[0].astype(bf16)

    d_gated = rounded(dot_nt(d_mixer[0], w_out[0]))
    out = core[0, 0]
    gate = pre[0, 0, pl.ds(HALO, out.shape[0]), pl.ds(pre.shape[3] - wide_value, wide_value)].astype(f32)
    scale = row_scale(out)
    normed = out * scale
    d_normed = d_gated * jax.nn.silu(gate)
    d_gate[0, 0] = (d_gated * normed * out_gain[...] * silu_slope(gate)).astype(bf16)
    gain_term = jnp.sum(d_normed * normed, axis=0, keepdims=True)

    @pl.when((i == 0) & (h == 0))
    def _():
        d_gain[...] = gain_term

    @pl.when((i > 0) | (h > 0))
    def _():
        d_gain[...] += gain_term

    d_core[0, 0] = norm_back(out, scale, out_gain[...], d_normed).astype(bf16)
    carry = jnp.ones((1, q_exp.shape[3]), f32)
    total = jnp.zeros((wide_value, q_exp.shape[3]), f32)
    for n in range(out.shape[0] // SPAN):
        at = pl.ds(n * SPAN, SPAN)
        term = dot_tn(d_core[0, 0, at], q_exp[0, 0, at])
        d_states[0, 0, n] = term.astype(bf16)
        total = total + carry * term
        carry = carry * jnp.exp(decay[0, 0, pl.ds((n + 1) * SPAN - 1, 1)])
    own_grad[0, 0] = total.astype(bf16)


def backward_one(d_hidden_in, w_out, core, pre, out_gain, q_exp, decay):
    heads, seqs, rows, key = q_exp.shape
    wide_value, width = w_out.shape[1:]
    blocks = rows // SPAN
    per = head_spec
    shape = lambda kind, *rest: jax.ShapeDtypeStruct((heads, seqs, *rest), kind)
    by_seq = pl.BlockSpec((1, rows, width), lambda i, h: (i, 0, 0))
    gain = pl.BlockSpec((1, wide_value), lambda i, h: (0, 0))
    return pl.pallas_call(
        backward_one_body,
        grid=(seqs, heads),
        in_specs=[
            by_seq, pl.BlockSpec((1, wide_value, width), lambda i, h: (h, 0, 0)), per(rows, wide_value),
            per(rows + HALO, pre.shape[3]), gain, per(rows, key), per(rows, key),
        ],
        out_specs=[
            by_seq, per(rows, wide_value), per(rows, wide_value), per(blocks, wide_value, key), per(wide_value, key),
            gain,
        ],
        out_shape=[
            jax.ShapeDtypeStruct((seqs, rows, width), bf16), shape(bf16, rows, wide_value),
            shape(bf16, rows, wide_value), shape(bf16, blocks, wide_value, key), shape(bf16, wide_value, key),
            jax.ShapeDtypeStruct((1, wide_value), f32),
        ],
        compiler_params=pltpu.CompilerParams(vmem_limit_bytes=48 * 2**20),
        name="attention_outputs_back",
    )(d_hidden_in, w_out, core, pre, out_gain.reshape(1, -1), q_exp, decay)


def backward_two_body(
    first, tokens, gain, d_hidden_in, w, taps, pre, q_exp, k_exp, k_end, value, decay, states, d_core, d_states, leaving,
    d_gate, d_projected, d_tokens, d_taps, d_gain, d_normed,
):
    i, h = pl.program_id(0), pl.program_id(1)
    key, wide_value = q_exp.shape[3], value.shape[3]
    rows = q_exp.shape[2]
    blocks = rows // SPAN
    scale = key**-0.5
    d_end = leaving[0, 0].astype(f32)
    pieces = [None] * blocks
    for n in reversed(range(blocks)):
        at = pl.ds(n * SPAN, SPAN)
        q, k, v, dc = q_exp[0, 0, at], k_exp[0, 0, at], value[0, 0, at], d_core[0, 0, at]
        log = decay[0, 0, at]
        last = log[SPAN - 1 :]
        d_end_low = d_end.astype(bf16)
        scores = causal_scores(q, k)
        d_scores = causal_scores(dc, v)
        d_query = (dot_nn(d_scores, k) + dot_nn(dc, states[0, 0, n])) * (scale * jnp.exp(log))
        d_key = dot_tn(d_scores, q) * jnp.exp(-log) + dot_nn(v, d_end_low) * jnp.exp(last - log)
        d_value = dot_tn(scores, dc) + dot_nt(k_end[0, 0, at], d_end_low)
        pieces[n] = jnp.concatenate([d_query, d_key, d_value], axis=1)
        d_end = jnp.exp(last) * d_end + d_states[0, 0, n].astype(f32)
    d_act = jnp.concatenate(pieces, axis=0)
    tap_count, wide = taps.shape[1:]
    ext = pre[0, 0, :, pl.ds(0, wide)].astype(f32)
    d_conv = d_act * silu_slope(short_conv(ext, taps[0], rows))
    lead = HALO - tap_count + 1
    padded = jnp.concatenate([jnp.zeros((HALO, wide), f32), d_conv], axis=0)
    d_ext = jnp.zeros((HALO + rows, wide), f32)
    tap_terms = []
    for j in range(tap_count):
        moved = rows_after(padded, tap_count - 1 - j)
        d_ext = d_ext + taps[0, pl.ds(j, 1)] * moved
        tap_terms.append(jnp.sum(moved * ext, axis=0, keepdims=True))
    tap_terms = jnp.concatenate(tap_terms, axis=0)

    @pl.when(i == 0)
    def _():
        d_taps[h] = tap_terms

    @pl.when(i > 0)
    def _():
        d_taps[h] += tap_terms

    d_gate_ext = jnp.concatenate([jnp.zeros((HALO, wide_value), bf16), d_gate[0, 0]], axis=0)
    d_projected[0, 0] = jnp.concatenate([d_ext.astype(bf16), d_gate_ext], axis=1)
    term = dot_nt(d_projected[0, 0], w[0])

    @pl.when(h == 0)
    def _():
        d_normed[...] = term

    @pl.when(h > 0)
    def _():
        d_normed[...] += term

    @pl.when(h == pl.num_programs(1) - 1)
    def _():
        values, upstream = without_first(tokens[0], first[0]), d_normed[...]
        inverse = row_scale(values)
        gain_term = jnp.sum(upstream * values * inverse, axis=0, keepdims=True)
        d_gain[0] = gain_term
        back = norm_back(values, inverse, gain[...], upstream)
        d_tokens[0, pl.ds(0, HALO)] = back[:HALO].astype(bf16)
        d_tokens[0, pl.ds(HALO, rows)] = (back[HALO:] + d_hidden_in[0]).astype(bf16)


def backward_two(
    first, tokens, gain, d_hidden_in, w, taps, pre, q_exp, k_exp, k_end, value, decay, states, d_core, d_states, leaving, d_gate
):
    heads, seqs, rows, key = q_exp.shape
    width, columns = w.shape[1:]
    wide_value = value.shape[3]
    tap_count, wide = taps.shape[1:]
    blocks = rows // SPAN
    tall = rows + HALO
    per = head_spec
    by_seq = lambda n: pl.BlockSpec((1, n, width), lambda i, h: (i, 0, 0))
    return pl.pallas_call(
        backward_two_body,
        grid=(seqs, heads),
        in_specs=[
            pl.BlockSpec(memory_space=pltpu.SMEM), by_seq(tall), pl.BlockSpec((1, width), lambda i, h: (0, 0)),
            by_seq(rows), pl.BlockSpec((1, width, columns), lambda i, h: (h, 0, 0)),
            pl.BlockSpec((1, tap_count, wide), lambda i, h: (h, 0, 0)),
            per(tall, columns), per(rows, key), per(rows, key), per(rows, key), per(rows, wide_value), per(rows, key),
            per(blocks, wide_value, key), per(rows, wide_value), per(blocks, wide_value, key), per(wide_value, key),
            per(rows, wide_value),
        ],
        out_specs=[
            per(tall, columns), by_seq(tall), pl.BlockSpec((heads, tap_count, wide), lambda i, h: (0, 0, 0)), by_seq(1),
        ],
        out_shape=[
            jax.ShapeDtypeStruct((heads, seqs, tall, columns), bf16),
            jax.ShapeDtypeStruct((seqs, tall, width), bf16),
            jax.ShapeDtypeStruct((heads, tap_count, wide), f32),
            jax.ShapeDtypeStruct((seqs, 1, width), f32),
        ],
        scratch_shapes=[pltpu.VMEM((tall, width), f32)],
        compiler_params=pltpu.CompilerParams(vmem_limit_bytes=48 * 2**20),
        name="attention_spans_back",
    )(
        first, tokens, gain.reshape(1, -1), d_hidden_in, w, taps, pre, q_exp, k_exp, k_end, value, decay, states, d_core,
        d_states, leaving, d_gate,
    )


def chunks(array, rows, count):
    return [(array, 0, i * (rows // count), rows // count) for i in range(count)]


def local(
    tokens,
    decay_codes,
    cotangent,
    attn_gain,
    w_query,
    w_key,
    w_value,
    w_out_gate,
    conv_query,
    conv_key,
    conv_value,
    out_gain,
    w_out,
    mlp_gain,
    w_gate,
    w_up,
    w_down,
):
    seqs, rows, own_width = tokens.shape
    heads = lax.axis_size("head")
    place = lax.axis_index("seq") * heads + lax.axis_index("head")
    mine = rows // heads
    width = own_width * heads
    key_width = w_query.shape[1]
    value_width = w_value.shape[1]
    conv_width = 2 * key_width + value_width
    mixer_width = conv_width + value_width

    half, ff = width // 2, w_gate.shape[1]
    out_half, ff_half = w_out.shape[0] // 2, ff // 2
    items = [(0, 0, 0, 0, 0, width, 0, key_width), (1, 1, 0, 0, 0, width, key_width, key_width)]
    items += [(i, 2, 0, 0, i * half, half, 2 * key_width, value_width) for i in range(2)]
    items += [(i, 3, 0, 0, i * half, half, conv_width, value_width) for i in range(2)]
    items += [(i, 4, 1, 0, i * out_half, out_half, 0, width) for i in range(2)]
    pair = [(2 + 2 * a + i, 5 + a, 2 + a, 1, i * ff_half, ff_half, 0, width) for a in range(2) for i in range(2)]
    tokens_ext, codes, taps, w_mixer, w_proj, w_gate_all, w_up_all = start_all(
        tokens,
        decay_codes.astype(jnp.int16),
        jnp.concatenate([conv_query, conv_key, conv_value], axis=1),
        (w_query, w_key, w_value, w_out_gate, w_out, w_gate.T, w_up.T),
        items + pair,
        [3] * len(items) + [1] * len(pair),
        ((width, mixer_width), w_out.shape, w_down.shape, w_down.shape),
        1,
    )
    upstream, low_part, codes = lax.optimization_barrier((cotangent, w_down, codes))
    upstream = lax.all_to_all(upstream, "head", 1, 2, tiled=True)
    w_low = whole(low_part)

    first = (place == 0).astype(jnp.int32).reshape(1)
    normed, pre, q_exp, k_exp, k_end, value, decay, starts, local_end, log_total = forward_one(
        first, tokens_ext, attn_gain, w_mixer, taps, codes
    )
    flat = (-1, key_width)
    log_total = log_total.reshape(flat)
    pair = [(item[0], 0, item[2] - 2, *item[3:]) for item in pair]
    incoming, w_gate_all, w_up_all = exchange(
        local_end.reshape(flat), log_total, 2, pair, (w_gate_all, w_up_all)
    )
    core, states, gated, hidden_in = forward_two(
        first, tokens_ext, pre, q_exp, k_exp, value, decay, starts, incoming.reshape(local_end.shape), out_gain, w_proj
    )
    layer_out, d_hidden_in, normed_two, hidden, d_gate, d_up, grad_mlp_gain = mlp(
        hidden_in.reshape(-1, width), mlp_gain, upstream.reshape(-1, width), w_gate_all, w_up_all, w_low
    )
    d_hidden_in = d_hidden_in.reshape(hidden_in.shape)
    layer_out = layer_out.reshape(hidden_in.shape)
    d_mixer, d_core, d_gate_rows, d_states, own_grad, grad_out_gain = backward_one(
        d_hidden_in, w_proj, core, pre, out_gain, q_exp, decay
    )
    ff_part = ff // 4
    ff_plan = [(a, 1, i * ff_part, ff_part) for a in range(3) for i in range(4)]
    leaving, layer_out, grad_gate, grad_up, grad_down = sums(
        layer_out,
        0,
        ff_plan,
        [(0, 0, False), (1, 0, False), (2, 1, False)],
        [w_down.shape] * 3,
        (),
        [a[:, None] for a in (d_gate, d_up, hidden)],
        [normed_two[None, None], upstream.reshape(1, 1, -1, width)],
        3,
        (own_grad.reshape(flat), log_total),
    )
    d_projected, tokens_grad, grad_taps, grad_attn_gain = backward_two(
        first, tokens_ext, attn_gain, d_hidden_in, w_mixer, taps, pre, q_exp, k_exp, k_end, value, decay, states, d_core,
        d_states, leaving.reshape(local_end.shape), d_gate_rows,
    )

    small = jnp.concatenate(
        [
            jnp.sum(grad_attn_gain, axis=0).reshape(heads, -1),
            grad_mlp_gain.reshape(heads, -1),
            jnp.broadcast_to(grad_out_gain, (heads, value_width)),
            grad_taps.reshape(heads, -1),
        ],
        axis=1,
    )
    small_rows = 256
    lanes = -(-small.shape[1] // (small_rows * 128)) * 128
    small = jnp.pad(small, ((0, 0), (0, small_rows * lanes - small.shape[1]))).reshape(heads, small_rows, lanes)
    mixer_plan = chunks(0, width, 4) + [(1, 1, i * out_half, out_half) for i in range(2)] + chunks(2, small_rows, 2)
    tokens_grad, halos, grad_mixer, grad_out, small = sums(
        tokens_grad,
        HALO,
        mixer_plan,
        [(0, 0, True), (1, 1, True), 0],
        [(width, mixer_width), w_out.shape, small.shape[1:]],
        [small.astype(bf16)],
        [normed[None], gated],
        [d_projected, d_mixer[None]],
        4,
    )
    grad_gate, grad_up, grad_down, grad_out, grad_mixer, small = (
        a.astype(f32) for a in (grad_gate, grad_up, grad_down, grad_out, grad_mixer, small)
    )
    layer_out = layer_out.astype(f32)
    last = lax.axis_index("seq") == lax.axis_size("seq") - 1
    halos = jnp.where(last & (jnp.arange(heads) == 0)[:, None, None, None], 0, halos).astype(f32)
    halos = jnp.moveaxis(jnp.roll(halos, -1, axis=0), 0, 1)
    halos = jnp.pad(halos, ((0, 0), (0, 0), (mine - HALO, 0), (0, 0))).reshape(tokens_grad.shape)
    tokens_grad = tokens_grad.astype(f32) + halos
    small = small.reshape(-1)
    at = 2 * own_width + value_width
    grad_taps = small[at : at + taps[0].size].reshape(taps.shape[1:])
    return (
        layer_out,
        tokens_grad,
        small[:own_width],
        grad_mixer[:, :key_width],
        grad_mixer[:, key_width : 2 * key_width],
        grad_mixer[:, 2 * key_width : conv_width],
        grad_mixer[:, conv_width:],
        grad_taps[:, :key_width],
        grad_taps[:, key_width : 2 * key_width],
        grad_taps[:, 2 * key_width :],
        small[2 * own_width : at],
        grad_out,
        small[own_width : 2 * own_width],
        grad_gate.T,
        grad_up.T,
        grad_down,
    )


def solution(mesh):
    in_specs = (
        P(None, "seq", "head"),
        P(None, "seq", "head"),
        P(None, "seq", "head"),
        P(),
        P(None, "head"),
        P(None, "head"),
        P(None, "head"),
        P(None, "head"),
        P(None, "head"),
        P(None, "head"),
        P(None, "head"),
        P(),
        P("head", None),
        P(),
        P(None, "head"),
        P(None, "head"),
        P("head", None),
    )
    out_specs = (
        P(None, "seq", "head"),
        P(None, "seq", "head"),
        P("head"),
        P(None, "head"),
        P(None, "head"),
        P(None, "head"),
        P(None, "head"),
        P(None, "head"),
        P(None, "head"),
        P(None, "head"),
        P(),
        P("head", None),
        P("head"),
        P(None, "head"),
        P(None, "head"),
        P("head", None),
    )
    return jax.shard_map(local, mesh=mesh, in_specs=in_specs, out_specs=out_specs, check_vma=False)
```

time: 592 us -> 549 us (0.927)
  Pallas kernels: 368 us -> 464 us
  matrix products: 89 us -> 0 us
  other arithmetic: 53.1 us -> 14 us
    pallas_call x1 -> x7, Pallas kernels: 173 us -> 309 us  [the longest x2 213 us: sums(): pl.pallas_call(partial(sums_body, seq, plan, sources, shapes, len(given),...]
    dot_general x29 -> x0, matrix products: 89 us -> none  [the longest x27 87 us: dot(): jnp.einsum(spec, left.astype(bf16), right.astype(bf16), preferred_element...]
    pallas_call x2 -> x1, Pallas kernels: 84.2 us -> 62.9 us  [exchange(): pl.pallas_call(partial(exchange_body, count, heads, rows // logs.shape[0]...]
    pallas_call x1, Pallas kernels: 111 us -> 92.4 us  [start_all(): pl.pallas_call(partial(start_body, seq, len(weights), items, steps), out_...]
    convert_element_type x10 -> x0, other arithmetic: 11.4 us -> none  [the longest x1 3.3 us: local(): tokens_grad.astype(bf16)]
    mul x3 -> x0, other arithmetic: 11.1 us -> none  [the longest x1 6.98 us: local(): taps[:, j, None, None, :] * d_conv]
    another operation x3 -> x2, other arithmetic: 7.5 us -> 0.73 us
    unnamed x177 -> x103, local copies, waits for them, and re-layouts: 37.2 us -> 36.9 us
  transfers between devices with their start and end apart: 2 -> 2, of which waited for: 0 -> 0; matrix products, arithmetic and copies ran while one was open for 8% -> 2% of each run, Pallas kernels for 28% -> 16%
where the time goes in v5:
time: 549 us; the launch traced here: 548 us
  Pallas kernels  464 us (85%)
  local copies, waits for them, and re-layouts  51 us (9%)
  between operations  14.4 us (3%)
  other arithmetic  14 us (3%)
    pallas_call x2, Pallas kernels, sums(): pl.pallas_call(partial(sums_body, seq, plan, sources, shapes, len(given),...  213 us
    pallas_call x1, Pallas kernels, start_all(): pl.pallas_call(partial(start_body, seq, len(weights), items, steps), out_...  92.4 us
    pallas_call x1, Pallas kernels, exchange(): pl.pallas_call(partial(exchange_body, count, heads, rows // logs.shape[0]...  62.9 us
    unnamed x103, local copies, waits for them, and re-layouts  36.9 us
    pallas_call x1, Pallas kernels, mlp(): pl.pallas_call(partial(mlp_body, per_head), grid=(heads * per_head,), in_...  36.9 us
    pallas_call x1, Pallas kernels, backward_two(): pl.pallas_call(backward_two_body, grid=(seqs, heads), in_specs=[pl.BlockS...  21 us
    pallas_call x1, Pallas kernels, forward_one(): pl.pallas_call(forward_one_body, grid=(heads, seqs), in_specs=[pl.BlockSp...  14 us
    pallas_call x1, Pallas kernels, forward_two(): pl.pallas_call(forward_two_body, grid=(seqs, heads), in_specs=[pl.BlockSp...  12.8 us
  transfers between devices with their start and end apart: 2, of which 0 were waited for; matrix products, arithmetic and copies ran while one was open for 2% of the time, Pallas kernels for 16%

profile of v5, /device:TPU:1, one launch (start us, length us, event | category | flops | bytes accessed | tf_op | source)
XLA Modules:
  0.0 547.8 jit_solution(17542031356323717421)
XLA Ops:
  7.3 1.4 convert_element_type.36.refs_1_
  9.4 1.4 copy-done.18
  10.8 1.2 copy-done.20
  13.1 1.0 copy-done.27
  17.0 92.4 %start_exchange.1 = (bf16[2,272,1024]{2,1,0:T(8,128)(2,1)S(1)}, s16[2,256,512]{2,1,0:T(8,128)(2,1)S(1)}, f32[4,4,512]{2,1,0:T(4,128)S(1)}, bf16[4,1024,768]{2,1,...) custom-call(bf16[2,1024,256]{2,1,0:T(8,128)(2,1)S(1)} %copy-done.20,, ...), custom_call_target="tpu_custom_call" | custom-call | tf_op jit(solution)/shard_map/start_exchange/pallas_call | solution.py:300
  109.4 2.7 copy-done.2
  112.1 2.4 copy-done.3
  114.5 2.5 copy-done.5
  118.0 1.3 copy-done.12
  120.8 3.4 copy.38
  124.2 4.4 all-to-all-start
  129.7 14.0 %attention_spans.1 = (bf16[2,272,1024]{2,1,0:T(8,128)(2,1)S(1)}, bf16[4,2,272,768]{3,2,1,0:T(8,128)(2,1)}, bf16[4,2,256,128]{3,2,1,0:T(8,128)(2,1)S(1)}, bf16[4,...) custom-call(s32[1]{0:T(128)} %bitcast.first, ...), custom_call_target="tpu_custom_call" | custom-call | tf_op jit(solution)/shard_map/attention_spans/pallas_call | solution.py:986
  144.7 3.7 copy-done.6
  148.4 62.9 %exchange_states.1 = (bf16[2048,128]{1,0:T(8,128)(2,1)S(1)}, bf16[4,704,1024]{2,1,0:T(8,128)(2,1)S(1)}, bf16[4,704,1024]{2,1,0:T(8,128)(2,1)S(1)}) custom-call(bf16[2048,128]{1,0:T(8,128)(2,1)S(1)} %bitcast.58, f32[8,128]{1,0:T(8,128)S(1)} %bitcast.60, bf16[4,704,1024]{2,1,0:T(8,128)(2,1)S(1)} %bitcast.51, ...), custom_call_target="tpu_custom_call", output_to_operand_aliasing={{1}: (2, {}), {2}: (3, {})} | custom-call | tf_op jit(solution)/shard_map/exchange_states/pallas_call | solution.py:439
  211.4 2.4 copy-done.7
  213.8 12.8 %attention_outputs.1 = (f32[4,2,256,256]{3,2,1,0:T(8,128)}, bf16[4,2,4,256,128]{4,3,2,1,0:T(8,128)(2,1)}, bf16[4,2,256,256]{3,2,1,0:T(8,128)(2,1)S(1)}, f32[2,256,1024]{2,1,0:T(8,128)}) custom-call(s32[1]{0:T(128)} %bitcast.first, bf16[2,272,1024]{2,1,0:T(8,128)(2,1)S(1)} %copy-done.9, bf16[4,2,272,768]{3,2,1,0:T(8,128)(2,1)} %get-tuple-element.75.pre, ...), custom_call_target="tpu_custom_call" | custom-call | tf_op jit(solution)/shard_map/attention_outputs/pallas_call | solution.py:1054
  227.7 2.0 copy.49
  229.7 1.6 reshape.131.refs_7_
  231.3 1.2 copy.42
  232.5 36.9 %feed_forward.1 = (bf16[512,1024]{1,0:T(8,128)(2,1)}, f32[512,1024]{1,0:T(8,128)}, bf16[512,1024]{1,0:T(8,128)(2,1)}, bf16[4,704,512]{2,1,0:T(8,128)(2,1)}, bf16...) custom-call(f32[512,1024]{1,0:T(8,128)} %bitcast.75, f32[1,1024]{1,0:T(1,128)} %bitcast.80, ...), custom_call_target="tpu_custom_call" | custom-call | tf_op jit(solution)/shard_map/feed_forward/pallas_call | solution.py:888
  270.1 11.4 %attention_outputs_back.1 = (bf16[2,256,1024]{2,1,0:T(8,128)(2,1)S(1)}, bf16[4,2,256,256]{3,2,1,0:T(8,128)(2,1)S(1)}, bf16[4,2,256,256]{3,2,1,0:T(8,128)(2,1)S(1...) custom-call(f32[2,256,1024]{2,1,0:T(8,128)} %bitcast.68, ...), custom_call_target="tpu_custom_call" | custom-call | tf_op jit(solution)/shard_map/attention_outputs_back/pallas_call | solution.py:1123
  285.3 136.3 %sum_gradients.2 = (bf16[2048,128]{1,0:T(8,128)(2,1)}, bf16[2,1024,256]{2,1,0:T(8,128)(2,1)}, bf16[704,1024]{1,0:T(8,128)(2,1)}, bf16[704,1024]{1,0:T(8,128)(2,1)}, bf16[704,1024]{1,0:T(8,128)(2,1)}) custom-call(bf16[2048,128]{1,0:T(8,128)(2,1)} %bitcast.57, f32[8,128]{1,0:T(8,128)} %bitcast.61, bf16[2,256,1024]{2,1,0:T(8,128)(2,1)} %bitcast.77, ...), custom_call_target="tpu_custom_call" | custom-call | tf_op jit(solution)/shard_map/sum_gradients/pallas_call | solution.py:811
  421.6 1.2 copy-done.24
  423.9 21.0 %attention_spans_back.1 = (bf16[4,2,272,768]{3,2,1,0:T(8,128)(2,1)}, bf16[2,272,1024]{2,1,0:T(8,128)(2,1)}, f32[4,4,512]{2,1,0:T(4,128)S(1)}, f32[2,1,1024]{2,1,0:T(1,128)S(1)}) custom-call(s32[1]{0:T(128)} %bitcast.first, bf16[2,272,1024]{2,1,0:T(8,128)(2,1)} %copy-done.8, f32[1,1024]{1,0:T(1,128)S(1)} %bitcast.63, f32[2,256,1024]{2,1,0:T(8,128)} %bitcast.69, ...), custom_call_target="tpu_custom_call" | custom-call | tf_op jit(solution)/shard_map/attention_spans_back/pallas_call | solution.py:1224
  445.8 76.4 %sum_gradients.3 = (bf16[2,1024,256]{2,1,0:T(8,128)(2,1)}, bf16[4,2,16,256]{3,2,1,0:T(8,128)(2,1)}, bf16[1024,768]{1,0:T(8,128)(2,1)}, bf16[256,1024]{1,0:T(8,128)(2,1)}, bf16[256,128]{1,0:T(8,128)(2,1)}) custom-call(bf16[2,272,1024]{2,1,0:T(8,128)(2,1)} %get-tuple-element.107.refs_0_, bf16[4,256,128]{2,1,0:T(8,128)(2,1)} %bitcast.76, ...), custom_call_target="tpu_custom_call" | custom-call | tf_op jit(solution)/shard_map/sum_gradients/pallas_call | solution.py:811
  526.0 2.1 fusion.1
  528.1 1.5 fusion
  530.2 1.1 convert_element_type.43
  531.3 1.5 convert_element_type.37
  533.3 1.9 convert_element_type.44
  535.2 1.5 bitcast_add_fusion
  537.8 3.2 convert_bitcast_fusion
  (119 shorter events, 22.7 us)
Async XLA Ops:
  7.2 112.9 %copy-start = (bf16[704,1024]{1,0:T(8,128)(2,1)S(1)}, bf16[704,1024]{1,0:T(8,128)(2,1)}, u32[]{:S(2)}) copy-start(bf16[704,1024]{1,0:T(8,128)(2,1)} %param.33) | copy-start | bytes 4325380
  7.2 2.2 copy-start.17
  7.2 225.3 %all-gather.2.cloned.1.call-start = ((), (), s32[]{:S(2)}) async-start(), calls=%async_computation.1 | async-start | bytes 5947392 | tf_op jit(solution)/shard_map/all_gather | solution.py:43
  109.4 2.7 copy-start.2
  112.1 2.4 copy-start.3
  114.5 2.5 copy-start.5
  120.8 7.9 %copy-start.38 = (f32[1024]{0:T(1024)S(1)}, f32[1024]{0:T(1024)}, u32[]{:S(2)}) copy-start(f32[1024]{0:T(1024)} %param.20) | copy-start | bytes 12292
  120.8 23.9 %slice-start = ((s8[5767168]{0:T(1024)(128)(4,1)}), s8[1572864]{0:T(1024)(128)(4,1)S(1)}, s32[]{:S(2)}) async-start(s8[5767168]{0:T(1024)(128)(4,1)} %bitcast.50), calls=%async_computation.2 | async-start | bytes 3145728
  124.2 103.5 %all-to-all-start = ((bf16[2,1024,256]{2,0,1:T(2,128)(2,1)}), bf16[2,1024,256]{2,0,1:T(2,128)(2,1)}, u32[]{:S(2)}, u32[]{:S(2)}) async-start(bf16[2,1024,256]{2,0,1:T(2,128)(2,1)} %copy.38), calls=%async_computation | async-start | bytes 2097152 | tf_op jit(solution)/shard_map/all_to_all | solution.py:1304
  129.7 15.0 %slice-start.1 = ((s8[5767168]{0:T(1024)(128)(4,1)}), s8[4194304]{0:T(1024)(128)(4,1)S(1)}, s32[]{:S(2)}) async-start(s8[5767168]{0:T(1024)(128)(4,1)} %bitcast.50), calls=%async_computation.3 | async-start | bytes 8388608
  144.6 66.7 %copy-start.29 = (bf16[4,2,256,128]{3,2,1,0:T(8,128)(2,1)}, bf16[4,2,256,128]{3,2,1,0:T(8,128)(2,1)S(1)}, u32[]{:S(2)}) copy-start(bf16[4,2,256,128]{3,2,1,0:T(8,128)(2,1)S(1)} %get-tuple-element.101.k_end) | copy-start | bytes 1572868
  144.6 66.7 %copy-start.37 = (f32[4,2,1,128]{3,2,1,0:T(1,128)}, f32[4,2,1,128]{3,2,1,0:T(1,128)S(1)}, u32[]{:S(2)}) copy-start(f32[4,2,1,128]{3,2,1,0:T(1,128)S(1)} %get-tuple-element.82) | copy-start | bytes 12292
  144.7 69.2 %copy-start.10 = (f32[4,2,256,128]{3,2,1,0:T(8,128)}, f32[4,2,256,128]{3,2,1,0:T(8,128)S(1)}, u32[]{:S(2)}) copy-start(f32[4,2,256,128]{3,2,1,0:T(8,128)S(1)} %get-tuple-element.79.decay) | copy-start | bytes 3145732
  144.7 69.2 %copy-start.13 = (bf16[4,2,256,256]{3,2,1,0:T(8,128)(2,1)}, bf16[4,2,256,256]{3,2,1,0:T(8,128)(2,1)S(1)}, u32[]{:S(2)}) copy-start(bf16[4,2,256,256]{3,2,1,0:T(8,128)(2,1)S(1)} %get-tuple-element.78.value) | copy-start | bytes 3145732
  144.7 69.2 %copy-start.15 = (bf16[4,2,256,128]{3,2,1,0:T(8,128)(2,1)}, bf16[4,2,256,128]{3,2,1,0:T(8,128)(2,1)S(1)}, u32[]{:S(2)}) copy-start(bf16[4,2,256,128]{3,2,1,0:T(8,128)(2,1)S(1)} %get-tuple-element.77.k_exp) | copy-start | bytes 1572868
  144.7 3.7 copy-start.6
  148.4 65.4 %copy-start.9 = (bf16[2,272,1024]{2,1,0:T(8,128)(2,1)S(1)}, bf16[2,272,1024]{2,1,0:T(8,128)(2,1)}, u32[]{:S(2)}) copy-start(bf16[2,272,1024]{2,1,0:T(8,128)(2,1)} %copy-done.8) | copy-start | bytes 3342340
  148.4 65.4 %copy-start.39 = (f32[256]{0:T(256)S(1)}, f32[256]{0:T(256)}, u32[]{:S(2)}) copy-start(f32[256]{0:T(256)} %param.28) | copy-start | bytes 3076
  211.4 2.5 copy-start.7
  213.8 12.8 %copy-start.4 = (bf16[4,704,1024]{2,1,0:T(8,128)(2,1)}, bf16[4,704,1024]{2,1,0:T(8,128)(2,1)S(1)}, u32[]{:S(2)}) copy-start(bf16[4,704,1024]{2,1,0:T(8,128)(2,1)S(1)} %get-tuple-element.89.w_gate) | copy-start | bytes 17301508
  232.5 37.6 %copy-start.11 = (f32[4,2,256,128]{3,2,1,0:T(8,128)S(1)}, f32[4,2,256,128]{3,2,1,0:T(8,128)}, u32[]{:S(2)}) copy-start(f32[4,2,256,128]{3,2,1,0:T(8,128)} %copy-done.10) | copy-start | bytes 3145732
  285.3 136.3 %copy-start.14 = (bf16[4,2,256,256]{3,2,1,0:T(8,128)(2,1)S(1)}, bf16[4,2,256,256]{3,2,1,0:T(8,128)(2,1)}, u32[]{:S(2)}) copy-start(bf16[4,2,256,256]{3,2,1,0:T(8,128)(2,1)} %copy-done.13) | copy-start | bytes 3145732
  285.3 136.3 %copy-start.16 = (bf16[4,2,256,128]{3,2,1,0:T(8,128)(2,1)S(1)}, bf16[4,2,256,128]{3,2,1,0:T(8,128)(2,1)}, u32[]{:S(2)}) copy-start(bf16[4,2,256,128]{3,2,1,0:T(8,128)(2,1)} %copy-done.15) | copy-start | bytes 1572868
  285.3 136.3 %copy-start.30 = (bf16[4,2,256,128]{3,2,1,0:T(8,128)(2,1)S(1)}, bf16[4,2,256,128]{3,2,1,0:T(8,128)(2,1)}, u32[]{:S(2)}) copy-start(bf16[4,2,256,128]{3,2,1,0:T(8,128)(2,1)} %copy-done.29) | copy-start | bytes 1572868
  522.2 5.9 %copy-start.40 = (bf16[1024,768]{1,0:T(8,128)(2,1)S(1)}, bf16[1024,768]{1,0:T(8,128)(2,1)}, u32[]{:S(2)}) copy-start(bf16[1024,768]{1,0:T(8,128)(2,1)} %get-tuple-element.119) | copy-start | bytes 4718596
  528.1 2.1 copy-start.46
  529.6 1.7 copy-start.44
  531.3 2.0 copy-start.41
  533.3 1.9 copy-start.45
  535.2 1.8 copy-start.42
  535.2 2.6 copy-start.43
  537.8 3.2 copy-start.1
  (19 other events, 19.7 us)
Sparse Core Ops, SparseCore 0:
  120.9 98.2 all-gather.1

commit v6 on v5

--- a/solution.py
+++ b/solution.py
@@ -308,7 +308,7 @@
             dma((count,)), dma((count,)), dma((count, 2)), dma((count, 2)), dma((count, 3, 3)), dma((count, 3, 3)),
         ],
         compiler_params=pltpu.CompilerParams(
-            collective_id=collective_id, has_side_effects=True, vmem_limit_bytes=24 * 2**20),
+            collective_id=collective_id, has_side_effects=True, vmem_limit_bytes=60 * 2**20),
         name="start_exchange",
     )(tokens, codes, taps, *weights)
 
@@ -445,7 +445,7 @@
         input_output_aliases={2 + i: 1 + i for i in range(more)},
         scratch_shapes=states_scratch(count, rows, width) + [dma((len(items), 3, 3)), dma((len(items), 3, 3))],
         compiler_params=pltpu.CompilerParams(
-            collective_id=collective_id, has_side_effects=True, vmem_limit_bytes=16 * 2**20),
+            collective_id=collective_id, has_side_effects=True, vmem_limit_bytes=60 * 2**20),
         name="exchange_states",
     )(value, logs, *gathered)
 
@@ -454,7 +454,7 @@
     return x if isinstance(x, int) else pl.multiple_of(x, size)
 
 
-def sums_body(seq, plan, sources, shapes, n_given, n_left, n_right, lead, states, *refs):
+def sums_body(seq, plan, sources, shapes, n_given, n_left, n_right, leads, states, spread, more, groups, *refs):
     heads = 4
     nz = 1
     seq_masks = [1 << k for k in range(seq.bit_length() - 1)]
@@ -468,13 +468,16 @@
         return taken
 
     value, logs = take(2) if states else (None, None)
-    (act,) = take(1)
+    acts = take(len(leads))
+    n_arrays, count = len(sources), len(plan)
+    blocks = take(len(shapes) - n_arrays)
+    orders = [c % 2 for c in range(count)] + [item[4] for item in more]
+    plan = [*plan, *(item[:4] for item in more)]
     given, lefts, rights = take(n_given), take(n_left), take(n_right)
     (new_state,) = take(1) if states else (None,)
-    (act_full,) = take(1)
-    (halos,) = take(1) if lead else (None,)
-    n_arrays, count = len(sources), len(plan)
-    outs = take(n_arrays)
+    acts_full = take(len(leads))
+    halos = take(sum(map(bool, leads)))
+    outs = take(len(shapes))
     per = ns + nj + nz
     owns = take(count)
     recvs = [take(per) for _ in range(count)]
@@ -490,34 +493,29 @@
     def remote(src, dst, send, recv, to_s, to_z):
         return pltpu.make_async_remote_copy(src, dst, send, recv, device_id=peer(to_s, to_z), device_id_type=MESH)
 
-    seqs, rows_here, _ = act.shape
-    mine = rows_here - lead
-    width = act_full.shape[2]
-
-    def features(q):
-        return pl.ds(aligned(q * width, width), width)
-
-    def rows_to(q):
-        return pl.ds(aligned(q * mine, mine), mine)
-
-    def back_copy(d, waits):
-        q = (z + d) % heads
-        to, of = (z, q) if waits else (q, z)
-        return remote(
-            act.at[:, pl.ds(lead, mine), features(to)], act_full.at[:, rows_to(of)], asend.at[q], arecv.at[of], s, q)
-
-    def stay_copy():
-        return pltpu.make_async_copy(
-            act.at[:, pl.ds(lead, mine), features(z)], act_full.at[:, rows_to(z)], stay.at[0])
-
-    def halo_copy(to_s, q, to, of):
-        return remote(act.at[:, pl.ds(0, lead), features(to)], halos.at[of], hsend.at[q], hrecv.at[of], to_s, q)
-
-    def halo_own():
-        return pltpu.make_async_copy(act.at[:, pl.ds(0, lead), features(z)], halos.at[z], stay.at[1])
-
-    def to_features(first):
-        stay_copy().start() if first else stay_copy().wait()
+    def to_features(a, first):
+        act, full, lead = acts[a], acts_full[a], leads[a]
+        mine, width = act.shape[1] - lead, full.shape[2]
+
+        def features(q):
+            return pl.ds(aligned(q * width, width), width)
+
+        def rows_to(q):
+            return pl.ds(aligned(q * mine, mine), mine)
+
+        def back_copy(d, waits):
+            q = (z + d) % heads
+            to, of = (z, q) if waits else (q, z)
+            return remote(
+                act.at[:, pl.ds(lead, mine), features(to)], full.at[:, rows_to(of)], asend.at[a, q], arecv.at[a, of], s, q)
+
+        def halo_copy(to_s, q, to, of):
+            return remote(
+                act.at[:, pl.ds(0, lead), features(to)], halos[0].at[of], hsend.at[q], hrecv.at[of], to_s, q)
+
+        stay_copy = pltpu.make_async_copy(
+            act.at[:, pl.ds(lead, mine), features(z)], full.at[:, rows_to(z)], stay.at[a])
+        stay_copy.start() if first else stay_copy.wait()
         for d in range(1, heads):
             back_copy(d, False).start() if first else back_copy(d, False).wait_send()
             if not first:
@@ -527,7 +525,8 @@
 
         @pl.when(z != 0)
         def _():
-            halo_own().start() if first else halo_own().wait()
+            halo_own = pltpu.make_async_copy(act.at[:, pl.ds(0, lead), features(z)], halos[0].at[z], stay.at[len(acts)])
+            halo_own.start() if first else halo_own.wait()
             for d in range(1, heads):
                 q = (z + d) % heads
                 halo_copy(s, q, q, z).start() if first else halo_copy(s, q, q, z).wait_send()
@@ -550,7 +549,7 @@
                 halo_copy(s + 1, 0, z, 0).wait_recv()
 
     def masks(c):
-        return split[:1] + (split[1:] if c % 2 == 0 else split[:0:-1])
+        return split[:1] + (split[1:] if orders[c] == 0 else split[:0:-1])
 
     def bit(c, k):
         return s // masks(c)[k] % 2
@@ -670,17 +669,22 @@
         size = extent(c)
         return in_array(c, sum(bit(c, j) * (size >> (j + 1)) for j in range(level)), size >> level)
 
+    def own_block(c):
+        if c >= count:
+            return blocks[plan[c][0] - n_arrays].at[pl.ds(plan[c][2], plan[c][3])]
+        return owns[c].at[z, *final(c)]
+
     def keep(c):
-        rows, columns = final(c)
-        to_rows, to_columns = held(c, ns)
-        return pltpu.make_async_copy(
-            owns[c].at[z, rows, columns], outs[plan[c][0]].at[to_rows, to_columns], keep_sem.at[c])
+        rows, columns = held(c, ns)
+        if not spread:
+            columns = slice(None)
+        return pltpu.make_async_copy(own_block(c), outs[plan[c][0]].at[rows, columns], keep_sem.at[c])
 
     def gather_copy(c, j):
         level = ns - j
         rows, columns = held(c, level)
         array = outs[plan[c][0]].at[rows, columns]
-        source = owns[c].at[z, *final(c)] if j == 0 else array
+        source = own_block(c) if j == 0 else array
         return remote(source, array, gsend.at[c, j], grecv.at[c, j], flipped(s, masks(c)[level - 1]), z)
 
     barrier = pltpu.get_barrier_semaphore()
@@ -715,7 +719,7 @@
         def _():
             pl.semaphore_wait(barrier, greeted)
 
-    last = per + ns
+    last = per + (ns if spread else 1)
 
     def copies(c, k, waits=False):
         if k < ns:
@@ -724,7 +728,7 @@
             return [joined_copy(c, k - ns)]
         if k < per:
             return [head_copy(c, d, waits) for d in range(1, heads)]
-        return [gather_copy(c, k - per)]
+        return [gather_copy(c, k - per)] if spread else []
 
     def advance(c, k):
         if k == 0 and c not in staged:
@@ -739,7 +743,7 @@
             add(c, k)
         if k + 1 == per:
             keep(c).start()
-        if k + 1 < last:
+        if k + 1 < last and c < count:
             for copy in copies(c, k + 1):
                 copy.start()
 
@@ -750,36 +754,45 @@
             load(c).start()
         seq_copy(c, 0).start()
 
-    pairs = count // 2
-    for t in range(pairs + last):
-        for k in reversed(range(last)):
-            p = t - 1 - k
-            if 0 <= p < pairs:
-                advance(2 * p, k)
-                advance(2 * p + 1, k)
-        if t < pairs:
-            begin_chunk(2 * t)
-            begin_chunk(2 * t + 1)
+    for t in range(len(groups) + last):
+        for k in range(last):
+            if 0 <= t - 1 - k < len(groups):
+                for c in groups[t - 1 - k]:
+                    advance(c, k)
+        if t < len(groups):
+            for c in groups[t]:
+                begin_chunk(c)
+        for c in range(count, len(plan)):
+            if t == 0:
+                keep(c).start()
+            elif t <= ns:
+                advance(c, per + t - 1)
+            if t < ns:
+                gather_copy(c, t).start()
         if t == 0:
-            to_features(True)
+            for a in range(len(acts)):
+                to_features(a, True)
         if t == 1 and states:
             add_up()
-    to_features(False)
+    for a in range(len(acts)):
+        to_features(a, False)
     for c in range(count):
         for k in range(last):
             if not ns <= k < ns + nj:
                 for copy in copies(c, k):
                     copy.wait_send()
+    for c in range(count, len(plan)):
+        for j in range(ns):
+            gather_copy(c, j).wait_send()
     if states:
         end()
 
 
-def sums(act, lead, plan, sources, shapes, given, lefts, rights, collective_id, states=()):
+def sums(acts, leads, plan, sources, shapes, given, lefts, rights, collective_id, states=(), spread=True, blocks=(), more=(), groups=None):
+    groups = groups or [(c, c + 1) for c in range(0, len(plan), 2)]
     seq, heads = lax.axis_size("seq"), lax.axis_size("head")
     nj = max(0, seq.bit_length() - 4)
     ns = 3
-    seqs, rows_here, features = act.shape
-    width = features // heads
     owns, recvs, staged = [], [], []
     for a, axis, first, rows in plan:
         columns = shapes[a][1]
@@ -790,18 +803,25 @@
         recvs.append(pltpu.VMEM((heads, *cut(ns)), bf16))
         if not isinstance(sources[a], int):
             staged.append(pltpu.VMEM((heads, *cut(1)), bf16))
-    count = len(plan)
+    count, every = len(plan), len(plan) + len(more)
     dma = pltpu.SemaphoreType.DMA
     sems = [
         dma((count,)), dma((count, ns)), dma((count, ns)), dma((count, max(nj, 1))), dma((count, max(nj, 1))),
-        dma((count, heads)), dma((count, heads)), dma((count, ns)), dma((count, ns)), dma((count,)),
-        dma((heads,)), dma((heads,)), dma((2,)), dma((heads,)), dma((heads,)),
+        dma((count, heads)), dma((count, heads)), dma((every, ns)), dma((every, ns)), dma((every,)),
+        dma((2, heads)), dma((2, heads)), dma((3,)), dma((heads,)), dma((heads,)),
     ]
     anywhere, near = pl.BlockSpec(memory_space=pl.ANY), pl.BlockSpec(memory_space=pltpu.VMEM)
-    out_shape = [jax.ShapeDtypeStruct((seqs, heads * (rows_here - lead), width), bf16)]
-    if lead:
-        out_shape += [jax.ShapeDtypeStruct((heads, seqs, lead, width), bf16)]
-    out_shape += [jax.ShapeDtypeStruct(shape, bf16) for shape in shapes]
+    out_shape, halo_shape = [], []
+    for act, lead in zip(acts, leads):
+        seqs, rows_here, features = act.shape
+        width = features // heads
+        out_shape.append(jax.ShapeDtypeStruct((seqs, heads * (rows_here - lead), width), bf16))
+        if lead:
+            halo_shape.append(jax.ShapeDtypeStruct((heads, seqs, lead, width), bf16))
+    out_shape += halo_shape
+    if not spread:
+        shapes_out = [(rows, columns >> ns) for rows, columns in shapes]
+    out_shape += [jax.ShapeDtypeStruct(shape, bf16) for shape in (shapes if spread else shapes_out)]
     out_specs = [anywhere] * len(out_shape)
     state_scratch = []
     if states:
@@ -809,15 +829,19 @@
         out_specs.insert(0, near)
         state_scratch = states_scratch(seq * heads, *states[0].shape)
     return pl.pallas_call(
-        partial(sums_body, seq, plan, sources, shapes, len(given), len(lefts), len(rights), lead, bool(states)),
+        partial(sums_body, seq, plan, sources, shapes, len(given), len(lefts), len(rights), leads, bool(states), spread, more, groups),
         out_shape=out_shape,
-        in_specs=[near] * len(states) + [anywhere] * (1 + len(given)) + [near] * (len(lefts) + len(rights)),
+        in_specs=[near] * len(states)
+        + [anywhere] * len(acts)
+        + [near] * len(blocks)
+        + [anywhere] * len(given)
+        + [near] * (len(lefts) + len(rights)),
         out_specs=out_specs,
         scratch_shapes=owns + recvs + staged + state_scratch + sems,
         compiler_params=pltpu.CompilerParams(
             collective_id=collective_id, has_side_effects=True, vmem_limit_bytes=60 * 2**20),
         name="sum_gradients",
-    )(*states, act, *given, *lefts, *rights)
+    )(*states, *acts, *blocks, *given, *lefts, *rights)
 
 
 def dot_nt(a, b):
@@ -878,7 +902,7 @@
 def mlp(hidden_in, gain, upstream, w_gate, w_up, w_low):
     tokens, width = hidden_in.shape
     heads, units, _ = w_gate.shape
-    per_head = 2
+    per_head = 1
     block = units // per_head
     weights = pl.BlockSpec((1, block, width), lambda i: (i // per_head, i % per_head, 0))
     units_out = pl.BlockSpec((1, block, tokens), lambda i: (i // per_head, i % per_head, 0))
@@ -894,7 +918,7 @@
         + [units_shape] * 3
         + [jax.ShapeDtypeStruct((1, width), f32)],
         scratch_shapes=[pltpu.VMEM((tokens, width), f32)] * 3,
-        compiler_params=pltpu.CompilerParams(vmem_limit_bytes=56 * 2**20),
+        compiler_params=pltpu.CompilerParams(vmem_limit_bytes=60 * 2**20),
         name="feed_forward",
     )(hidden_in, gain.reshape(1, width), upstream, w_gate, w_up, w_low)
 
@@ -1006,7 +1030,7 @@
             shape(bf16, wide_value, key), shape(f32, 1, key),
         ],
         scratch_shapes=[pltpu.VMEM((seqs, tall, width), bf16)],
-        compiler_params=pltpu.CompilerParams(vmem_limit_bytes=48 * 2**20),
+        compiler_params=pltpu.CompilerParams(vmem_limit_bytes=60 * 2**20),
         name="attention_spans",
     )(first, tokens, gain.reshape(1, -1), w, taps, codes)
 
@@ -1070,7 +1094,7 @@
             shape(f32, rows, wide_value), shape(bf16, blocks, wide_value, key), shape(bf16, rows, wide_value),
             jax.ShapeDtypeStruct((seqs, rows, width), f32),
         ],
-        compiler_params=pltpu.CompilerParams(vmem_limit_bytes=48 * 2**20),
+        compiler_params=pltpu.CompilerParams(vmem_limit_bytes=60 * 2**20),
         name="attention_outputs",
     )(first, tokens, pre, q_exp, k_exp, value, decay, starts, incoming, out_gain.reshape(1, -1), w_out)
 
@@ -1136,7 +1160,7 @@
             shape(bf16, rows, wide_value), shape(bf16, blocks, wide_value, key), shape(bf16, wide_value, key),
             jax.ShapeDtypeStruct((1, wide_value), f32),
         ],
-        compiler_params=pltpu.CompilerParams(vmem_limit_bytes=48 * 2**20),
+        compiler_params=pltpu.CompilerParams(vmem_limit_bytes=60 * 2**20),
         name="attention_outputs_back",
     )(d_hidden_in, w_out, core, pre, out_gain.reshape(1, -1), q_exp, decay)
 
@@ -1242,12 +1266,67 @@
             jax.ShapeDtypeStruct((seqs, 1, width), f32),
         ],
         scratch_shapes=[pltpu.VMEM((tall, width), f32)],
-        compiler_params=pltpu.CompilerParams(vmem_limit_bytes=48 * 2**20),
+        compiler_params=pltpu.CompilerParams(vmem_limit_bytes=60 * 2**20),
         name="attention_spans_back",
     )(
         first, tokens, gain.reshape(1, -1), d_hidden_in, w, taps, pre, q_exp, k_exp, k_end, value, decay, states, d_core,
         d_states, leaving, d_gate,
     )
+
+
+def finalize_body(key, value, last, lay, tok, halo, mixer, out, gate, up, down, small, *outs):
+    step = pl.program_id(0)
+    o_lay, o_tok, o_query, o_key, o_value, o_gate_proj, o_out, o_gate, o_up, o_down, o_small = outs
+    o_lay[...] = lay[...].astype(f32)
+    o_tok[...] = tok[...].astype(f32)
+    steps = pl.num_programs(0)
+
+    @pl.when((step % 2 == 1) & ((step < steps - 1) | (last[0] == 0)))
+    def _():
+        at = pl.ds(tok.shape[1] - HALO, HALO)
+        o_tok[:, at] += halo[0].astype(f32)
+
+    begin = 0
+    for ref, wide in ((o_query, key), (o_key, key), (o_value, value), (o_gate_proj, value)):
+        ref[...] = mixer[:, pl.ds(begin, wide)].astype(f32)
+        begin += wide
+    for to, of in ((o_out, out), (o_gate, gate), (o_up, up), (o_down, down)):
+        to[...] = of[...].astype(f32)
+
+    @pl.when(step == 0)
+    def _():
+        o_small[...] = small[...].astype(f32)
+
+
+def finalize(last, lay, tok, halos, mixer, out, gate, up, down, small, key, value):
+    heads, seqs, _, width = halos.shape
+    steps = 2 * heads
+    rows = lay.shape[1] // steps
+    acts = pl.BlockSpec((seqs, rows, width), lambda i: (0, i, 0))
+
+    def by_rows(array, columns=None):
+        return pl.BlockSpec((array.shape[0] // steps, columns or array.shape[1]), lambda i: (i, 0))
+
+    whole_small = pl.BlockSpec(small.shape, lambda i: (0, 0))
+    full = lambda *shape: jax.ShapeDtypeStruct(shape, f32)
+    tall = mixer.shape[0]
+    grads = (out, gate, up, down)
+    return pl.pallas_call(
+        partial(finalize_body, key, value),
+        grid=(steps,),
+        in_specs=[
+            pl.BlockSpec(memory_space=pltpu.SMEM), acts, acts,
+            pl.BlockSpec((1, seqs, HALO, width), lambda i: ((i + 1) // 2 % heads, 0, 0, 0)),
+            by_rows(mixer), *map(by_rows, grads), whole_small,
+        ],
+        out_specs=[acts, acts] + [by_rows(mixer, n) for n in (key, key, value, value)] + [*map(by_rows, grads), whole_small],
+        out_shape=[full(*lay.shape), full(*tok.shape)]
+        + [full(tall, n) for n in (key, key, value, value)]
+        + [full(*a.shape) for a in grads]
+        + [full(*small.shape)],
+        compiler_params=pltpu.CompilerParams(vmem_limit_bytes=60 * 2**20),
+        name="outputs",
+    )(last, lay, tok, halos, mixer, out, gate, up, down, small)
 
 
 def chunks(array, rows, count):
@@ -1327,9 +1406,9 @@
     )
     ff_part = ff // 4
     ff_plan = [(a, 1, i * ff_part, ff_part) for a in range(3) for i in range(4)]
-    leaving, layer_out, grad_gate, grad_up, grad_down = sums(
-        layer_out,
-        0,
+    leaving, *blocks = sums(
+        (),
+        (),
         ff_plan,
         [(0, 0, False), (1, 0, False), (2, 1, False)],
         [w_down.shape] * 3,
@@ -1338,6 +1417,7 @@
         [normed_two[None, None], upstream.reshape(1, 1, -1, width)],
         3,
         (own_grad.reshape(flat), log_total),
+        False,
     )
     d_projected, tokens_grad, grad_taps, grad_attn_gain = backward_two(
         first, tokens_ext, attn_gain, d_hidden_in, w_mixer, taps, pre, q_exp, k_exp, k_end, value, decay, states, d_core,
@@ -1357,26 +1437,26 @@
     lanes = -(-small.shape[1] // (small_rows * 128)) * 128
     small = jnp.pad(small, ((0, 0), (0, small_rows * lanes - small.shape[1]))).reshape(heads, small_rows, lanes)
     mixer_plan = chunks(0, width, 4) + [(1, 1, i * out_half, out_half) for i in range(2)] + chunks(2, small_rows, 2)
-    tokens_grad, halos, grad_mixer, grad_out, small = sums(
-        tokens_grad,
-        HALO,
+    more = [(3 + a, axis, row, size, c % 2) for c, (a, axis, row, size) in enumerate(ff_plan)]
+    layer_out, tokens_grad, halos, grad_mixer, grad_out, small, grad_gate, grad_up, grad_down = sums(
+        (layer_out, tokens_grad),
+        (0, HALO),
         mixer_plan,
         [(0, 0, True), (1, 1, True), 0],
-        [(width, mixer_width), w_out.shape, small.shape[1:]],
+        [(width, mixer_width), w_out.shape, small.shape[1:]] + [w_down.shape] * 3,
         [small.astype(bf16)],
         [normed[None], gated],
         [d_projected, d_mixer[None]],
         4,
+        blocks=blocks,
+        more=more,
+        groups=[(0, 1, 4, 5), (2, 3, 6, 7)],
     )
-    grad_gate, grad_up, grad_down, grad_out, grad_mixer, small = (
-        a.astype(f32) for a in (grad_gate, grad_up, grad_down, grad_out, grad_mixer, small)
+    last = lax.axis_index("seq") == lax.axis_size("seq") - 1
+    (layer_out, tokens_grad, grad_query, grad_key, grad_value, grad_out_gate, grad_out, grad_gate, grad_up, grad_down, small) = finalize(
+        last.astype(jnp.int32).reshape(1), layer_out, tokens_grad, halos, grad_mixer, grad_out, grad_gate, grad_up, grad_down,
+        small, key_width, value_width,
     )
-    layer_out = layer_out.astype(f32)
-    last = lax.axis_index("seq") == lax.axis_size("seq") - 1
-    halos = jnp.where(last & (jnp.arange(heads) == 0)[:, None, None, None], 0, halos).astype(f32)
-    halos = jnp.moveaxis(jnp.roll(halos, -1, axis=0), 0, 1)
-    halos = jnp.pad(halos, ((0, 0), (0, 0), (mine - HALO, 0), (0, 0))).reshape(tokens_grad.shape)
-    tokens_grad = tokens_grad.astype(f32) + halos
     small = small.reshape(-1)
     at = 2 * own_width + value_width
     grad_taps = small[at : at + taps[0].size].reshape(taps.shape[1:])
@@ -1384,10 +1464,10 @@
         layer_out,
         tokens_grad,
         small[:own_width],
-        grad_mixer[:, :key_width],
-        grad_mixer[:, key_width : 2 * key_width],
-        grad_mixer[:, 2 * key_width : conv_width],
-        grad_mixer[:, conv_width:],
+        grad_query,
+        grad_key,
+        grad_value,
+        grad_out_gate,
         grad_taps[:, :key_width],
         grad_taps[:, key_width : 2 * key_width],
         grad_taps[:, 2 * key_width :],

time: 549 us -> 509 us (0.927)
  local copies, waits for them, and re-layouts: 51 us -> 10.4 us
  Pallas kernels: 464 us -> 472 us
  other arithmetic: 14 us -> 6.41 us
    unnamed x103 -> x10, local copies, waits for them, and re-layouts: 36.9 us -> 2.02 us
    pallas_call x0 -> x1, Pallas kernels: none -> 11 us  [finalize(): pl.pallas_call(partial(finalize_body, key, value), grid=(steps,), in_spec...]
    pallas_call x1, Pallas kernels: 36.9 us -> 29.6 us  [mlp(): pl.pallas_call(partial(mlp_body, per_head), grid=(heads * per_head,), in_...]
    convert_element_type x5 -> x0, other arithmetic: 6.28 us -> none  [the longest x3 3.87 us: local(): a.astype(f32)]
  transfers between devices with their start and end apart: 2 -> 2, of which waited for: 0 -> 0; matrix products, arithmetic and copies ran while one was open for 2% -> 1% of each run, Pallas kernels for 16% -> 18%
where the time goes in v6:
time: 509 us; the launch traced here: 507 us
  Pallas kernels  472 us (93%)
  between operations  14.2 us (3%)
  local copies, waits for them, and re-layouts  10.4 us (2%)
  other arithmetic  6.41 us (1%)
    pallas_call x2, Pallas kernels, sums(): pl.pallas_call(partial(sums_body, seq, plan, sources, shapes, len(given),...  213 us
    pallas_call x1, Pallas kernels, start_all(): pl.pallas_call(partial(start_body, seq, len(weights), items, steps), out_...  94.4 us
    pallas_call x1, Pallas kernels, exchange(): pl.pallas_call(partial(exchange_body, count, heads, rows // logs.shape[0]...  63.4 us
    pallas_call x1, Pallas kernels, mlp(): pl.pallas_call(partial(mlp_body, per_head), grid=(heads * per_head,), in_...  29.6 us
    pallas_call x1, Pallas kernels, backward_two(): pl.pallas_call(backward_two_body, grid=(seqs, heads), in_specs=[pl.BlockS...  21.5 us
    pallas_call x1, Pallas kernels, forward_one(): pl.pallas_call(forward_one_body, grid=(heads, seqs), in_specs=[pl.BlockSp...  15.2 us
    pallas_call x1, Pallas kernels, forward_two(): pl.pallas_call(forward_two_body, grid=(seqs, heads), in_specs=[pl.BlockSp...  12.8 us
    pallas_call x1, Pallas kernels, backward_one(): pl.pallas_call(backward_one_body, grid=(seqs, heads), in_specs=[by_seq, p...  11.9 us
  transfers between devices with their start and end apart: 2, of which 0 were waited for; matrix products, arithmetic and copies ran while one was open for 1% of the time, Pallas kernels for 18%

profile of v6, /device:TPU:1, one launch (start us, length us, event | category | flops | bytes accessed | tf_op | source)
XLA Modules:
  0.0 507.2 jit_solution(13854406164161927969)
XLA Ops:
  7.2 0.0 copy-start
  7.2 0.0 all-gather.2.cloned.1.call-start
  7.2 2.2 convert_element_type.10.refs_1_
  9.4 1.3 pad_maximum_fusion.1.refs_2_
  10.8 94.4 %start_exchange.1 = (bf16[2,272,1024]{2,1,0:T(8,128)(2,1)}, s16[2,256,512]{2,1,0:T(8,128)(2,1)}, f32[4,4,512]{2,1,0:T(4,128)}, bf16[4,1024,768]{2,1,0:T(8,128)(2...) custom-call(bf16[2,1024,256]{2,1,0:T(8,128)(2,1)} %refs_0_.1, ...), custom_call_target="tpu_custom_call" | custom-call | tf_op jit(solution)/shard_map/start_exchange/pallas_call | solution.py:300
  105.1 0.7 constant_dynamic-slice_fusion
  105.8 0.0 all-gather.2.cloned.1.call-update
  105.9 2.0 copy.36
  107.9 3.7 all-to-all-start
  111.6 15.2 %attention_spans.1 = (bf16[2,272,1024]{2,1,0:T(8,128)(2,1)}, bf16[4,2,272,768]{3,2,1,0:T(8,128)(2,1)}, bf16[4,2,256,128]{3,2,1,0:T(8,128)(2,1)}, bf16[4,2,256,12...) custom-call(s32[1]{0:T(128)} %bitcast.1.first, ...), custom_call_target="tpu_custom_call" | custom-call | tf_op jit(solution)/shard_map/attention_spans/pallas_call | solution.py:1010
  126.8 63.4 %exchange_states.1 = (bf16[2048,128]{1,0:T(8,128)(2,1)}, bf16[4,704,1024]{2,1,0:T(8,128)(2,1)}, bf16[4,704,1024]{2,1,0:T(8,128)(2,1)}) custom-call(bf16[2048,128]{1,0:T(8,128)(2,1)} %bitcast.65, f32[8,128]{1,0:T(8,128)} %bitcast.68, bf16[4,704,1024]{2,1,0:T(8,128)(2,1)} %get-tuple-element.97.refs_2_, ...), custom_call_target="tpu_custom_call", output_to_operand_aliasing={{1}: (2, {}), {2}: (3, {})} | custom-call | tf_op jit(solution)/shard_map/exchange_states/pallas_call | solution.py:439
  190.2 12.8 %attention_outputs.1 = (f32[4,2,256,256]{3,2,1,0:T(8,128)}, bf16[4,2,4,256,128]{4,3,2,1,0:T(8,128)(2,1)}, bf16[4,2,256,256]{3,2,1,0:T(8,128)(2,1)}, f32[2,256,1024]{2,1,0:T(8,128)}) custom-call(s32[1]{0:T(128)} %bitcast.1.first, bf16[2,272,1024]{2,1,0:T(8,128)(2,1)} %get-tuple-element.84.tokens, bf16[4,2,272,768]{3,2,1,0:T(8,128)(2,1)} %get-tuple-element.89.pre, ...), custom_call_target="tpu_custom_call" | custom-call | tf_op jit(solution)/shard_map/attention_outputs/pallas_call | solution.py:1078
  203.0 0.8 copy.45
  203.9 1.6 reshape.129.refs_6_
  205.4 1.2 copy.38
  206.6 29.6 %feed_forward.1 = (bf16[512,1024]{1,0:T(8,128)(2,1)}, f32[512,1024]{1,0:T(8,128)}, bf16[512,1024]{1,0:T(8,128)(2,1)}, bf16[4,704,512]{2,1,0:T(8,128)(2,1)}, bf16...) custom-call(f32[512,1024]{1,0:T(8,128)} %bitcast.55, f32[1,1024]{1,0:T(1,128)} %bitcast.74, ...), custom_call_target="tpu_custom_call" | custom-call | tf_op jit(solution)/shard_map/feed_forward/pallas_call | solution.py:912
  236.2 0.7 convert_reduce_fusion
  237.0 11.9 %attention_outputs_back.1 = (bf16[2,256,1024]{2,1,0:T(8,128)(2,1)}, bf16[4,2,256,256]{3,2,1,0:T(8,128)(2,1)}, bf16[4,2,256,256]{3,2,1,0:T(8,128)(2,1)}, bf16[4,2...) custom-call(f32[2,256,1024]{2,1,0:T(8,128)} %bitcast.47, ...), custom_call_target="tpu_custom_call" | custom-call | tf_op jit(solution)/shard_map/attention_outputs_back/pallas_call | solution.py:1147
  248.8 0.7 convert_reduce_fusion.1
  249.5 112.9 %sum_gradients.2 = (bf16[2048,128]{1,0:T(8,128)(2,1)}, bf16[704,128]{1,0:T(8,128)(2,1)}, bf16[704,128]{1,0:T(8,128)(2,1)}, bf16[704,128]{1,0:T(8,128)(2,1)}) custom-call(bf16[2048,128]{1,0:T(8,128)(2,1)} %bitcast.64, f32[8,128]{1,0:T(8,128)} %bitcast.69, bf16[4,1,704,512]{3,2,1,0:T(8,128)(2,1)} %bitcast.53, bf16[4,1,704,512]{3,2,1,0:T(8,128)(2,1)} %bitcast.54, ...), custom_call_target="tpu_custom_call" | custom-call | tf_op jit(solution)/shard_map/sum_gradients/pallas_call | solution.py:831
  362.4 21.5 %attention_spans_back.1 = (bf16[4,2,272,768]{3,2,1,0:T(8,128)(2,1)}, bf16[2,272,1024]{2,1,0:T(8,128)(2,1)}, f32[4,4,512]{2,1,0:T(4,128)}, f32[2,1,1024]{2,1,0:T(1,128)}) custom-call(s32[1]{0:T(128)} %bitcast.1.first, bf16[2,272,1024]{2,1,0:T(8,128)(2,1)} %get-tuple-element.84.tokens, f32[1,1024]{1,0:T(1,128)} %bitcast.71, f32[2,256,1024]{2,1,0:T(8,128)} %bitcast.48, ...), custom_call_target="tpu_custom_call" | custom-call | tf_op jit(solution)/shard_map/attention_spans_back/pallas_call | solution.py:1248
  384.0 0.7 reduce_sum.9
  384.7 0.8 convert_bitcast_fusion
  385.5 0.1 pad_bitcast_fusion
  385.6 0.7 copy.44
  386.3 99.7 %sum_gradients.3 = (bf16[2,1024,256]{2,1,0:T(8,128)(2,1)}, bf16[2,1024,256]{2,1,0:T(8,128)(2,1)}, bf16[4,2,16,256]{3,2,1,0:T(8,128)(2,1)}, bf16[1024,768]{1,0:T(...) custom-call(bf16[2,256,1024]{2,1,0:T(8,128)(2,1)} %bitcast.59, ...), custom_call_target="tpu_custom_call" | custom-call | tf_op jit(solution)/shard_map/sum_gradients/pallas_call | solution.py:831
  486.0 0.0 copy-start.1
  486.0 11.0 %outputs.1 = (f32[2,1024,256]{2,1,0:T(8,128)}, f32[2,1024,256]{2,1,0:T(8,128)}, f32[1024,128]{1,0:T(8,128)}, f32[1024,128]{1,0:T(8,128)}, f32[1024,256]{1,0:T(8,...) custom-call(s32[1]{0:T(128)} %bitcast.last, ...), custom_call_target="tpu_custom_call" | custom-call | tf_op jit(solution)/shard_map/outputs/pallas_call | solution.py:1314
  497.1 1.4 slice_bitcast_fusion
  498.5 0.7 slice.33
  499.2 0.6 slice.43
  499.8 0.6 fusion
  (12 shorter events, 0.1 us)
Async XLA Ops:
  7.2 97.9 %copy-start = (bf16[704,1024]{1,0:T(8,128)(2,1)S(1)}, bf16[704,1024]{1,0:T(8,128)(2,1)}, u32[]{:S(2)}) copy-start(bf16[704,1024]{1,0:T(8,128)(2,1)} %param.33) | copy-start | bytes 4325380
  7.2 199.4 %all-gather.2.cloned.1.call-start = ((), (), s32[]{:S(2)}) async-start(), calls=%async_computation.1 | async-start | bytes 5947392 | tf_op jit(solution)/shard_map/all_gather | solution.py:43
  10.8 95.1 %copy-start.2 = (bf16[2,1024,256]{2,1,0:T(8,128)(2,1)S(1)}, bf16[2,1024,256]{2,1,0:T(8,128)(2,1)}, u32[]{:S(2)}) copy-start(bf16[2,1024,256]{2,1,0:T(8,128)(2,1)} %param.19) | copy-start | bytes 3145732
  107.9 95.1 %all-to-all-start = ((bf16[2,1024,256]{2,0,1:T(2,128)(2,1)}), bf16[2,1024,256]{2,0,1:T(2,128)(2,1)S(1)}, u32[]{:S(2)}, u32[]{:S(2)}) async-start(bf16[2,1024,256]{2,0,1:T(2,128)(2,1)} %copy.36), calls=%async_computation | async-start | bytes 2097152 | tf_op jit(solution)/shard_map/all_to_all | solution.py:1383
  486.0 14.3 %copy-start.1 = (bf16[704,1024]{1,0:T(8,128)(2,1)S(1)}, bf16[704,1024]{1,0:T(8,128)(2,1)}, u32[]{:S(2)}) copy-start(bf16[704,1024]{1,0:T(8,128)(2,1)} %param.33) | copy-start | bytes 4325380
Sparse Core Ops, SparseCore 0:
  106.0 92.0 all-gather.1

commit v7 on v6

--- a/solution.py
+++ b/solution.py
@@ -34,14 +34,6 @@
 
 def rounded(values):
     return values.astype(bf16).astype(f32)
-
-
-def whole(weight):
-    seq = lax.axis_size("seq")
-    part = weight.shape[0] // seq
-    mine = lax.dynamic_slice_in_dim(weight, lax.axis_index("seq") * part, part, 0)
-    every = lax.all_gather(mine, ("head", "seq"), axis=0, tiled=True)
-    return every.reshape(lax.axis_size("head"), *weight.shape)
 
 
 def flipped(place, mask):
@@ -240,6 +232,7 @@
             return [far_copy(i)]
         return near_copies(i) if k == 1 else seq_copies(i, k - 2)
 
+    sends_at = 4
     stages = 2 + len(masks)
     pairs = (max(item[0] for item in items) + 2) // 2
     for t in range(pairs + stages):
@@ -253,9 +246,10 @@
                 if k < 2 + steps[i]:
                     for copy in stage(i, k):
                         copy.start()
-        if t == 0:
+        if t == sends_at:
             for target in range(heads):
                 sends(target, "start")
+        if t == 0:
             for i in range(count):
                 own_load(i).start()
     for i in range(count):
@@ -429,7 +423,7 @@
             copy.wait_send()
 
 
-def exchange(value, logs, collective_id, items, gathered):
+def exchange(value, logs, collective_id, items=(), gathered=()):
     heads = lax.axis_size("head")
     count = lax.axis_size("seq") * heads
     rows, width = value.shape
@@ -443,7 +437,8 @@
         in_specs=[near] * 2 + [far] * more,
         out_specs=[near] + [far] * more,
         input_output_aliases={2 + i: 1 + i for i in range(more)},
-        scratch_shapes=states_scratch(count, rows, width) + [dma((len(items), 3, 3)), dma((len(items), 3, 3))],
+        scratch_shapes=states_scratch(count, rows, width)
+        + [dma((max(len(items), 1), 3, 3)), dma((max(len(items), 1), 3, 3))],
         compiler_params=pltpu.CompilerParams(
             collective_id=collective_id, has_side_effects=True, vmem_limit_bytes=60 * 2**20),
         name="exchange_states",
@@ -454,7 +449,7 @@
     return x if isinstance(x, int) else pl.multiple_of(x, size)
 
 
-def sums_body(seq, plan, sources, shapes, n_given, n_left, n_right, leads, states, spread, more, groups, *refs):
+def sums_body(seq, plan, sources, shapes, n_given, n_left, n_right, leads, states, spread, more, groups, n_ring, rider, *refs):
     heads = 4
     nz = 1
     seq_masks = [1 << k for k in range(seq.bit_length() - 1)]
@@ -474,15 +469,20 @@
     orders = [c % 2 for c in range(count)] + [item[4] for item in more]
     plan = [*plan, *(item[:4] for item in more)]
     given, lefts, rights = take(n_given), take(n_left), take(n_right)
+    rider_in = take(rider[0]) if rider else None
     (new_state,) = take(1) if states else (None,)
     acts_full = take(len(leads))
     halos = take(sum(map(bool, leads)))
     outs = take(len(shapes))
+    rider_out = take(rider[1]) if rider else None
     per = ns + nj + nz
     owns = take(count)
     recvs = [take(per) for _ in range(count)]
-    staged = {c: take(1)[0] for c in range(count) if not isinstance(sources[plan[c][0]], int)}
+    dots = [c for c in range(count) if not isinstance(sources[plan[c][0]], int)]
+    ring = take(min(len(dots), n_ring))
+    staged = {c: ring[n % n_ring] for n, c in enumerate(dots)}
     state_scratch = take(7) if states else None
+    rider_scratch = take(rider[2]) if rider else None
     (load_sem, send_sem, recv_sem, jsend, jrecv, zsend, zrecv, gsend, grecv, keep_sem, asend, arecv, stay, hsend,
      hrecv) = refs
     s, z = lax.axis_index("seq"), lax.axis_index("head")
@@ -749,11 +749,14 @@
 
     def begin_chunk(c):
         if c in staged:
+            if dots.index(c) >= n_ring:
+                seq_copy(dots[dots.index(c) - n_ring], 0).wait_send()
             product(c)
         else:
             load(c).start()
         seq_copy(c, 0).start()
 
+    ride_at, ride_parts = 4, 4
     for t in range(len(groups) + last):
         for k in range(last):
             if 0 <= t - 1 - k < len(groups):
@@ -774,26 +777,35 @@
                 to_features(a, True)
         if t == 1 and states:
             add_up()
+        if states and t == ride_at:
+            end()
+            load_first, run, finish_run = rider[3](s * heads + z == 0, new_state, rider_in, rider_out, rider_scratch)
+            load_first()
+        if states and ride_at <= t < ride_at + ride_parts:
+            run(t - ride_at, ride_parts)
     for a in range(len(acts)):
         to_features(a, False)
     for c in range(count):
         for k in range(last):
-            if not ns <= k < ns + nj:
+            if not ns <= k < ns + nj and not (k == 0 and c in dots[: max(len(dots) - n_ring, 0)]):
                 for copy in copies(c, k):
                     copy.wait_send()
     for c in range(count, len(plan)):
         for j in range(ns):
             gather_copy(c, j).wait_send()
     if states:
-        end()
-
-
-def sums(acts, leads, plan, sources, shapes, given, lefts, rights, collective_id, states=(), spread=True, blocks=(), more=(), groups=None):
+        finish_run()
+
+
+def sums(acts, leads, plan, sources, shapes, given, lefts, rights, collective_id, states=(), spread=True, blocks=(), more=(), groups=None, rider=None):
     groups = groups or [(c, c + 1) for c in range(0, len(plan), 2)]
     seq, heads = lax.axis_size("seq"), lax.axis_size("head")
     nj = max(0, seq.bit_length() - 4)
     ns = 3
     owns, recvs, staged = [], [], []
+    n_ring = 4 if states else 8
+    ride_args, ride_specs, ride_shapes, ride_outs, ride_scratch, ride_body = rider or ((), (), (), (), (), None)
+    ride = (len(ride_args), len(ride_shapes), len(ride_scratch), ride_body) if rider else None
     for a, axis, first, rows in plan:
         columns = shapes[a][1]
         cut = lambda k: (rows >> k, columns) if axis == 0 else (rows, columns >> k)
@@ -822,26 +834,28 @@
     if not spread:
         shapes_out = [(rows, columns >> ns) for rows, columns in shapes]
     out_shape += [jax.ShapeDtypeStruct(shape, bf16) for shape in (shapes if spread else shapes_out)]
-    out_specs = [anywhere] * len(out_shape)
+    out_specs = [anywhere] * len(out_shape) + list(ride_outs)
+    out_shape += ride_shapes
     state_scratch = []
     if states:
         out_shape.insert(0, jax.ShapeDtypeStruct(states[0].shape, bf16))
         out_specs.insert(0, near)
         state_scratch = states_scratch(seq * heads, *states[0].shape)
     return pl.pallas_call(
-        partial(sums_body, seq, plan, sources, shapes, len(given), len(lefts), len(rights), leads, bool(states), spread, more, groups),
+        partial(sums_body, seq, plan, sources, shapes, len(given), len(lefts), len(rights), leads, bool(states), spread, more, groups, n_ring, ride),
         out_shape=out_shape,
         in_specs=[near] * len(states)
         + [anywhere] * len(acts)
         + [near] * len(blocks)
         + [anywhere] * len(given)
-        + [near] * (len(lefts) + len(rights)),
+        + [near] * (len(lefts) + len(rights))
+        + list(ride_specs),
         out_specs=out_specs,
-        scratch_shapes=owns + recvs + staged + state_scratch + sems,
+        scratch_shapes=owns + recvs + staged[:n_ring] + state_scratch + list(ride_scratch) + sems,
         compiler_params=pltpu.CompilerParams(
             collective_id=collective_id, has_side_effects=True, vmem_limit_bytes=60 * 2**20),
         name="sum_gradients",
-    )(*states, *acts, *blocks, *given, *lefts, *rights)
+    )(*states, *acts, *blocks, *given, *lefts, *rights, *ride_args)
 
 
 def dot_nt(a, b):
@@ -1165,16 +1179,15 @@
     )(d_hidden_in, w_out, core, pre, out_gain.reshape(1, -1), q_exp, decay)
 
 
-def backward_two_body(
-    first, tokens, gain, d_hidden_in, w, taps, pre, q_exp, k_exp, k_end, value, decay, states, d_core, d_states, leaving,
+def backward_two_step(
+    i, h, heads, first, tokens, gain, d_hidden_in, w, taps, pre, q_exp, k_exp, k_end, value, decay, states, d_core, d_states, leaving,
     d_gate, d_projected, d_tokens, d_taps, d_gain, d_normed,
 ):
-    i, h = pl.program_id(0), pl.program_id(1)
     key, wide_value = q_exp.shape[3], value.shape[3]
     rows = q_exp.shape[2]
     blocks = rows // SPAN
     scale = key**-0.5
-    d_end = leaving[0, 0].astype(f32)
+    d_end = leaving[...].astype(f32)
     pieces = [None] * blocks
     for n in reversed(range(blocks)):
         at = pl.ds(n * SPAN, SPAN)
@@ -1223,9 +1236,9 @@
     def _():
         d_normed[...] += term
 
-    @pl.when(h == pl.num_programs(1) - 1)
-    def _():
-        values, upstream = without_first(tokens[0], first[0]), d_normed[...]
+    @pl.when(h == heads - 1)
+    def _():
+        values, upstream = without_first(tokens[0], first), d_normed[...]
         inverse = row_scale(values)
         gain_term = jnp.sum(upstream * values * inverse, axis=0, keepdims=True)
         d_gain[0] = gain_term
@@ -1234,43 +1247,97 @@
         d_tokens[0, pl.ds(HALO, rows)] = (back[HALO:] + d_hidden_in[0]).astype(bf16)
 
 
-def backward_two(
-    first, tokens, gain, d_hidden_in, w, taps, pre, q_exp, k_exp, k_end, value, decay, states, d_core, d_states, leaving, d_gate
-):
-    heads, seqs, rows, key = q_exp.shape
+def backward_two_body(first, leaving, operands, outs, scratch):
+    tokens, d_hidden_in, w, *by_head, gain, taps = operands
+    d_projected, d_tokens, d_taps, d_gain = outs
+    tokens_here, hidden_here, w_here, *here, projected_here, tokens_out, d_normed, load_sem, once_sem, store_sem = scratch
+    heads, seqs, rows, key = by_head[1].shape
+    wide_value = by_head[4].shape[3]
+    steps = heads * seqs
+    first = first.astype(jnp.int32)
+
+    def once():
+        return [
+            pltpu.make_async_copy(tokens, tokens_here, once_sem.at[0]),
+            pltpu.make_async_copy(d_hidden_in, hidden_here, once_sem.at[1]),
+        ]
+
+    def loads(n):
+        i, h = n // heads, n % heads
+        copies = [pltpu.make_async_copy(w.at[pl.ds(h, 1)], w_here, load_sem.at[0])]
+        return copies + [
+            pltpu.make_async_copy(a.at[pl.ds(h, 1), pl.ds(i, 1)], b, load_sem.at[1 + k])
+            for k, (a, b) in enumerate(zip(by_head, here))
+        ]
+
+    def store(n):
+        return pltpu.make_async_copy(
+            projected_here, d_projected.at[pl.ds(n % heads, 1), pl.ds(n // heads, 1)], store_sem.at[0])
+
+    def step(n, carry):
+        i, h = n // heads, n % heads
+        for copy in loads(n):
+            copy.wait()
+
+        @pl.when(n > 0)
+        def _():
+            store(n - 1).wait()
+
+        at = pl.ds(pl.multiple_of((h * seqs + i) * wide_value, wide_value), wide_value)
+        backward_two_step(
+            i, h, heads, first, tokens_here.at[pl.ds(i, 1)], gain, hidden_here.at[pl.ds(i, 1)], w_here, taps.at[pl.ds(h, 1)],
+            *here[:-1], leaving.at[at], here[-1], projected_here, tokens_out, d_taps, d_gain.at[pl.ds(i, 1)], d_normed)
+        store(n).start()
+
+        @pl.when(n < steps - 1)
+        def _():
+            for copy in loads(n + 1):
+                copy.start()
+
+        @pl.when(h == heads - 1)
+        def _():
+            copy = pltpu.make_async_copy(tokens_out, d_tokens.at[pl.ds(i, 1)], store_sem.at[1])
+            copy.start()
+            copy.wait()
+
+        return carry
+
+    def load_first():
+        for copy in once() + loads(0):
+            copy.start()
+        for copy in once():
+            copy.wait()
+
+    def run(part, parts):
+        lax.fori_loop(part * steps // parts, (part + 1) * steps // parts, step, 0)
+
+    def finish_run():
+        store(steps - 1).wait()
+
+    return load_first, run, finish_run
+
+
+def backward_two(tokens, gain, d_hidden_in, w, taps, *by_head):
+    heads, seqs, rows, key = by_head[1].shape
     width, columns = w.shape[1:]
-    wide_value = value.shape[3]
     tap_count, wide = taps.shape[1:]
-    blocks = rows // SPAN
     tall = rows + HALO
-    per = head_spec
-    by_seq = lambda n: pl.BlockSpec((1, n, width), lambda i, h: (i, 0, 0))
-    return pl.pallas_call(
+    anywhere, near = pl.BlockSpec(memory_space=pl.ANY), pl.BlockSpec(memory_space=pltpu.VMEM)
+    dma = pltpu.SemaphoreType.DMA
+    shape = jax.ShapeDtypeStruct
+    return (
+        (tokens, d_hidden_in, w, *by_head, gain.reshape(1, -1), taps),
+        [anywhere] * (3 + len(by_head)) + [near] * 2,
+        [
+            shape((heads, seqs, tall, columns), bf16), shape((seqs, tall, width), bf16), shape((heads, tap_count, wide), f32),
+            shape((seqs, 1, width), f32),
+        ],
+        [anywhere] * 2 + [near] * 2,
+        [pltpu.VMEM(tokens.shape, bf16), pltpu.VMEM(d_hidden_in.shape, f32), pltpu.VMEM((1, *w.shape[1:]), bf16)]
+        + [pltpu.VMEM((1, 1, *a.shape[2:]), a.dtype) for a in by_head]
+        + [pltpu.VMEM((1, 1, tall, columns), bf16), pltpu.VMEM((1, tall, width), bf16), pltpu.VMEM((tall, width), f32)]
+        + [dma((1 + len(by_head),)), dma((2,)), dma((2,))],
         backward_two_body,
-        grid=(seqs, heads),
-        in_specs=[
-            pl.BlockSpec(memory_space=pltpu.SMEM), by_seq(tall), pl.BlockSpec((1, width), lambda i, h: (0, 0)),
-            by_seq(rows), pl.BlockSpec((1, width, columns), lambda i, h: (h, 0, 0)),
-            pl.BlockSpec((1, tap_count, wide), lambda i, h: (h, 0, 0)),
-            per(tall, columns), per(rows, key), per(rows, key), per(rows, key), per(rows, wide_value), per(rows, key),
-            per(blocks, wide_value, key), per(rows, wide_value), per(blocks, wide_value, key), per(wide_value, key),
-            per(rows, wide_value),
-        ],
-        out_specs=[
-            per(tall, columns), by_seq(tall), pl.BlockSpec((heads, tap_count, wide), lambda i, h: (0, 0, 0)), by_seq(1),
-        ],
-        out_shape=[
-            jax.ShapeDtypeStruct((heads, seqs, tall, columns), bf16),
-            jax.ShapeDtypeStruct((seqs, tall, width), bf16),
-            jax.ShapeDtypeStruct((heads, tap_count, wide), f32),
-            jax.ShapeDtypeStruct((seqs, 1, width), f32),
-        ],
-        scratch_shapes=[pltpu.VMEM((tall, width), f32)],
-        compiler_params=pltpu.CompilerParams(vmem_limit_bytes=60 * 2**20),
-        name="attention_spans_back",
-    )(
-        first, tokens, gain.reshape(1, -1), d_hidden_in, w, taps, pre, q_exp, k_exp, k_end, value, decay, states, d_core,
-        d_states, leaving, d_gate,
     )
 
 
@@ -1368,20 +1435,19 @@
     items += [(i, 2, 0, 0, i * half, half, 2 * key_width, value_width) for i in range(2)]
     items += [(i, 3, 0, 0, i * half, half, conv_width, value_width) for i in range(2)]
     items += [(i, 4, 1, 0, i * out_half, out_half, 0, width) for i in range(2)]
-    pair = [(2 + 2 * a + i, 5 + a, 2 + a, 1, i * ff_half, ff_half, 0, width) for a in range(2) for i in range(2)]
-    tokens_ext, codes, taps, w_mixer, w_proj, w_gate_all, w_up_all = start_all(
+    pair = [(2 + 2 * a + i, 5 + a, 2 + a, 1, i * ff_half, ff_half, 0, width) for a in range(3) for i in range(2)]
+    tokens_ext, codes, taps, w_mixer, w_proj, w_gate_all, w_up_all, w_low = start_all(
         tokens,
         decay_codes.astype(jnp.int16),
         jnp.concatenate([conv_query, conv_key, conv_value], axis=1),
-        (w_query, w_key, w_value, w_out_gate, w_out, w_gate.T, w_up.T),
+        (w_query, w_key, w_value, w_out_gate, w_out, w_gate.T, w_up.T, w_down),
         items + pair,
-        [3] * len(items) + [1] * len(pair),
-        ((width, mixer_width), w_out.shape, w_down.shape, w_down.shape),
+        [3] * (len(items) + len(pair)),
+        ((width, mixer_width), w_out.shape, w_down.shape, w_down.shape, w_down.shape),
         1,
     )
-    upstream, low_part, codes = lax.optimization_barrier((cotangent, w_down, codes))
+    upstream, codes = lax.optimization_barrier((cotangent, codes))
     upstream = lax.all_to_all(upstream, "head", 1, 2, tiled=True)
-    w_low = whole(low_part)
 
     first = (place == 0).astype(jnp.int32).reshape(1)
     normed, pre, q_exp, k_exp, k_end, value, decay, starts, local_end, log_total = forward_one(
@@ -1389,10 +1455,7 @@
     )
     flat = (-1, key_width)
     log_total = log_total.reshape(flat)
-    pair = [(item[0], 0, item[2] - 2, *item[3:]) for item in pair]
-    incoming, w_gate_all, w_up_all = exchange(
-        local_end.reshape(flat), log_total, 2, pair, (w_gate_all, w_up_all)
-    )
+    (incoming,) = exchange(local_end.reshape(flat), log_total, 2)
     core, states, gated, hidden_in = forward_two(
         first, tokens_ext, pre, q_exp, k_exp, value, decay, starts, incoming.reshape(local_end.shape), out_gain, w_proj
     )
@@ -1406,7 +1469,7 @@
     )
     ff_part = ff // 4
     ff_plan = [(a, 1, i * ff_part, ff_part) for a in range(3) for i in range(4)]
-    leaving, *blocks = sums(
+    _, *blocks, d_projected, tokens_grad, grad_taps, grad_attn_gain = sums(
         (),
         (),
         ff_plan,
@@ -1418,12 +1481,11 @@
         3,
         (own_grad.reshape(flat), log_total),
         False,
+        rider=backward_two(
+            tokens_ext, attn_gain, d_hidden_in, w_mixer, taps, pre, q_exp, k_exp, k_end, value, decay, states, d_core, d_states,
+            d_gate_rows,
+        ),
     )
-    d_projected, tokens_grad, grad_taps, grad_attn_gain = backward_two(
-        first, tokens_ext, attn_gain, d_hidden_in, w_mixer, taps, pre, q_exp, k_exp, k_end, value, decay, states, d_core,
-        d_states, leaving.reshape(local_end.shape), d_gate_rows,
-    )
-
     small = jnp.concatenate(
         [
             jnp.sum(grad_attn_gain, axis=0).reshape(heads, -1),

time: 509 us -> 473 us (0.929)
  Pallas kernels: 472 us -> 447 us
  between operations: 14.2 us -> 1.21 us
    pallas_call x1, Pallas kernels: 63.4 us -> 34 us  [exchange(): pl.pallas_call(partial(exchange_body, count, heads, rows // logs.shape[0]...]
    pallas_call x1 -> x0, Pallas kernels: 21.5 us -> none  [backward_two(): pl.pallas_call(backward_two_body, grid=(seqs, heads), in_specs=[pl.BlockS...]
    pallas_call x1, Pallas kernels: 94.4 us -> 113 us  [start_all(): pl.pallas_call(partial(start_body, seq, len(weights), items, steps), out_...]
    pallas_call x2, Pallas kernels: 213 us -> 219 us  [sums(): pl.pallas_call(partial(sums_body, seq, plan, sources, shapes, len(given),...]
  transfers between devices with their start and end apart: 2 -> 1, of which waited for: 0 -> 0; matrix products, arithmetic and copies ran while one was open for 1% -> 0% of each run, Pallas kernels for 18% -> 13%
where the time goes in v7:
time: 473 us; the launch traced here: 468 us
  Pallas kernels  447 us (95%)
  local copies, waits for them, and re-layouts  9.74 us (2%)
  other arithmetic  6.31 us (1%)
    pallas_call x2, Pallas kernels, sums(): pl.pallas_call(partial(sums_body, seq, plan, sources, shapes, len(given),...  219 us
    pallas_call x1, Pallas kernels, start_all(): pl.pallas_call(partial(start_body, seq, len(weights), items, steps), out_...  113 us
    pallas_call x1, Pallas kernels, exchange(): pl.pallas_call(partial(exchange_body, count, heads, rows // logs.shape[0]...  34 us
    pallas_call x1, Pallas kernels, mlp(): pl.pallas_call(partial(mlp_body, per_head), grid=(heads * per_head,), in_...  29.6 us
    pallas_call x1, Pallas kernels, forward_one(): pl.pallas_call(forward_one_body, grid=(heads, seqs), in_specs=[pl.BlockSp...  15.1 us
    pallas_call x1, Pallas kernels, forward_two(): pl.pallas_call(forward_two_body, grid=(seqs, heads), in_specs=[pl.BlockSp...  12.7 us
    pallas_call x1, Pallas kernels, backward_one(): pl.pallas_call(backward_one_body, grid=(seqs, heads), in_specs=[by_seq, p...  11.9 us
    pallas_call x1, Pallas kernels, finalize(): pl.pallas_call(partial(finalize_body, key, value), grid=(steps,), in_spec...  10.9 us
  transfers between devices with their start and end apart: 1, of which 0 were waited for; matrix products, arithmetic and copies ran while one was open for 0% of the time, Pallas kernels for 13%

profile of v7, /device:TPU:1, one launch (start us, length us, event | category | flops | bytes accessed | tf_op | source)
XLA Modules:
  0.0 467.8 jit_solution(11984282571504881301)
XLA Ops:
  0.6 2.1 convert_element_type.10.refs_1_
  2.7 1.3 pad_maximum_fusion.1.refs_2_
  4.0 0.0 copy-start
  4.1 113.4 %start_exchange.1 = (bf16[2,272,1024]{2,1,0:T(8,128)(2,1)}, s16[2,256,512]{2,1,0:T(8,128)(2,1)}, f32[4,4,512]{2,1,0:T(4,128)}, bf16[4,1024,768]{2,1,0:T(8,128)(2...) custom-call(bf16[2,1024,256]{2,1,0:T(8,128)(2,1)} %refs_0_.1, ...), custom_call_target="tpu_custom_call" | custom-call | tf_op jit(solution)/shard_map/start_exchange/pallas_call | solution.py:294
  117.5 0.0 copy-done
  117.5 2.0 copy.34
  119.6 3.7 all-to-all-start
  123.3 15.1 %attention_spans.1 = (bf16[2,272,1024]{2,1,0:T(8,128)(2,1)}, bf16[4,2,272,768]{3,2,1,0:T(8,128)(2,1)}, bf16[4,2,256,128]{3,2,1,0:T(8,128)(2,1)}, bf16[4,2,256,12...) custom-call(s32[1]{0:T(128)} %bitcast.1.first, ...), custom_call_target="tpu_custom_call" | custom-call | tf_op jit(solution)/shard_map/attention_spans/pallas_call | solution.py:1024
  138.4 34.0 %exchange_states.1 = bf16[2048,128]{1,0:T(8,128)(2,1)} custom-call(bf16[2048,128]{1,0:T(8,128)(2,1)} %bitcast.62, f32[8,128]{1,0:T(8,128)} %bitcast.66), custom_call_target="tpu_custom_call" | custom-call | tf_op jit(solution)/shard_map/exchange_states/pallas_call | solution.py:433
  172.4 12.7 %attention_outputs.1 = (f32[4,2,256,256]{3,2,1,0:T(8,128)}, bf16[4,2,4,256,128]{4,3,2,1,0:T(8,128)(2,1)}, bf16[4,2,256,256]{3,2,1,0:T(8,128)(2,1)}, f32[2,256,1024]{2,1,0:T(8,128)}) custom-call(s32[1]{0:T(128)} %bitcast.1.first, bf16[2,272,1024]{2,1,0:T(8,128)(2,1)} %get-tuple-element.80.tokens.refs_7_, ...), custom_call_target="tpu_custom_call" | custom-call | tf_op jit(solution)/shard_map/attention_outputs/pallas_call | solution.py:1092
  185.1 0.0 all-to-all-done
  185.2 0.8 copy.43
  186.0 1.6 reshape.122.refs_6_
  187.5 1.2 copy.36
  188.7 29.6 %feed_forward.1 = (bf16[512,1024]{1,0:T(8,128)(2,1)}, f32[512,1024]{1,0:T(8,128)}, bf16[512,1024]{1,0:T(8,128)(2,1)}, bf16[4,704,512]{2,1,0:T(8,128)(2,1)}, bf16...) custom-call(f32[512,1024]{1,0:T(8,128)} %bitcast.53, f32[1,1024]{1,0:T(1,128)} %bitcast.70, ...), custom_call_target="tpu_custom_call" | custom-call | tf_op jit(solution)/shard_map/feed_forward/pallas_call | solution.py:926
  218.4 0.7 convert_reduce_fusion
  219.1 11.9 %attention_outputs_back.1 = (bf16[2,256,1024]{2,1,0:T(8,128)(2,1)}, bf16[4,2,256,256]{3,2,1,0:T(8,128)(2,1)}, bf16[4,2,256,256]{3,2,1,0:T(8,128)(2,1)}, bf16[4,2...) custom-call(f32[2,256,1024]{2,1,0:T(8,128)} %bitcast.45, ...), custom_call_target="tpu_custom_call" | custom-call | tf_op jit(solution)/shard_map/attention_outputs_back/pallas_call | solution.py:1161
  230.9 0.7 convert_reduce_fusion.1
  231.6 123.0 %sum_gradients.2 = (bf16[2048,128]{1,0:T(8,128)(2,1)}, bf16[704,128]{1,0:T(8,128)(2,1)}, bf16[704,128]{1,0:T(8,128)(2,1)}, bf16[704,128]{1,0:T(8,128)(2,1)}, bf1...) custom-call(bf16[2048,128]{1,0:T(8,128)(2,1)} %bitcast.61, ...), custom_call_target="tpu_custom_call" | custom-call | tf_op jit(solution)/shard_map/sum_gradients/pallas_call | solution.py:844
  354.7 0.7 reduce_sum.9
  355.4 0.8 convert_bitcast_fusion
  356.2 0.1 pad_bitcast_fusion
  356.3 0.7 copy.42
  357.1 96.1 %sum_gradients.3 = (bf16[2,1024,256]{2,1,0:T(8,128)(2,1)}, bf16[2,1024,256]{2,1,0:T(8,128)(2,1)}, bf16[4,2,16,256]{3,2,1,0:T(8,128)(2,1)}, bf16[1024,768]{1,0:T(...) custom-call(bf16[2,256,1024]{2,1,0:T(8,128)(2,1)} %bitcast.57, ...), custom_call_target="tpu_custom_call" | custom-call | tf_op jit(solution)/shard_map/sum_gradients/pallas_call | solution.py:844
  453.2 10.9 %outputs.1 = (f32[2,1024,256]{2,1,0:T(8,128)}, f32[2,1024,256]{2,1,0:T(8,128)}, f32[1024,128]{1,0:T(8,128)}, f32[1024,128]{1,0:T(8,128)}, f32[1024,256]{1,0:T(8,...) custom-call(s32[1]{0:T(128)} %bitcast.last, ...), custom_call_target="tpu_custom_call" | custom-call | tf_op jit(solution)/shard_map/outputs/pallas_call | solution.py:1381
  464.1 1.4 slice_bitcast_fusion
  465.5 0.7 slice.33
  466.2 0.6 slice.43
  466.8 0.6 fusion
  (6 shorter events, 0.1 us)
Async XLA Ops:
  4.0 113.4 %copy-start = (bf16[2,1024,256]{2,1,0:T(8,128)(2,1)S(1)}, bf16[2,1024,256]{2,1,0:T(8,128)(2,1)}, u32[]{:S(2)}) copy-start(bf16[2,1024,256]{2,1,0:T(8,128)(2,1)} %param.19) | copy-start | bytes 3145732
  119.6 65.6 %all-to-all-start = ((bf16[2,1024,256]{2,0,1:T(2,128)(2,1)}), bf16[2,1024,256]{2,0,1:T(2,128)(2,1)S(1)}, u32[]{:S(2)}, u32[]{:S(2)}) async-start(bf16[2,1024,256]{2,0,1:T(2,128)(2,1)} %copy.34), calls=%async_computation | async-start | bytes 2097152 | tf_op jit(solution)/shard_map/all_to_all | solution.py:1450
